TPU v7x, 32 devices: a whole 2x2x4 slice. The times are simulated.
32 devices in a mesh: cin: 8 (over z, x), cout: 2 (over y), depth: 2 (over core).
Axes of the slice: x: 2, y: 2, z: 4, core: 2. Of those that a mesh axis runs over, the one named last changes fastest.
Arguments:
- features: bfloat16 [8, 512, 4, 128], P(None, 'cin', 'depth'), may hold values from -6 to 6
- kernel: bfloat16 [27, 512, 512], P(None, 'cout', 'cin'), may hold values from -0.0546875 to 0.0546875
- grad_out: bfloat16 [8, 512, 4, 128], P('cin', 'cout', 'depth'), may hold values from -6 to 6
Outputs:
- output: bfloat16 [8, 512, 4, 128], P('cin', 'cout', 'depth')
- input_grad: bfloat16 [8, 512, 4, 128], P('cout', 'cin', 'depth')
- kernel_grad: float32 [27, 512, 512], P(None, 'cout', 'cin')
All inputs are finite; a program needn't handle non-finite values.
Results may differ from a plain program's by a relative error of at most 0.001.
Values may be sent and summed in bfloat16 or wider, within the bound.
No kernel may reach another device: no remote copies, remote signals or barrier semaphores. Data moves between devices by JAX's collectives and lax.ppermute only.
A program may use at most 128 MiB of HBM per device.

v0:
```python
import math

import jax
import jax.numpy as jnp
from jax import lax
from jax.sharding import PartitionSpec as P


def padded_2(x, sides, width):
    for axis, dim in sides:
        size, length = (lax.axis_size(axis), x.shape[dim])
        up = [(i, (i + 1) % size) for i in range(size - 1)]
        down = [(j, i) for i, j in up]
        last = lax.slice_in_dim(x, length - width, length, axis=dim)
        first = lax.slice_in_dim(x, 0, width, axis=dim)
        before = lax.ppermute(last, axis, up)
        after = lax.ppermute(first, axis, down)
        x = jnp.concatenate([before, x, after], axis=dim)
    return x


def conv_rows(padded, weight, count, slab, width):
    total = None
    for depth_off in range(3):
        pieces = [
            padded[
                row_off : row_off + count,
                :,
                depth_off : depth_off + slab,
                col_off : col_off + width,
            ]
            for row_off in range(3)
            for col_off in range(3)
        ]
        stacked = jnp.stack(pieces, axis=1)
        term = jnp.einsum(
            "toc,htcdw->hodw",
            weight[9 * depth_off : 9 * depth_off + 9],
            stacked,
            preferred_element_type=jnp.float32,
        )
        total = term if total is None else total + term
    return total


def weight_terms(padded, grad_own, count, slab, width):
    parts = []
    for depth_off in range(3):
        pieces = [
            padded[
                row_off : row_off + count,
                :,
                depth_off : depth_off + slab,
                col_off : col_off + width,
            ]
            for row_off in range(3)
            for col_off in range(3)
        ]
        stacked = jnp.stack(pieces, axis=1)
        parts.append(
            jnp.einsum("hodw,htcdw->toc", grad_own, stacked, preferred_element_type=jnp.float32)
        )
    return jnp.concatenate(parts, axis=0)


def per_device(features, kernel, grad_out):
    rows_all = features.shape[0]
    slab = features.shape[2]
    width = features.shape[3]
    chan_in = features.shape[1]
    rows_own = rows_all // lax.axis_size("cin")
    slab_ext = padded_2(features, (("depth", 2),), 1)
    feat_pad = jnp.pad(slab_ext, ((1, 1), (0, 0), (0, 0), (1, 1)))
    block = feat_pad
    output = lax.psum_scatter(
        conv_rows(block, kernel, lax.axis_size("cin") * rows_own, slab, width),
        "cin",
        scatter_dimension=0,
        tiled=True,
    ).astype(jnp.bfloat16)
    grad_full = lax.all_gather(grad_out, "cin", axis=0, tiled=True)
    grad_full = padded_2(grad_full, (("depth", 2),), 1)
    grad_pad = jnp.pad(grad_full, ((1, 1), (0, 0), (0, 0), (0, 0)))
    rows_grad = rows_all // lax.axis_size("cout")
    block = grad_pad
    total = jnp.zeros((lax.axis_size("cout") * rows_grad, chan_in, slab, width), jnp.float32)
    for depth_off in range(3):
        part = block[:, :, 2 - depth_off : 2 - depth_off + slab, :]
        mixed = jnp.einsum(
            "toc,hodw->thcdw",
            kernel[9 * depth_off : 9 * depth_off + 9],
            part,
            preferred_element_type=jnp.float32,
        )
        mixed = jnp.pad(mixed, ((0, 0), (0, 0), (0, 0), (0, 0), (1, 1)))
        for row_off in range(3):
            for col_off in range(3):
                total = (
                    total
                    + mixed[
                        3 * row_off + col_off,
                        2 - row_off : 2 - row_off + lax.axis_size("cout") * rows_grad,
                        :,
                        :,
                        2 - col_off : 2 - col_off + width,
                    ]
                )
    input_grad = lax.psum_scatter(total, "cout", scatter_dimension=0, tiled=True).astype(
        jnp.bfloat16
    )
    grad_own = grad_full[:, :, 1 : 1 + slab, :]
    local_terms = weight_terms(feat_pad, grad_own, rows_all, slab, width)
    summed = lax.psum(local_terms, "depth")
    cells = rows_all * slab * lax.axis_size("depth") * width
    kernel_grad = summed * (1.0 / math.sqrt(cells))
    return (output, input_grad, kernel_grad)


def solution(mesh):
    return jax.shard_map(
        per_device,
        mesh=mesh,
        in_specs=(
            P(None, "cin", "depth", None),
            P(None, "cout", "cin"),
            P("cin", "cout", "depth", None),
        ),
        out_specs=(
            P("cin", "cout", "depth", None),
            P("cout", "cin", "depth", None),
            P(None, "cout", "cin"),
        ),
        check_vma=False,
    )
```

profile of v0, /device:TPU:0, one launch (start us, length us, event | category | flops | bytes accessed | tf_op | source)
XLA Modules:
  0.0 189.4 jit_solution(8112478354780090528)
XLA Ops:
  7.2 1.0 copy.40
  8.2 2.4 %collective-permute-start = (bf16[8,64,1,128]{3,1,2,0:T(8,128)(2,1)S(1)}, bf16[8,64,1,128]{3,1,2,0:T(8,128)(2,1)S(1)}, u32[]{:S(2)}, u32[]{:S(2)}) collective-permute-start(bf16[8,64,1,128]{3,1,2,0:T(8,128)(2,1)S(1)} %get-tuple-element.25), channel_id=1, source_target_pairs={{0,1},{2,3},{4,5},{6,7},{8,9},{10,11},{12,13},{14,15},{16,17},{18,... | collective-permute-start | bytes 393224 | tf_op jit(solution)/shard_map/ppermute | solution.py:16
  10.6 1.3 collective-permute-start.1
  11.9 1.6 copy.55
  19.3 1.0 fusion.83
  28.7 28.0 %all-gather.2.cloned.1.call-done = bf16[8,256,2,128]{3,1,2,0:T(8,128)(2,1)} async-done(((bf16[1,256,2,128]{3,1,2,0:T(8,128)(2,1)}), bf16[8,256,2,128]{3,1,2,0:T(8,128)(2,1)}) %all-gather.2.cloned.1.call-update) | async-done | bytes 1048592 | tf_op jit(solution)/shard_map/all_gather | solution.py:81
  56.7 1.4 fusion.104
  58.0 1.3 collective-permute-start.2
  59.4 1.3 collective-permute-start.3
  61.6 1.0 fusion.78
  66.5 0.9 convolution_bitcast_fusion
  67.4 3.3 %fusion.54 = f32[8,64,2,128]{3,1,2,0:T(8,128)} fusion(f32[9,10,64,2,128]{4,2,3,1,0:T(8,128)S(1)} %convolution_bitcast_fusion, f32[9,10,64,2,128]{4,2,3,1,0:T(8,128)S(1)} %convolution_bitcast_fusion.1, f32[9,10,64,2,128]{4,2,0,3,1:T(8,128)S(1)} %convolution_bitcast_fusion.2), kind=kLoop, calls=%fused_computation.90 | loop fusion | flops 3407872 | bytes 22937600 | tf_op jit(solution)/shard_map/add | solution.py:99
  70.8 2.5 %convolution_bitcast_fusion.3 = f32[9,256,64]{1,2,0:T(8,128)S(1)} fusion(bf16[8,9,64,2,128]{4,2,3,0,1:T(8,128)(2,1)} %fusion.68, bf16[8,256,2,128]{3,1,2,0:T(8,128)(2,1)S(1)} %copy-done), kind=kOutput, calls=%fused_computation.55 | convolution fusion | flops 603979776 | bytes 3997696 | tf_op jit(solution)/shard_map/hodw,htcdw->toc/dot_general | solution.py:61
  73.3 2.5 %convolution_bitcast_fusion.4 = f32[9,256,64]{1,2,0:T(8,128)S(1)} fusion(bf16[8,9,64,2,128]{4,2,3,0,1:T(8,128)(2,1)} %get-tuple-element.9, bf16[8,256,2,128]{3,1,2,0:T(8,128)(2,1)S(1)} %copy-done), kind=kOutput, calls=%fused_computation.56 | convolution fusion | flops 603979776 | bytes 3997696 | tf_op jit(solution)/shard_map/hodw,htcdw->toc/dot_general | solution.py:61
  75.8 2.6 %fusion.19 = f32[9,256,64]{1,2,0:T(8,128)S(1)} fusion(bf16[8,9,64,2,128]{4,2,1,3,0:T(8,128)(2,1)} %fusion.86, bf16[8,256,2,128]{3,1,2,0:T(8,128)(2,1)S(1)} %copy-done), kind=kOutput, calls=%fused_computation.54 | convolution fusion | flops 603979776 | bytes 3997696 | tf_op jit(solution)/shard_map/hodw,htcdw->toc/dot_general | solution.py:61
  78.3 1.4 pad_maximum_fusion
  80.0 2.7 %fusion.13 = f32[8,2,128,256,1]{3,2,0,1,4:T(8,128)S(1)} fusion(bf16[8,9,64,2,128]{4,2,3,0,1:T(8,128)(2,1)} %get-tuple-element.9, bf16[27,256,64]{1,2,0:T(8,128)(2,1)S(1)} %copy-done.1), kind=kOutput, calls=%fused_computation.40 | convolution fusion | flops 603979776 | bytes 4751360 | tf_op jit(solution)/shard_map/toc,htcdw->hodw/dot_general | solution.py:36
  82.7 2.7 %fusion.11 = f32[8,2,128,256,1]{3,2,0,1,4:T(8,128)S(1)} fusion(bf16[8,9,64,2,128]{4,2,3,0,1:T(8,128)(2,1)} %fusion.68, bf16[27,256,64]{1,2,0:T(8,128)(2,1)S(1)} %copy-done.1), kind=kOutput, calls=%fused_computation.38 | convolution fusion | flops 603979776 | bytes 4751360 | tf_op jit(solution)/shard_map/toc,htcdw->hodw/dot_general | solution.py:36
  85.5 4.1 %fusion.15 = f32[8,256,2,128]{1,3,2,0:T(8,128)} fusion(f32[8,2,128,256,1]{3,2,0,1,4:T(8,128)S(1)} %fusion.11, f32[8,2,128,256,1]{3,2,0,1,4:T(8,128)S(1)} %fusion.13, bf16[8,9,64,2,128]{4,2,1,3,0:T(8,128)(2,1)} %fusion.86, bf16[27,256,64]{1,2,0:T(8,128)(2,1)S(1)} %copy-done.1), kind=kOutput, calls=%fused_computation.43 | convolution fusion | flops 605028352 | bytes 8945664 | tf_op jit(solution)/shard_map/toc,htcdw->hodw/dot_general | solution.py:36
  89.6 1.0 convert_element_type.15
  91.4 17.4 %all-reduce.7.cloned.1.call-done = f32[27,256,64]{1,2,0:T(8,128)} async-done(((f32[27,256,64]{1,2,0:T(8,128)}), f32[27,256,64]{1,2,0:T(8,128)}) %all-reduce.7.cloned.1.call-update) | async-done | bytes 1769488 | tf_op jit(solution)/shard_map/psum | solution.py:113
  108.8 2.9 %broadcast_multiply_fusion = f32[27,256,64]{1,2,0:T(8,128)} fusion(f32[27,256,64]{1,2,0:T(8,128)} %all-reduce.7.cloned.1.call-done), kind=kLoop, calls=%fused_computation.58 | loop fusion | flops 442368 | bytes 3538944 | tf_op jit(solution)/shard_map/mul | solution.py:115
  111.7 69.4 %reduce-scatter.3.cloned.1.call-done = f32[1,256,2,128]{1,3,2,0:T(8,128)} async-done(((f32[8,256,2,128]{1,3,2,0:T(8,128)}), f32[1,256,2,128]{1,3,2,0:T(8,128)}) %reduce-scatter.3.cloned.1.call-update) | async-done | bytes 262160 | tf_op jit(solution)/shard_map/reduce_scatter | solution.py:75
  181.1 1.0 convert_element_type.14
  (44 shorter events, 20.9 us)
Async XLA Ops:
  7.2 49.5 %all-gather.2.cloned.1.call-start = ((), (), s32[]{:S(2)}) async-start(), calls=%async_computation.3 | async-start | bytes 1179648 | tf_op jit(solution)/shard_map/all_gather | solution.py:81
  8.2 5.3 %collective-permute-start = (bf16[8,64,1,128]{3,1,2,0:T(8,128)(2,1)S(1)}, bf16[8,64,1,128]{3,1,2,0:T(8,128)(2,1)S(1)}, u32[]{:S(2)}, u32[]{:S(2)}) collective-permute-start(bf16[8,64,1,128]{3,1,2,0:T(8,128)(2,1)S(1)} %get-tuple-element.25), channel_id=1, source_target_pairs={{0,1},{2,3},{4,5},{6,7},{8,9},{10,11},{12,13},{14,15},{16,17},{18,... | collective-permute-start | bytes 393224 | tf_op jit(solution)/shard_map/ppermute | solution.py:16
  10.6 3.2 %collective-permute-start.1 = (bf16[8,64,1,128]{3,1,2,0:T(8,128)(2,1)S(1)}, bf16[8,64,1,128]{3,1,2,0:T(8,128)(2,1)S(1)}, u32[]{:S(2)}, u32[]{:S(2)}) collective-permute-start(bf16[8,64,1,128]{3,1,2,0:T(8,128)(2,1)S(1)} %get-tuple-element.26), channel_id=1, source_target_pairs={{1,0},{3,2},{5,4},{7,6},{9,8},{11,10},{13,12},{15,14},{17,16},{19,... | collective-permute-start | bytes 393224 | tf_op jit(solution)/shard_map/ppermute | solution.py:17
  13.5 76.1 %reduce-scatter.5.cloned.1.call-start = ((), (), s32[]{:S(2)}) async-start(), calls=%async_computation.4 | async-start | bytes 786432 | tf_op jit(solution)/shard_map/reduce_scatter | solution.py:108
  16.8 5.2 %copy-start.2 = (bf16[8,64,2,128]{3,2,1,0:T(2,128)(2,1)S(1)}, bf16[8,64,2,128]{3,2,1,0:T(2,128)(2,1)}, u32[]{:S(2)}) copy-start(bf16[8,64,2,128]{3,2,1,0:T(2,128)(2,1)} %param.3) | copy-start | bytes 786436
  56.7 6.8 %copy-start = (bf16[8,256,2,128]{3,1,2,0:T(8,128)(2,1)S(1)}, bf16[8,256,2,128]{3,1,2,0:T(8,128)(2,1)}, u32[]{:S(2)}) copy-start(bf16[8,256,2,128]{3,1,2,0:T(8,128)(2,1)} %all-gather.2.cloned.1.call-done) | copy-start | bytes 3145732
  58.0 5.4 %collective-permute-start.2 = (bf16[8,256,1,128]{3,1,2,0:T(8,128)(2,1)S(1)}, bf16[8,256,1,128]{3,1,2,0:T(8,128)(2,1)S(1)}, u32[]{:S(2)}, u32[]{:S(2)}) collective-permute-start(bf16[8,256,1,128]{3,1,2,0:T(8,128)(2,1)S(1)} %get-tuple-element.23), channel_id=1, source_target_pairs={{0,1},{2,3},{4,5},{6,7},{8,9},{10,11},{12,13},{14,15},{16,17},{18,... | collective-permute-start | bytes 1572872 | tf_op jit(solution)/shard_map/ppermute | solution.py:16
  59.4 4.1 %collective-permute-start.3 = (bf16[8,256,1,128]{3,1,2,0:T(8,128)(2,1)S(1)}, bf16[8,256,1,128]{3,1,2,0:T(8,128)(2,1)S(1)}, u32[]{:S(2)}, u32[]{:S(2)}) collective-permute-start(bf16[8,256,1,128]{3,1,2,0:T(8,128)(2,1)S(1)} %get-tuple-element.24), channel_id=1, source_target_pairs={{1,0},{3,2},{5,4},{7,6},{9,8},{11,10},{13,12},{15,14},{17,16},{19,... | collective-permute-start | bytes 1572872 | tf_op jit(solution)/shard_map/ppermute | solution.py:17
  63.4 1.2 copy-start.1
  70.8 38.1 %all-reduce.7.cloned.1.call-start = ((), (), s32[]{:S(2)}) async-start(), calls=%async_computation.5 | async-start | bytes 3538944 | tf_op jit(solution)/shard_map/psum | solution.py:113
  79.7 101.4 %reduce-scatter.3.cloned.1.call-start = ((), (), s32[]{:S(2)}) async-start(), calls=%async_computation.2 | async-start | bytes 2359296 | tf_op jit(solution)/shard_map/reduce_scatter | solution.py:75
Sparse Core Ops, SparseCore 0:
  13.6 42.9 all-gather.1
  70.9 14.0 reduce-scatter.4
  88.1 20.6 all-reduce.6
  112.2 68.8 reduce-scatter.2
where the time goes:
time: 190 us; the launch traced here: 189 us
  waiting for transfers between devices  115 us (61%)
  local copies, waits for them, and re-layouts  21.9 us (12%)
  matrix products  19.9 us (10%)
  between operations  13.9 us (7%)
  other arithmetic  11.9 us (6%)
  starting transfers between devices  6.61 us (3%)
    reduce_scatter x1, waiting for transfers between devices, per_device(): lax.psum_scatter(conv_rows(block, kernel, lax.axis_size('cin') * rows_own...  69.4 us
    all_gather x1, waiting for transfers between devices, per_device(): grad_full = lax.all_gather(grad_out, 'cin', axis=0, tiled=True)  28 us
    unnamed x25, local copies, waits for them, and re-layouts  17.7 us
    psum x1, waiting for transfers between devices, per_device(): summed = lax.psum(local_terms, 'depth')  17.4 us
    dot_general x3, matrix products, conv_rows(): jnp.einsum('toc,htcdw->hodw', weight[9 * depth_off:9 * depth_off + 9], st...  9.56 us
    dot_general x3, matrix products, weight_terms(): jnp.einsum('hodw,htcdw->toc', grad_own, stacked, preferred_element_type=j...  7.5 us
  transfers between devices with their start and end apart: 8, of which 4 were waited for; matrix products, arithmetic and copies ran while one was open for 22% of the time, Pallas kernels for 0%

commit v1 on v0

v1 whole, which is shorter than its diff:
```python
import functools
import math

import jax
import jax.numpy as jnp
from jax import lax
from jax.experimental import pallas as pl
from jax.experimental.pallas import tpu as pltpu
from jax.sharding import PartitionSpec as P

F32 = jnp.float32
BF16 = jnp.bfloat16
VMEM_LIMIT = 48 * 1024 * 1024


def ring_of(size):
    return list(range(0, size, 2)) + list(range(size - 1 - size % 2, 0, -2))


def shifted(x, by):
    width = x.shape[1]
    lane = lax.broadcasted_iota(jnp.int32, x.shape, 1)
    edge = 0 if by == 1 else width - 1
    return jnp.where(lane == edge, 0.0, pltpu.roll(x, by % width, 1))


def forward_kernel(rows_ref, feat_ref, weight_ref, ext_ref, part_ref):
    count, layers, chan, width = feat_ref.shape
    slab = layers - 2
    ext_ref[0] = jnp.zeros(ext_ref.shape[1:], BF16)
    ext_ref[count + 1] = jnp.zeros(ext_ref.shape[1:], BF16)

    @pl.loop(0, count)
    def _(h):
        for d in range(layers):
            x = feat_ref[h, d]
            wide = x.astype(F32)
            cols = slice(d * width, (d + 1) * width)
            ext_ref[h + 1, 0:chan, cols] = shifted(wide, 1).astype(BF16)
            ext_ref[h + 1, chan : 2 * chan, cols] = x
            ext_ref[h + 1, 2 * chan : 3 * chan, cols] = shifted(wide, -1).astype(BF16)

    @pl.loop(0, count)
    def _(k):
        row = rows_ref[k]
        total = None
        for a in range(3):
            right = ext_ref[pl.ds(row, 3), :, a * width : (a + slab) * width]
            right = right.reshape(9 * chan, slab * width)
            term = jnp.dot(weight_ref[a], right, preferred_element_type=F32)
            total = term if total is None else total + term
        part_ref[k] = total


def weight_kernel(rows_ref, ext_ref, *refs):
    grads, acc_ref = refs[:-1], refs[-1]
    chan3 = ext_ref.shape[1]
    cells = grads[0].shape[1]
    width = ext_ref.shape[2] - cells
    width = width // 2
    for a in range(3):
        total = None
        for k, g_ref in enumerate(grads):
            right = ext_ref[pl.ds(rows_ref[k], 3), :, a * width : a * width + cells]
            right = right.reshape(3 * chan3, cells)
            term = lax.dot_general(
                g_ref[...], right, (((1,), (1,)), ((), ())), preferred_element_type=F32
            )
            if k == 0:
                acc_ref[a] = term
            else:
                acc_ref[a] += term


def input_kernel(rows_ref, weight_ref, halo_ref, *refs):
    grads, out_ref, pad_ref = refs[:-2], refs[-2], refs[-1]
    count = len(grads)
    chan = out_ref.shape[1]
    cells = out_ref.shape[2]
    width = halo_ref.shape[3]
    slab = cells // width
    pad_ref[0] = jnp.zeros(pad_ref.shape[1:], BF16)
    pad_ref[count + 1] = jnp.zeros(pad_ref.shape[1:], BF16)
    for k, g_ref in enumerate(grads):
        row = rows_ref[k] + 1
        pad_ref[row, :, 0:width] = halo_ref[0, k]
        pad_ref[row, :, width : width + cells] = g_ref[...]
        pad_ref[row, :, width + cells :] = halo_ref[1, k]

    @pl.loop(0, count)
    def _(h):
        total = None
        for a in range(3):
            right = pad_ref[pl.ds(h, 3), :, (2 - a) * width : (2 - a) * width + cells]
            right = right.reshape(3 * right.shape[1], cells)
            term = jnp.dot(weight_ref[a], right, preferred_element_type=F32)
            total = term if total is None else total + term
        for d in range(slab):
            cols = slice(d * width, (d + 1) * width)
            out_ref[h, :, cols] = (
                shifted(total[0:chan, cols], -1)
                + total[chan : 2 * chan, cols]
                + shifted(total[2 * chan : 3 * chan, cols], 1)
            )


def finish_kernel(scale, own_ref, other_ref, out_ref):
    chan = out_ref.shape[2]
    for a in range(3):
        for j in range(9):
            cols = slice(j * chan, (j + 1) * chan)
            out_ref[9 * a + j] = (own_ref[a, :, cols] + other_ref[a, :, cols]) * scale


def call(kernel, out_shape, args, smem=1, scratch=(), flops=0):
    whole = pl.BlockSpec(memory_space=pltpu.VMEM)
    specs = [pl.BlockSpec(memory_space=pltpu.SMEM)] * smem + [whole] * (len(args) - smem)
    outs = jax.tree.map(lambda _: whole, out_shape)
    moved = sum(x.size * x.dtype.itemsize for x in (*args, *jax.tree.leaves(out_shape)))
    return pl.pallas_call(
        kernel,
        out_shape=out_shape,
        in_specs=specs,
        out_specs=outs,
        scratch_shapes=list(scratch),
        compiler_params=pltpu.CompilerParams(vmem_limit_bytes=VMEM_LIMIT),
        cost_estimate=pl.CostEstimate(flops=flops, bytes_accessed=moved, transcendentals=0),
    )(*args)


def neighbours(x_first, x_last, axis):
    size = lax.axis_size(axis)
    if size == 2:
        here = lax.axis_index(axis)
        sent = jnp.where(here == 0, x_last, x_first)
        got = lax.ppermute(sent, axis, [(0, 1), (1, 0)])
        none = jnp.zeros_like(got)
        return jnp.where(here == 0, none, got), jnp.where(here == 0, got, none)
    up = [(i, i + 1) for i in range(size - 1)]
    down = [(j, i) for i, j in up]
    return lax.ppermute(x_last, axis, up), lax.ppermute(x_first, axis, down)


def per_device(features, kernel, grad_out):
    count, chan, slab, width = features.shape
    outs = kernel.shape[1]
    ring_size = lax.axis_size("cin")
    assert count == ring_size and grad_out.shape[0] == 1
    cells = slab * width
    half = ring_size // 2
    ring = ring_of(ring_size)
    fwd = [(ring[i], ring[(i + 1) % ring_size]) for i in range(ring_size)]
    bwd = [(j, i) for i, j in fwd]
    place = [ring.index(i) for i in range(ring_size)]
    table = jnp.array(
        [[ring[(place[i] + k) % ring_size] for k in range(ring_size)] for i in range(ring_size)],
        jnp.int32,
    )
    rows = lax.dynamic_index_in_dim(table, lax.axis_index("cin"), 0, keepdims=False)

    own = grad_out.reshape(outs, cells)
    grads = [None] * ring_size
    grads[0] = own
    f = b = own
    for s in range(1, half):
        f = lax.ppermute(f, "cin", fwd)
        b = lax.ppermute(b, "cin", bwd)
        grads[ring_size - s] = f
        grads[s] = b
    mid = outs // 2
    f = lax.ppermute(f[:mid], "cin", fwd)
    b = lax.ppermute(b[mid:], "cin", bwd)
    grads[half] = jnp.concatenate([f, b], axis=0)

    before, after = neighbours(features[:, :, :1], features[:, :, slab - 1 :], "depth")
    feat = jnp.concatenate([before, features, after], axis=2).transpose(0, 2, 1, 3)
    taps = kernel.reshape(3, 9, outs, chan)
    w_out = taps.transpose(0, 2, 1, 3).reshape(3, outs, 9 * chan)
    flops = 2 * 27 * outs * chan * count * cells
    ext, part = call(
        forward_kernel,
        (
            jax.ShapeDtypeStruct((count + 2, 3 * chan, cells + 2 * width), BF16),
            jax.ShapeDtypeStruct((count, outs, cells), F32),
        ),
        (rows, feat, w_out),
        flops=flops,
    )
    f = lax.ppermute(part[half, :mid], "cin", fwd)
    b = lax.ppermute(part[half, mid:], "cin", bwd)
    f = jnp.concatenate([part[half - 1, :mid] + f, part[half - 1, mid:]])
    b = jnp.concatenate([part[half + 1, :mid], part[half + 1, mid:] + b])
    for s in range(half - 2, -1, -1):
        f = lax.ppermute(f, "cin", fwd)
        b = lax.ppermute(b, "cin", bwd)
        if s:
            f = f + part[s]
            b = b + part[ring_size - s]
    output = (part[0] + f + b).astype(BF16).reshape(1, outs, slab, width)

    acc = call(
        weight_kernel,
        jax.ShapeDtypeStruct((3, outs, 9 * chan), F32),
        (rows, ext, *grads),
        flops=flops,
    )
    scale = 1.0 / math.sqrt(count * cells * lax.axis_size("depth"))
    if lax.axis_size("depth") == 2:
        other = lax.ppermute(acc, "depth", [(0, 1), (1, 0)])
    else:
        other = lax.psum(acc, "depth") - acc
    kernel_grad = call(
        functools.partial(finish_kernel, scale),
        jax.ShapeDtypeStruct((27, outs, chan), F32),
        (acc, other),
        smem=0,
    )

    stack = jnp.stack(grads)
    before, after = neighbours(stack[:, :, :width], stack[:, :, cells - width :], "depth")
    halo = jnp.stack([before, after])
    w_in = (
        kernel.reshape(3, 3, 3, outs, chan)[:, ::-1]
        .transpose(0, 2, 4, 1, 3)
        .reshape(3, 3 * chan, 3 * outs)
    )
    back = call(
        input_kernel,
        jax.ShapeDtypeStruct((count, chan, cells), F32),
        (rows, w_in, halo, *grads),
        scratch=[pltpu.VMEM((count + 2, outs, cells + 2 * width), BF16)],
        flops=flops,
    )
    parts = lax.axis_size("cout")
    if parts == 2:
        here = lax.axis_index("cout")
        halves = back.reshape(2, count // 2, chan, cells)
        mine = jnp.where(here == 0, halves[0], halves[1])
        sent = jnp.where(here == 0, halves[1], halves[0])
        total = mine + lax.ppermute(sent, "cout", [(0, 1), (1, 0)])
    else:
        total = lax.psum_scatter(back, "cout", scatter_dimension=0, tiled=True)
    input_grad = total.astype(BF16).reshape(count // parts, chan, slab, width)
    return (output, input_grad, kernel_grad)


def solution(mesh):
    return jax.shard_map(
        per_device,
        mesh=mesh,
        in_specs=(
            P(None, "cin", "depth", None),
            P(None, "cout", "cin"),
            P("cin", "cout", "depth", None),
        ),
        out_specs=(
            P("cin", "cout", "depth", None),
            P("cout", "cin", "depth", None),
            P(None, "cout", "cin"),
        ),
        check_vma=False,
    )
```

time: 190 us -> 85.4 us (0.45)
  waiting for transfers between devices: 115 us -> 18.8 us
  matrix products: 19.9 us -> 0 us
  Pallas kernels: 0 us -> 15.4 us
  between operations: 13.9 us -> 1.08 us
  starting transfers between devices: 6.61 us -> 19.2 us
  other arithmetic: 11.9 us -> 5.49 us
  local copies, waits for them, and re-layouts: 21.9 us -> 25 us
    reduce_scatter x2 -> x0, waiting for transfers between devices: 69.5 us -> none  [the longest x1 69.4 us: per_device(): lax.psum_scatter(conv_rows(block, kernel, lax.axis_size('cin') * rows_own...]
    all_gather x1 -> x0, waiting for transfers between devices: 28 us -> none  [per_device(): grad_full = lax.all_gather(grad_out, 'cin', axis=0, tiled=True)]
    dot_general x9 -> x0, matrix products: 19.9 us -> none  [the longest x3 9.56 us: conv_rows(): jnp.einsum('toc,htcdw->hodw', weight[9 * depth_off:9 * depth_off + 9], st...]
    ppermute x4 -> x20, waiting for transfers between devices: 0.29 us -> 18.8 us  [the longest x6 5.93 us: per_device(): f = lax.ppermute(f, 'cin', fwd)]
    psum x1 -> x0, waiting for transfers between devices: 17.4 us -> none  [per_device(): summed = lax.psum(local_terms, 'depth')]
    pallas_call x0 -> x4, Pallas kernels: none -> 15.4 us  [call(): pl.pallas_call(kernel, out_shape=out_shape, in_specs=specs, out_specs=out...]
    ppermute x4 -> x20, starting transfers between devices: 6.27 us -> 19.2 us  [the longest x6 11.9 us: per_device(): f = lax.ppermute(f, 'cin', fwd)]
    unnamed x25 -> x45, local copies, waits for them, and re-layouts: 17.7 us -> 7.14 us
  transfers between devices with their start and end apart: 8 -> 20, of which waited for: 4 -> 7; matrix products, arithmetic and copies ran while one was open for 22% -> 25% of each run, Pallas kernels for 0% -> 15%
where the time goes in v1:
time: 85.4 us; the launch traced here: 84.9 us
  local copies, waits for them, and re-layouts  25 us (29%)
  starting transfers between devices  19.2 us (22%)
  waiting for transfers between devices  18.8 us (22%)
  Pallas kernels  15.4 us (18%)
  other arithmetic  5.49 us (6%)
  between operations  1.08 us (1%)
    pallas_call x4, Pallas kernels, call(): pl.pallas_call(kernel, out_shape=out_shape, in_specs=specs, out_specs=out...  15.4 us
    ppermute x6, starting transfers between devices, per_device(): f = lax.ppermute(f, 'cin', fwd)  11.9 us
    unnamed x45, local copies, waits for them, and re-layouts  7.14 us
    ppermute x6, waiting for transfers between devices, per_device(): f = lax.ppermute(f, 'cin', fwd)  5.93 us
    rev x1, local copies, waits for them, and re-layouts, per_device(): kernel.reshape(3, 3, 3, outs, chan)[:, ::-1].transpose(0, 2, 4, 1, 3)  4.91 us
    ppermute x1, waiting for transfers between devices, per_device(): total = mine + lax.ppermute(sent, 'cout', [(0, 1), (1, 0)])  4.61 us
    ppermute x1, local copies, waits for them, and re-layouts, per_device(): other = lax.ppermute(acc, 'depth', [(0, 1), (1, 0)])  2.8 us
    reshape x1, local copies, waits for them, and re-layouts, per_device(): w_in = kernel.reshape(3, 3, 3, outs, chan)[:, ::-1].transpose(0, 2, 4, 1,...  2.68 us
  transfers between devices with their start and end apart: 20, of which 7 were waited for; matrix products, arithmetic and copies ran while one was open for 25% of the time, Pallas kernels for 15%

profile of v1, /device:TPU:0, one launch (start us, length us, event | category | flops | bytes accessed | tf_op | source)
XLA Modules:
  0.0 84.9 jit_solution(11993271566218771352)
XLA Ops:
  1.7 3.1 %collective-permute-start.12 = (bf16[256,256]{1,0:T(8,128)(2,1)S(1)}, bf16[256,256]{1,0:T(8,128)(2,1)S(1)}, u32[]{:S(2)}, u32[]{:S(2)}) collective-permute-start(bf16[256,256]{1,0:T(8,128)(2,1)S(1)} %bitcast.60), channel_id=1, source_target_pairs={{0,8},{8,16},{16,24},{24,28},{28,20},{20,12},{12,4},{4,0},{1,9},{9... | collective-permute-start | bytes 393224 | tf_op jit(solution)/shard_map/ppermute | solution.py:166
  8.4 5.1 %shard_map.67 = (bf16[10,192,512]{2,1,0:T(8,128)(2,1)S(1)}, f32[8,256,256]{2,1,0:T(8,128)S(1)}) custom-call(s32[8]{0:T(128)S(1)} %dynamic-slice_bitcast_fusion.rows_ref, bf16[8,4,64,128]{3,2,1,0:T(8,128)(2,1)S(1)} %maximum_bitcast_fusion.feat_ref, bf16[3,256,576]{2,1,0:T(8,128)(2,1)S(1)} %copy.22.weight_ref), custom_call_target="tpu_custom_call" | custom-call | flops 1811939328 | bytes 5472288 | tf_op jit(solution)/shard_map/pallas_call | solution.py:120
  13.5 2.1 %collective-permute-start.1 = (f32[128,256]{1,0:T(8,128)S(1)}, f32[128,256]{1,0:T(8,128)S(1)}, u32[]{:S(2)}, u32[]{:S(2)}) collective-permute-start(f32[128,256]{1,0:T(8,128)S(1)} %get-tuple-element.22), channel_id=1, source_target_pairs={{0,8},{8,16},{16,24},{24,28},{28,20},{20,12},{12,4},{4,0},{1,9},{9... | collective-permute-start | bytes 393224 | tf_op jit(solution)/shard_map/ppermute | solution.py:189
  15.6 2.0 %collective-permute-start.13 = (bf16[256,256]{1,0:T(8,128)(2,1)S(1)}, bf16[256,256]{1,0:T(8,128)(2,1)S(1)}, u32[]{:S(2)}, u32[]{:S(2)}) collective-permute-start(bf16[256,256]{1,0:T(8,128)(2,1)S(1)} %collective-permute-done.12.refs_7_), channel_id=1, source_target_pairs={{0,8},{8,16},{16,24},{24,28},{28,20},{20,12},{12,4},{4,0},{1,9},{9... | collective-permute-start | bytes 393224 | tf_op jit(solution)/shard_map/ppermute | solution.py:166
  17.7 2.2 %collective-permute-done.1 = f32[128,256]{1,0:T(8,128)S(1)} collective-permute-done((f32[128,256]{1,0:T(8,128)S(1)}, f32[128,256]{1,0:T(8,128)S(1)}, u32[]{:S(2)}, u32[]{:S(2)}) %collective-permute-start.1) | collective-permute-done | bytes 131104 | tf_op jit(solution)/shard_map/ppermute | solution.py:189
  20.0 2.0 %collective-permute-done.5 = f32[128,256]{1,0:T(8,128)S(1)} collective-permute-done((f32[128,256]{1,0:T(8,128)S(1)}, f32[128,256]{1,0:T(8,128)S(1)}, u32[]{:S(2)}, u32[]{:S(2)}) %collective-permute-start.5) | collective-permute-done | bytes 131104 | tf_op jit(solution)/shard_map/ppermute | solution.py:190
  22.1 2.1 %collective-permute-start.2 = (f32[256,256]{1,0:T(8,128)S(1)}, f32[256,256]{1,0:T(8,128)S(1)}, u32[]{:S(2)}, u32[]{:S(2)}) collective-permute-start(f32[256,256]{1,0:T(8,128)S(1)} %pad_maximum_fusion.1), channel_id=1, source_target_pairs={{0,8},{8,16},{16,24},{24,28},{28,20},{20,12},{12,4},{4,0},{1,9},{9... | collective-permute-start | bytes 786440 | tf_op jit(solution)/shard_map/ppermute | solution.py:194
  24.2 1.6 %collective-permute-start.14 = (bf16[256,256]{1,0:T(8,128)(2,1)S(1)}, bf16[256,256]{1,0:T(8,128)(2,1)S(1)}, u32[]{:S(2)}, u32[]{:S(2)}) collective-permute-start(bf16[256,256]{1,0:T(8,128)(2,1)S(1)} %collective-permute-done.13.refs_6_), channel_id=1, source_target_pairs={{0,8},{8,16},{16,24},{24,28},{28,20},{20,12},{12,4},{4,0},{1,9},{9... | collective-permute-start | bytes 393224 | tf_op jit(solution)/shard_map/ppermute | solution.py:166
  26.2 5.9 %collective-permute-done.14.refs_5_ = bf16[256,256]{1,0:T(8,128)(2,1)S(1)} collective-permute-done((bf16[256,256]{1,0:T(8,128)(2,1)S(1)}, bf16[256,256]{1,0:T(8,128)(2,1)S(1)}, u32[]{:S(2)}, u32[]{:S(2)}) %collective-permute-start.14) | collective-permute-done | bytes 131104 | tf_op jit(solution)/shard_map/ppermute | solution.py:166
  34.3 2.2 %collective-permute-done.15 = bf16[128,256]{1,0:T(8,128)(2,1)S(1)} collective-permute-done((bf16[128,256]{1,0:T(8,128)(2,1)S(1)}, bf16[128,256]{1,0:T(8,128)(2,1)S(1)}, u32[]{:S(2)}, u32[]{:S(2)}) %collective-permute-start.15) | collective-permute-done | bytes 65568 | tf_op jit(solution)/shard_map/ppermute | solution.py:171
  39.8 1.6 %collective-permute-start.3 = (f32[256,256]{1,0:T(8,128)}, f32[256,256]{1,0:T(8,128)}, u32[]{:S(2)}, u32[]{:S(2)}) collective-permute-start(f32[256,256]{1,0:T(8,128)} %get-tuple-element.18), channel_id=1, source_target_pairs={{0,8},{8,16},{16,24},{24,28},{28,20},{20,12},{12,4},{4,0},{1,9},{9... | collective-permute-start | bytes 786440 | tf_op jit(solution)/shard_map/ppermute | solution.py:194
  41.8 3.2 %shard_map.69.own_ref = f32[3,256,576]{2,1,0:T(8,128)S(1)} custom-call(s32[8]{0:T(128)S(1)} %dynamic-slice_bitcast_fusion.rows_ref, bf16[10,192,512]{2,1,0:T(8,128)(2,1)S(1)} %get-tuple-element.6.ext_ref, bf16[256,256]{1,0:T(8,128)(2,1)S(1)} %bitcast.62, bf16[256,256]{1,0:T(8,128)(2,1)S(1)} %collective-permute-done.9.refs_1_, ...), custom_call_target="tpu_custom_call" | custom-call | flops 1811939328 | bytes 4784160 | tf_op jit(solution)/shard_map/pallas_call | solution.py:120
  45.1 1.7 %copy.24 = f32[3,256,576]{1,2,0:T(8,128)} copy(f32[3,256,576]{2,1,0:T(8,128)S(1)} %shard_map.69.own_ref) | data formatting | bytes 3538944 | tf_op jit(solution)/shard_map/pallas_call | solution.py:120
  46.8 1.9 %copy.23 = bf16[3,3,3,256,64]{3,1,4,2,0:T(4,128)(2,1)S(1)} copy(bf16[3,3,3,256,64]{3,4,2,1,0:T(8,128)(2,1)} %bitcast.65) | data formatting | bytes 1769472 | tf_op jit(solution)/shard_map/reshape | solution.py:223
  48.7 4.9 %rev.3 = bf16[3,3,3,256,64]{3,1,4,2,0:T(4,128)(2,1)} reverse(bf16[3,3,3,256,64]{3,1,4,2,0:T(4,128)(2,1)S(1)} %copy.23), dimensions={1} | reverse | bytes 1769472 | tf_op jit(solution)/shard_map/rev | solution.py:223
  53.6 2.7 %reshape.36.weight_ref = bf16[3,192,768]{2,1,0:T(8,128)(2,1)S(1)} reshape(bf16[3,3,64,3,256]{4,3,2,1,0:T(4,128)(2,1)} %bitcast.64) | data formatting | bytes 1769472 | tf_op jit(solution)/shard_map/reshape | solution.py:225
  57.7 1.6 %collective-permute-start.4 = (f32[256,256]{1,0:T(8,128)S(1)}, f32[256,256]{1,0:T(8,128)S(1)}, u32[]{:S(2)}, u32[]{:S(2)}) collective-permute-start(f32[256,256]{1,0:T(8,128)S(1)} %get-tuple-element.16), channel_id=1, source_target_pairs={{0,8},{8,16},{16,24},{24,28},{28,20},{20,12},{12,4},{4,0},{1,9},{9... | collective-permute-start | bytes 786440 | tf_op jit(solution)/shard_map/ppermute | solution.py:194
  61.0 4.7 %shard_map.68 = f32[8,64,256]{2,1,0:T(8,128)S(1)} custom-call(s32[8]{0:T(128)S(1)} %dynamic-slice_bitcast_fusion.rows_ref, bf16[3,192,768]{2,1,0:T(8,128)(2,1)S(1)} %reshape.36.weight_ref, bf16[2,8,256,128]{3,2,1,0:T(8,128)(2,1)S(1)} %pad_maximum_fusion.halo_ref, bf16[256,256]{1,0:T(8,128)(2,1)S(1)} %bitcast.63, bf16[256,256]{1,0:T(8,128)(2,1)S(1)} %copy-done.11, ...), custom_call_target="tpu_custom_call" | custom-call | flops 1811939328 | bytes 3506208 | tf_op jit(solution)/shard_map/pallas_call | solution.py:120
  65.8 1.6 %collective-permute-start.18 = (f32[4,64,256]{2,1,0:T(8,128)S(1)}, f32[4,64,256]{2,1,0:T(8,128)S(1)}, u32[]{:S(2)}, u32[]{:S(2)}) collective-permute-start(f32[4,64,256]{2,1,0:T(8,128)S(1)} %slice_select_fusion.1), channel_id=1, source_target_pairs={{0,2},{2,0},{1,3},{3,1},{4,6},{6,4},{5,7},{7,5},{8,10},{10,8},{9,1... | collective-permute-start | bytes 786440 | tf_op jit(solution)/shard_map/ppermute | solution.py:240
  69.4 4.6 %collective-permute-done.18 = f32[4,64,256]{2,1,0:T(8,128)S(1)} collective-permute-done((f32[4,64,256]{2,1,0:T(8,128)S(1)}, f32[4,64,256]{2,1,0:T(8,128)S(1)}, u32[]{:S(2)}, u32[]{:S(2)}) %collective-permute-start.18) | collective-permute-done | bytes 262176 | tf_op jit(solution)/shard_map/ppermute | solution.py:240
  74.8 2.8 %copy.25.other_ref = f32[3,256,576]{2,1,0:T(8,128)} copy(f32[3,256,576]{1,2,0:T(8,128)} %collective-permute-done.19) | data formatting | bytes 3538944 | tf_op jit(solution)/shard_map/ppermute | solution.py:209
  77.6 1.5 %copy-done = f32[3,256,576]{2,1,0:T(8,128)S(1)} copy-done((f32[3,256,576]{2,1,0:T(8,128)S(1)}, f32[3,256,576]{2,1,0:T(8,128)}, u32[]{:S(2)}) %copy-start) | copy-done | bytes 1769496
  79.1 2.4 %shard_map.70 = f32[27,256,64]{2,1,0:T(8,128)} custom-call(f32[3,256,576]{2,1,0:T(8,128)S(1)} %shard_map.69.own_ref, f32[3,256,576]{2,1,0:T(8,128)S(1)} %copy-done), custom_call_target="tpu_custom_call" | custom-call | bytes 5308416 | tf_op jit(solution)/shard_map/pallas_call | solution.py:120
  81.5 3.4 %copy.26 = f32[27,256,64]{1,2,0:T(8,128)} copy(f32[27,256,64]{2,1,0:T(8,128)} %shard_map.70) | data formatting | bytes 3538944
  (94 shorter events, 16.9 us)
Async XLA Ops:
  1.6 40.2 %copy-start.6 = (bf16[32,8,2,128]{3,1,2,0:T(8,128)(2,1)}, bf16[32,8,2,128]{3,1,2,0:T(8,128)(2,1)S(1)}, u32[]{:S(2)}) copy-start(bf16[32,8,2,128]{3,1,2,0:T(8,128)(2,1)S(1)} %copy.29) | copy-start | bytes 393220
  1.7 14.0 %collective-permute-start.12 = (bf16[256,256]{1,0:T(8,128)(2,1)S(1)}, bf16[256,256]{1,0:T(8,128)(2,1)S(1)}, u32[]{:S(2)}, u32[]{:S(2)}) collective-permute-start(bf16[256,256]{1,0:T(8,128)(2,1)S(1)} %bitcast.60), channel_id=1, source_target_pairs={{0,8},{8,16},{16,24},{24,28},{28,20},{20,12},{12,4},{4,0},{1,9},{9... | collective-permute-start | bytes 393224 | tf_op jit(solution)/shard_map/ppermute | solution.py:166
  4.7 12.9 %collective-permute-start.9 = (bf16[256,256]{1,0:T(8,128)(2,1)S(1)}, bf16[256,256]{1,0:T(8,128)(2,1)S(1)}, u32[]{:S(2)}, u32[]{:S(2)}) collective-permute-start(bf16[256,256]{1,0:T(8,128)(2,1)S(1)} %bitcast.61), channel_id=1, source_target_pairs={{8,0},{16,8},{24,16},{28,24},{20,28},{12,20},{4,12},{0,4},{9,1},{1... | collective-permute-start | bytes 393224 | tf_op jit(solution)/shard_map/ppermute | solution.py:167
  5.8 2.5 %collective-permute-start = (bf16[8,64,1,128]{3,1,2,0:T(8,128)(2,1)S(1)}, bf16[8,64,1,128]{3,1,2,0:T(8,128)(2,1)S(1)}, u32[]{:S(2)}, u32[]{:S(2)}) collective-permute-start(bf16[8,64,1,128]{3,1,2,0:T(8,128)(2,1)S(1)} %slice_select_fusion.2), channel_id=1, source_target_pairs={{0,1},{1,0},{2,3},{3,2},{4,5},{5,4},{6,7},{7,6},{8,9},{9,8},{10,11... | collective-permute-start | bytes 393224 | tf_op jit(solution)/shard_map/ppermute | solution.py:136
  13.5 25.4 %copy-start.1 = (f32[8,256,256]{2,1,0:T(8,128)}, f32[8,256,256]{2,1,0:T(8,128)S(1)}, u32[]{:S(2)}) copy-start(f32[8,256,256]{2,1,0:T(8,128)S(1)} %get-tuple-element.5) | copy-start | bytes 6291460
  13.5 6.4 %collective-permute-start.1 = (f32[128,256]{1,0:T(8,128)S(1)}, f32[128,256]{1,0:T(8,128)S(1)}, u32[]{:S(2)}, u32[]{:S(2)}) collective-permute-start(f32[128,256]{1,0:T(8,128)S(1)} %get-tuple-element.22), channel_id=1, source_target_pairs={{0,8},{8,16},{16,24},{24,28},{28,20},{20,12},{12,4},{4,0},{1,9},{9... | collective-permute-start | bytes 393224 | tf_op jit(solution)/shard_map/ppermute | solution.py:189
  15.6 6.3 %collective-permute-start.5 = (f32[128,256]{1,0:T(8,128)S(1)}, f32[128,256]{1,0:T(8,128)S(1)}, u32[]{:S(2)}, u32[]{:S(2)}) collective-permute-start(f32[128,256]{1,0:T(8,128)S(1)} %get-tuple-element.23), channel_id=1, source_target_pairs={{8,0},{16,8},{24,16},{28,24},{20,28},{12,20},{4,12},{0,4},{9,1},{1... | collective-permute-start | bytes 393224 | tf_op jit(solution)/shard_map/ppermute | solution.py:190
  15.6 26.2 %copy-start.8 = (bf16[256,256]{1,0:T(8,128)(2,1)}, bf16[256,256]{1,0:T(8,128)(2,1)S(1)}, u32[]{:S(2)}) copy-start(bf16[256,256]{1,0:T(8,128)(2,1)S(1)} %collective-permute-done.12.refs_7_) | copy-start | bytes 393220
  15.6 8.5 %collective-permute-start.13 = (bf16[256,256]{1,0:T(8,128)(2,1)S(1)}, bf16[256,256]{1,0:T(8,128)(2,1)S(1)}, u32[]{:S(2)}, u32[]{:S(2)}) collective-permute-start(bf16[256,256]{1,0:T(8,128)(2,1)S(1)} %collective-permute-done.12.refs_7_), channel_id=1, source_target_pairs={{0,8},{8,16},{16,24},{24,28},{28,20},{20,12},{12,4},{4,0},{1,9},{9... | collective-permute-start | bytes 393224 | tf_op jit(solution)/shard_map/ppermute | solution.py:166
  17.7 24.2 %copy-start.10 = (bf16[256,256]{1,0:T(8,128)(2,1)}, bf16[256,256]{1,0:T(8,128)(2,1)S(1)}, u32[]{:S(2)}) copy-start(bf16[256,256]{1,0:T(8,128)(2,1)S(1)} %collective-permute-done.9.refs_1_) | copy-start | bytes 393220
  17.7 8.1 %collective-permute-start.10 = (bf16[256,256]{1,0:T(8,128)(2,1)S(1)}, bf16[256,256]{1,0:T(8,128)(2,1)S(1)}, u32[]{:S(2)}, u32[]{:S(2)}) collective-permute-start(bf16[256,256]{1,0:T(8,128)(2,1)S(1)} %collective-permute-done.9.refs_1_), channel_id=1, source_target_pairs={{8,0},{16,8},{24,16},{28,24},{20,28},{12,20},{4,12},{0,4},{9,1},{1... | collective-permute-start | bytes 393224 | tf_op jit(solution)/shard_map/ppermute | solution.py:167
  22.0 16.9 %collective-permute-start.6 = (f32[256,256]{1,0:T(8,128)S(1)}, f32[256,256]{1,0:T(8,128)S(1)}, u32[]{:S(2)}, u32[]{:S(2)}) collective-permute-start(f32[256,256]{1,0:T(8,128)S(1)} %pad_maximum_fusion.2), channel_id=1, source_target_pairs={{8,0},{16,8},{24,16},{28,24},{20,28},{12,20},{4,12},{0,4},{9,1},{1... | collective-permute-start | bytes 786440 | tf_op jit(solution)/shard_map/ppermute | solution.py:195
  22.1 16.8 %collective-permute-start.2 = (f32[256,256]{1,0:T(8,128)S(1)}, f32[256,256]{1,0:T(8,128)S(1)}, u32[]{:S(2)}, u32[]{:S(2)}) collective-permute-start(f32[256,256]{1,0:T(8,128)S(1)} %pad_maximum_fusion.1), channel_id=1, source_target_pairs={{0,8},{8,16},{16,24},{24,28},{28,20},{20,12},{12,4},{4,0},{1,9},{9... | collective-permute-start | bytes 786440 | tf_op jit(solution)/shard_map/ppermute | solution.py:194
  24.2 8.0 %collective-permute-start.14 = (bf16[256,256]{1,0:T(8,128)(2,1)S(1)}, bf16[256,256]{1,0:T(8,128)(2,1)S(1)}, u32[]{:S(2)}, u32[]{:S(2)}) collective-permute-start(bf16[256,256]{1,0:T(8,128)(2,1)S(1)} %collective-permute-done.13.refs_6_), channel_id=1, source_target_pairs={{0,8},{8,16},{16,24},{24,28},{28,20},{20,12},{12,4},{4,0},{1,9},{9... | collective-permute-start | bytes 393224 | tf_op jit(solution)/shard_map/ppermute | solution.py:166
  25.8 7.8 %collective-permute-start.11 = (bf16[256,256]{1,0:T(8,128)(2,1)S(1)}, bf16[256,256]{1,0:T(8,128)(2,1)S(1)}, u32[]{:S(2)}, u32[]{:S(2)}) collective-permute-start(bf16[256,256]{1,0:T(8,128)(2,1)S(1)} %collective-permute-done.10.refs_2_), channel_id=1, source_target_pairs={{8,0},{16,8},{24,16},{28,24},{20,28},{12,20},{4,12},{0,4},{9,1},{1... | collective-permute-start | bytes 393224 | tf_op jit(solution)/shard_map/ppermute | solution.py:167
  32.1 4.3 %collective-permute-start.15 = (bf16[128,256]{1,0:T(8,128)(2,1)S(1)}, bf16[128,256]{1,0:T(8,128)(2,1)S(1)}, u32[]{:S(2)}, u32[]{:S(2)}) collective-permute-start(bf16[128,256]{1,0:T(8,128)(2,1)S(1)} %slice.82), channel_id=1, source_target_pairs={{0,8},{8,16},{16,24},{24,28},{28,20},{20,12},{12,4},{4,0},{1,9},{9... | collective-permute-start | bytes 196616 | tf_op jit(solution)/shard_map/ppermute | solution.py:171
  33.6 4.3 %collective-permute-start.16 = (bf16[128,256]{1,0:T(8,128)(2,1)S(1)}, bf16[128,256]{1,0:T(8,128)(2,1)S(1)}, u32[]{:S(2)}, u32[]{:S(2)}) collective-permute-start(bf16[128,256]{1,0:T(8,128)(2,1)S(1)} %slice.83), channel_id=1, source_target_pairs={{8,0},{16,8},{24,16},{28,24},{20,28},{12,20},{4,12},{0,4},{9,1},{1... | collective-permute-start | bytes 196616 | tf_op jit(solution)/shard_map/ppermute | solution.py:172
  38.9 20.9 %collective-permute-start.17 = (bf16[8,256,128]{2,1,0:T(8,128)(2,1)}, bf16[8,256,128]{2,1,0:T(8,128)(2,1)}, u32[]{:S(2)}, u32[]{:S(2)}) collective-permute-start(bf16[8,256,128]{2,1,0:T(8,128)(2,1)} %slice_select_fusion), channel_id=1, source_target_pairs={{0,1},{1,0},{2,3},{3,2},{4,5},{5,4},{6,7},{7,6},{8,9},{9,8},{10,11... | collective-permute-start | bytes 1572872 | tf_op jit(solution)/shard_map/ppermute | solution.py:136
  39.8 16.5 %collective-permute-start.3 = (f32[256,256]{1,0:T(8,128)}, f32[256,256]{1,0:T(8,128)}, u32[]{:S(2)}, u32[]{:S(2)}) collective-permute-start(f32[256,256]{1,0:T(8,128)} %get-tuple-element.18), channel_id=1, source_target_pairs={{0,8},{8,16},{16,24},{24,28},{28,20},{20,12},{12,4},{4,0},{1,9},{9... | collective-permute-start | bytes 786440 | tf_op jit(solution)/shard_map/ppermute | solution.py:194
  41.4 15.0 %collective-permute-start.7 = (f32[256,256]{1,0:T(8,128)}, f32[256,256]{1,0:T(8,128)}, u32[]{:S(2)}, u32[]{:S(2)}) collective-permute-start(f32[256,256]{1,0:T(8,128)} %get-tuple-element.19), channel_id=1, source_target_pairs={{8,0},{16,8},{24,16},{28,24},{20,28},{12,20},{4,12},{0,4},{9,1},{1... | collective-permute-start | bytes 786440 | tf_op jit(solution)/shard_map/ppermute | solution.py:195
  46.8 28.0 %collective-permute-start.19 = (f32[3,256,576]{1,2,0:T(8,128)}, f32[3,256,576]{1,2,0:T(8,128)}, u32[]{:S(2)}, u32[]{:S(2)}) collective-permute-start(f32[3,256,576]{1,2,0:T(8,128)} %copy.24), channel_id=1, source_target_pairs={{0,1},{1,0},{2,3},{3,2},{4,5},{5,4},{6,7},{7,6},{8,9},{9,8},{10,11... | collective-permute-start | bytes 5308424 | tf_op jit(solution)/shard_map/ppermute | solution.py:209
  57.7 9.7 %collective-permute-start.4 = (f32[256,256]{1,0:T(8,128)S(1)}, f32[256,256]{1,0:T(8,128)S(1)}, u32[]{:S(2)}, u32[]{:S(2)}) collective-permute-start(f32[256,256]{1,0:T(8,128)S(1)} %get-tuple-element.16), channel_id=1, source_target_pairs={{0,8},{8,16},{16,24},{24,28},{28,20},{20,12},{12,4},{4,0},{1,9},{9... | collective-permute-start | bytes 786440 | tf_op jit(solution)/shard_map/ppermute | solution.py:194
  59.3 8.4 %collective-permute-start.8 = (f32[256,256]{1,0:T(8,128)S(1)}, f32[256,256]{1,0:T(8,128)S(1)}, u32[]{:S(2)}, u32[]{:S(2)}) collective-permute-start(f32[256,256]{1,0:T(8,128)S(1)} %get-tuple-element.17), channel_id=1, source_target_pairs={{8,0},{16,8},{24,16},{28,24},{20,28},{12,20},{4,12},{0,4},{9,1},{1... | collective-permute-start | bytes 786440 | tf_op jit(solution)/shard_map/ppermute | solution.py:195
  65.8 8.2 %collective-permute-start.18 = (f32[4,64,256]{2,1,0:T(8,128)S(1)}, f32[4,64,256]{2,1,0:T(8,128)S(1)}, u32[]{:S(2)}, u32[]{:S(2)}) collective-permute-start(f32[4,64,256]{2,1,0:T(8,128)S(1)} %slice_select_fusion.1), channel_id=1, source_target_pairs={{0,2},{2,0},{1,3},{3,1},{4,6},{6,4},{5,7},{7,5},{8,10},{10,8},{9,1... | collective-permute-start | bytes 786440 | tf_op jit(solution)/shard_map/ppermute | solution.py:240
  (13 other events, 78.0 us)

commit v2 on v1

v2 whole, which is shorter than its diff:
```python
import functools
import math

import jax
import jax.numpy as jnp
from jax import lax
from jax.experimental import pallas as pl
from jax.experimental.pallas import tpu as pltpu
from jax.sharding import PartitionSpec as P

F32 = jnp.float32
BF16 = jnp.bfloat16
VMEM_LIMIT = 8 * 1024 * 1024


def ring_of(size):
    return list(range(0, size, 2)) + list(range(size - 1 - size % 2, 0, -2))


def shifted(x, by):
    width = x.shape[1]
    lane = lax.broadcasted_iota(jnp.int32, x.shape, 1)
    edge = 0 if by == 1 else width - 1
    return jnp.where(lane == edge, 0.0, pltpu.roll(x, by % width, 1))


def extend_kernel(feat_ref, ext_ref):
    count, layers, chan, width = feat_ref.shape
    ext_ref[0] = jnp.zeros(ext_ref.shape[1:], BF16)
    ext_ref[count + 1] = jnp.zeros(ext_ref.shape[1:], BF16)

    @pl.loop(0, count)
    def _(h):
        for d in range(layers):
            x = feat_ref[h, d]
            wide = x.astype(F32)
            cols = slice(d * width, (d + 1) * width)
            ext_ref[h + 1, 0:chan, cols] = shifted(wide, 1).astype(BF16)
            ext_ref[h + 1, chan : 2 * chan, cols] = x
            ext_ref[h + 1, 2 * chan : 3 * chan, cols] = shifted(wide, -1).astype(BF16)


def forward_kernel(offsets, width, rows_ref, ext_ref, weight_ref, *part_refs):
    chan3 = ext_ref.shape[1]
    cells = ext_ref.shape[2] - 2 * width
    for k, part_ref in zip(offsets, part_refs):
        row = rows_ref[k]
        total = None
        for a in range(3):
            right = ext_ref[pl.ds(row, 3), :, a * width : a * width + cells]
            right = right.reshape(3 * chan3, cells)
            term = jnp.dot(weight_ref[a], right, preferred_element_type=F32)
            total = term if total is None else total + term
        part_ref[...] = total


def weight_kernel(offsets, width, first, rows_ref, ext_ref, *refs):
    size = len(offsets)
    grads = refs[:size]
    acc_ref, token_ref = refs[-2:]
    token_ref[...] = jnp.zeros(token_ref.shape, F32)
    chan3 = ext_ref.shape[1]
    cells = grads[0].shape[1]
    for a in range(3):
        for b in range(3):
            part = slice(b * chan3, (b + 1) * chan3)
            total = None if first else refs[size][a, part]
            for k, g_ref in zip(offsets, grads):
                left = ext_ref[rows_ref[k] + b, :, a * width : a * width + cells]
                term = lax.dot_general(
                    left, g_ref[...], (((1,), (1,)), ((), ())), preferred_element_type=F32
                )
                total = term if total is None else total + term
            acc_ref[a, part] = total


def input_kernel(offsets, first, rows_ref, here_ref, weight_ref, halo_ref, *refs):
    size = len(offsets)
    grads = refs[:size]
    acc_ref, token_ref, pad_ref = refs[-3:]
    token_ref[...] = jnp.zeros(token_ref.shape, F32)
    chan, cells = acc_ref.shape[1:]
    width = halo_ref.shape[2]
    outer = here_ref[0]
    if first:
        acc_ref[...] = jnp.zeros(acc_ref.shape, F32)
    else:
        acc_ref[...] = refs[size][...]
    for i, (k, g_ref) in enumerate(zip(offsets, grads)):
        halo = halo_ref[i]
        none = jnp.zeros_like(halo)
        pad_ref[i, :, 0:width] = jnp.where(outer == 0, none, halo)
        pad_ref[i, :, width : width + cells] = g_ref[...]
        pad_ref[i, :, width + cells :] = jnp.where(outer == 0, halo, none)
        for b in range(3):
            total = None
            for a in range(3):
                right = pad_ref[i, :, (2 - a) * width : (2 - a) * width + cells]
                left = weight_ref[a, 3 * b * chan : 3 * (b + 1) * chan]
                term = jnp.dot(left, right, preferred_element_type=F32)
                total = term if total is None else total + term
            row = rows_ref[k] + b
            for d in range(cells // width):
                cols = slice(d * width, (d + 1) * width)
                acc_ref[row, :, cols] += (
                    shifted(total[0:chan, cols], -1)
                    + total[chan : 2 * chan, cols]
                    + shifted(total[2 * chan :, cols], 1)
                )


def power(k):
    whole = k.astype(jnp.int32)
    size = jnp.abs(whole)
    out = jnp.ones(k.shape, F32)
    for i in range(7):
        step = jnp.where(whole > 0, 2.0 ** (2**i), 2.0 ** -(2**i))
        out = out * jnp.where((size >> i) & 1 == 1, step, 1.0)
    return out


def packed(out_ref, at, spot, x):
    rows, cols = x.shape
    most = jnp.max(jnp.max(jnp.abs(x), axis=0, keepdims=True), axis=1, keepdims=True)
    most = jnp.broadcast_to(jnp.maximum(most, 2.0**-100), (8, cols))
    k = 13.0 - jnp.floor(jnp.log2(most))
    out_ref[at : at + rows] = x * power(k)[0:1]
    out_ref[spot : spot + 8] = k


def unpacked(ref, at, rows, spot):
    return ref[at : at + rows] * power(-ref[spot : spot + 8])[0:1]


def relay_kernel(plan, here_ref, *refs):
    ins, outs = refs[: plan["ins"]], list(refs[plan["ins"] :])
    rows_in, sums_in, rows_out, packs = (plan[n] for n in ("rows_in", "sums_in", "rows_out", "packs"))
    parts = ins[:2]
    held = ins[plan["ins"] - plan["tokens"] - plan["held"] : plan["ins"] - plan["tokens"]]
    came, sums = [None, None], [None, None]
    at = 2
    if plan["unpack"]:
        for i in range(2):
            ref = ins[at + i]
            spot = ref.shape[0] - 16
            if rows_in:
                came[i] = unpacked(ref, 0, rows_in, spot).astype(BF16)
            sums[i] = unpacked(ref, rows_in, sums_in, spot + 8)
        at += 2
    else:
        if rows_in:
            came = [ins[at][...], ins[at + 1][...]]
            at += 2
        if sums_in:
            sums = [ins[at][...], ins[at + 1][...]]
    full = parts[0].shape[0]
    mid = full // 2
    if sums_in == 0:
        sums = [parts[0][0:mid], parts[0][mid:]]
    elif sums_in == mid:
        zero = jnp.zeros_like(sums[0])
        sums = [
            parts[0][...] + jnp.concatenate([sums[0], zero], axis=0),
            parts[1][...] + jnp.concatenate([zero, sums[1]], axis=0),
        ]
    else:
        sums = [parts[0][...] + sums[0], parts[1][...] + sums[1]]
    for i in range(2):
        passed = None
        if rows_out:
            passed = came[i][0:rows_out] if i == 0 else came[i][rows_in - rows_out :]
        if packs:
            out_ref = outs.pop(0)
            spot = out_ref.shape[0] - 16
            if rows_out:
                packed(out_ref, 0, spot, passed.astype(F32))
            else:
                out_ref[spot : spot + 8] = jnp.zeros((8, out_ref.shape[1]), F32)
            packed(out_ref, rows_out, spot + 8, sums[i])
        else:
            if rows_out:
                outs.pop(0)[...] = passed
            outs.pop(0)[...] = sums[i]
    if plan["keep"]:
        if rows_in == mid:
            came = [jnp.concatenate(came, axis=0)]
        for row in came:
            outs.pop(0)[...] = row
    if plan["edges"]:
        edge_out = outs.pop(0)
        width = edge_out.shape[2]
        outer = here_ref[0]
        for i, row in enumerate([ref[...] for ref in held] + came):
            cells = row.shape[1]
            edge_out[i] = jnp.where(outer == 0, row[:, cells - width :], row[:, 0:width])


def scale_kernel(scale, own_ref, other_ref, out_ref, token_ref, held_ref, sems):
    token_ref[...] = jnp.zeros(token_ref.shape, F32)
    copies = []
    for a in range(own_ref.shape[0]):
        held_ref[a] = (own_ref[a] + other_ref[a]) * scale
        copies.append(pltpu.make_async_copy(held_ref.at[a], out_ref.at[a], sems.at[a]))
        copies[-1].start()
    for copy in copies:
        copy.wait()


def add_kernel(count, *refs):
    out_ref = refs[-1]
    total = refs[0][...]
    for ref in refs[1:count]:
        total = total + ref[...]
    out_ref[...] = total.astype(BF16)


def call(kernel, out_shape, args, smem=1, scratch=(), alias=None):
    whole = pl.BlockSpec(memory_space=pltpu.VMEM)
    specs = [pl.BlockSpec(memory_space=pltpu.SMEM)] * smem + [whole] * (len(args) - smem)
    outs = jax.tree.map(lambda _: whole, out_shape)
    return pl.pallas_call(
        kernel,
        out_shape=out_shape,
        in_specs=specs,
        out_specs=outs,
        scratch_shapes=list(scratch),
        input_output_aliases=alias or {},
        compiler_params=pltpu.CompilerParams(vmem_limit_bytes=VMEM_LIMIT),
        cost_estimate=pl.CostEstimate(flops=0, bytes_accessed=0, transcendentals=0),
    )(*args)


def per_device(features, kernel, grad_out):
    count, chan, slab, width = features.shape
    outs = kernel.shape[1]
    ring_size = lax.axis_size("cin")
    assert count == ring_size and grad_out.shape[0] == 1 and lax.axis_size("depth") == 2
    cells = slab * width
    half = ring_size // 2
    mid = outs // 2
    ring = ring_of(ring_size)
    fwd = [(ring[i], ring[(i + 1) % ring_size]) for i in range(ring_size)]
    bwd = [(j, i) for i, j in fwd]
    swap = [(0, 1), (1, 0)]
    me = lax.axis_index("cin")
    spot = jnp.where(me % 2 == 0, me // 2, ring_size - 1 - me // 2)
    spots = (spot + lax.iota(jnp.int32, ring_size)) % ring_size
    even = 2 * spots < ring_size + ring_size % 2
    rows = jnp.where(even, 2 * spots, 2 * (ring_size - 1 - spots) + 1)
    here = lax.axis_index("depth")
    core = jnp.full((1,), here, jnp.int32)
    token = jax.ShapeDtypeStruct((8, 128), F32)

    def send(pair):
        return lax.ppermute(pair[0], "cin", fwd), lax.ppermute(pair[1], "cin", bwd)

    grads = [None] * ring_size
    own = lax.optimization_barrier(grad_out.reshape(outs, cells))
    grads[0] = own
    going = send((own, own))

    edge = jnp.where(here == 0, features[:, :, slab - 1 :], features[:, :, :1])
    edge = lax.ppermute(edge, "depth", swap)
    none = jnp.zeros_like(edge)
    feat = [jnp.where(here == 0, none, edge), features, jnp.where(here == 0, edge, none)]
    feat = jnp.concatenate(feat, axis=2).transpose(0, 2, 1, 3)
    taps = kernel.transpose(0, 2, 1).reshape(3, 9 * chan, outs)
    w_out = taps.transpose(0, 2, 1)
    ext = call(
        extend_kernel,
        jax.ShapeDtypeStruct((count + 2, 3 * chan, cells + 2 * width), BF16),
        (feat,),
        smem=0,
    )

    def forward(offsets):
        return call(
            functools.partial(forward_kernel, offsets, width),
            [jax.ShapeDtypeStruct((outs, cells), F32)] * len(offsets),
            (rows, ext, w_out),
        )

    def weight_part(group, acc):
        held = [grads[k] for k in group]
        first = acc is None
        return call(
            functools.partial(weight_kernel, group, width, first),
            [jax.ShapeDtypeStruct((3, 9 * chan, outs), F32), token],
            (rows, ext, *held) if first else (rows, ext, *held, acc),
            alias=None if first else {2 + len(group): 0},
        )

    def input_part(group, halo, back):
        held = [grads[k] for k in group]
        first = back is None
        size = len(group)
        return call(
            functools.partial(input_kernel, group, first),
            [jax.ShapeDtypeStruct((count + 2, chan, cells), F32), token],
            (rows, core, taps, halo, *held) if first else (rows, core, taps, halo, *held, back),
            smem=2,
            scratch=[pltpu.VMEM((size, outs, cells + 2 * width), BF16)],
            alias=None if first else {4 + size: 0},
        )

    grads[ring_size - 1], grads[1] = going
    going = send(going)
    part = forward(list(range(ring_size)))
    grads[ring_size - 2], grads[2] = going
    near = [0, ring_size - 1, 1, ring_size - 2, 2]
    far = [k for k in range(ring_size) if k not in near]

    def slim(r):
        return r < half and 8 * r * r <= 9 * ring_size

    acc = back = None
    tokens = []
    going = (going, None, False)
    for r in range(1, half + 1):
        came, came_sums, unpack = going
        rows_in = 0 if r + 1 > half else mid if r + 1 == half else outs
        rows_out = 0 if r + 2 > half else mid if r + 2 == half else outs
        sums_in = 0 if r == 1 else mid if r == 2 else outs
        sums_out = mid if r == 1 else outs
        packs = slim(r)
        keep = bool(rows_in) and r > 1
        if r == 1:
            group = near
        elif r + 1 == half:
            group = far
        else:
            group = []
        new = [half] if rows_in == mid else [ring_size - r - 1, r + 1]
        held = [k for k in group if k not in new]
        left = half + 1 - r
        ins = [part[left], part[ring_size - left]]
        if unpack:
            ins += [x.astype(F32) for x in came]
        else:
            ins += list(came) if rows_in else []
            ins += list(came_sums) if sums_in else []
        ins += [grads[k] for k in held] + tokens
        if packs:
            shapes = [jax.ShapeDtypeStruct((rows_out + sums_out + 16, cells), F32)] * 2
        else:
            shapes = [jax.ShapeDtypeStruct((rows_out, cells), BF16)] if rows_out else []
            shapes = (shapes + [jax.ShapeDtypeStruct((sums_out, cells), F32)]) * 2
        sent = len(shapes)
        if keep:
            shapes = shapes + [jax.ShapeDtypeStruct((outs, cells), BF16)] * len(new)
        if group:
            shapes = shapes + [jax.ShapeDtypeStruct((len(group), outs, width), BF16)]
        plan = dict(
            ins=len(ins),
            held=len(held),
            tokens=len(tokens),
            rows_in=rows_in,
            sums_in=sums_in,
            rows_out=rows_out,
            packs=packs,
            unpack=unpack,
            keep=keep,
            edges=bool(group),
        )
        made = call(functools.partial(relay_kernel, plan), shapes, (core, *ins))
        if keep:
            for k, row in zip(new, made[sent:]):
                grads[k] = row
        if packs:
            going = (send([x.astype(jnp.float16) for x in made[:2]]), None, True)
        elif rows_out:
            going = (send((made[0], made[2])), send((made[1], made[3])), False)
        else:
            going = (None, send((made[0], made[1])), False)
        tokens = []
        if group:
            group = held + new
            halo = lax.ppermute(made[-1], "depth", swap)
            acc, token_w = weight_part(group, acc)
            back, token_i = input_part(group, halo, back)
            tokens = [token_w, token_i]
    f, b = going[1]

    scale = 1.0 / math.sqrt(count * cells * lax.axis_size("depth"))
    acc_shape = acc.shape
    whole = pl.BlockSpec(memory_space=pltpu.VMEM)
    kernel_grad, token_k = pl.pallas_call(
        functools.partial(scale_kernel, scale),
        out_shape=[jax.ShapeDtypeStruct(acc_shape, F32), token],
        in_specs=[whole, whole],
        out_specs=[pl.BlockSpec(memory_space=pl.ANY), whole],
        scratch_shapes=[pltpu.VMEM(acc_shape, F32), pltpu.SemaphoreType.DMA((acc_shape[0],))],
        compiler_params=pltpu.CompilerParams(vmem_limit_bytes=VMEM_LIMIT),
        cost_estimate=pl.CostEstimate(flops=0, bytes_accessed=0, transcendentals=0),
    )(acc, lax.ppermute(acc, "depth", swap))
    kernel_grad = kernel_grad.reshape(27, chan, outs).transpose(0, 2, 1)
    back = back[1 : count + 1]
    parts = lax.axis_size("cout")
    if parts == 2:
        side = lax.axis_index("cout")
        halves = back.reshape(2, count // 2, chan, cells)
        mine = jnp.where(side == 0, halves[0], halves[1])
        sent = jnp.where(side == 0, halves[1], halves[0])
        terms = [mine, lax.ppermute(sent, "cout", swap)]
    else:
        terms = [lax.psum_scatter(back, "cout", scatter_dimension=0, tiled=True)]
    input_grad = call(
        functools.partial(add_kernel, len(terms)),
        jax.ShapeDtypeStruct((count // parts, chan, cells), BF16),
        (*terms, token_k),
        smem=0,
    )
    output = call(
        functools.partial(add_kernel, 3),
        jax.ShapeDtypeStruct((outs, cells), BF16),
        (part[0], f, b, token_k),
        smem=0,
    )
    input_grad = input_grad.reshape(count // parts, chan, slab, width)
    output = output.reshape(1, outs, slab, width)
    return (output, input_grad, kernel_grad)


def solution(mesh):
    return jax.shard_map(
        per_device,
        mesh=mesh,
        in_specs=(
            P(None, "cin", "depth", None),
            P(None, "cout", "cin"),
            P("cin", "cout", "depth", None),
        ),
        out_specs=(
            P("cin", "cout", "depth", None),
            P("cout", "cin", "depth", None),
            P(None, "cout", "cin"),
        ),
        check_vma=False,
    )
```

time: 85.4 us -> 63.7 us (0.75)
  local copies, waits for them, and re-layouts: 25 us -> 8.94 us
  starting transfers between devices: 19.2 us -> 15.8 us
  other arithmetic: 5.49 us -> 3.62 us
  waiting for transfers between devices: 18.8 us -> 17.1 us
  Pallas kernels: 15.4 us -> 17 us
    reshape x5 -> x2, local copies, waits for them, and re-layouts: 6.69 us -> 1.39 us  [the longest x1 0.69 us: per_device(): input_grad = input_grad.reshape(count // parts, chan, slab, width)]
    rev x1 -> x0, local copies, waits for them, and re-layouts: 4.91 us -> none  [per_device(): kernel.reshape(3, 3, 3, outs, chan)[:, ::-1].transpose(0, 2, 4, 1, 3)]
    ppermute x20 -> x17, starting transfers between devices: 19.2 us -> 15.8 us  [the longest x6 11.1 us: send(): lax.ppermute(pair[1], 'cin', bwd)]
    ppermute x1 -> x0, local copies, waits for them, and re-layouts: 2.8 us -> none  [per_device(): other = lax.ppermute(acc, 'depth', [(0, 1), (1, 0)])]
    pallas_call x0 -> x1, Pallas kernels: none -> 2.76 us  [per_device(): pl.pallas_call(functools.partial(scale_kernel, scale), out_shape=[jax.Sha...]
    convert_element_type x2 -> x12, other arithmetic: 1.04 us -> 3.47 us  [the longest x6 2.01 us: per_device(): ins += [x.astype(F32) for x in came]]
    add x3 -> x0, other arithmetic: 2.18 us -> none  [the longest x2 2.15 us: per_device(): f = f + part[s]]
    pallas_call x1 -> x0, local copies, waits for them, and re-layouts: 1.71 us -> none  [call(): pl.pallas_call(kernel, out_shape=out_shape, in_specs=specs, out_specs=out...]
  transfers between devices with their start and end apart: 20 -> 17, of which waited for: 7 -> 10; matrix products, arithmetic and copies ran while one was open for 25% -> 9% of each run, Pallas kernels for 15% -> 18%
where the time goes in v2:
time: 63.7 us; the launch traced here: 63.4 us
  waiting for transfers between devices  17.1 us (27%)
  Pallas kernels  17 us (27%)
  starting transfers between devices  15.8 us (25%)
  local copies, waits for them, and re-layouts  8.94 us (14%)
  other arithmetic  3.62 us (6%)
  between operations  0.95 us (1%)
    pallas_call x12, Pallas kernels, call(): pl.pallas_call(kernel, out_shape=out_shape, in_specs=specs, out_specs=out...  14.2 us
    ppermute x6, waiting for transfers between devices, send(): lax.ppermute(pair[1], 'cin', bwd)  12 us
    ppermute x6, starting transfers between devices, send(): lax.ppermute(pair[1], 'cin', bwd)  11.1 us
    unnamed x32, local copies, waits for them, and re-layouts  6.86 us
    ppermute x6, waiting for transfers between devices, send(): lax.ppermute(pair[0], 'cin', fwd)  4.41 us
    pallas_call x1, Pallas kernels, per_device(): pl.pallas_call(functools.partial(scale_kernel, scale), out_shape=[jax.Sha...  2.76 us
    ppermute x6, starting transfers between devices, send(): lax.ppermute(pair[0], 'cin', fwd)  2.39 us
    convert_element_type x6, other arithmetic, per_device(): ins += [x.astype(F32) for x in came]  2.01 us
  transfers between devices with their start and end apart: 17, of which 10 were waited for; matrix products, arithmetic and copies ran while one was open for 9% of the time, Pallas kernels for 18%

profile of v2, /device:TPU:0, one launch (start us, length us, event | category | flops | bytes accessed | tf_op | source)
XLA Modules:
  0.0 63.4 jit_solution(10496636883672819118)
XLA Ops:
  0.6 1.0 %copy.14 = bf16[32,8,2,128]{3,1,2,0:T(8,128)(2,1)S(1)} copy(bf16[32,8,2,128]{3,2,1,0:T(2,128)(2,1)} %bitcast.24) | data formatting | bytes 262144
  1.6 3.0 %collective-permute-start.3 = (bf16[256,256]{1,0:T(8,128)(2,1)S(1)}, bf16[256,256]{1,0:T(8,128)(2,1)S(1)}, u32[]{:S(2)}, u32[]{:S(2)}) collective-permute-start(bf16[256,256]{1,0:T(8,128)(2,1)S(1)} %bitcast.19), channel_id=1, source_target_pairs={{8,0},{16,8},{24,16},{28,24},{20,28},{12,20},{4,12},{0,4},{9,1},{1... | collective-permute-start | bytes 393224 | tf_op jit(solution)/shard_map/ppermute | solution.py:255
  4.8 1.0 %copy.8 = bf16[8,64,2,128]{3,1,2,0:T(8,128)(2,1)S(1)} copy(bf16[8,64,2,128]{3,2,1,0:T(2,128)(2,1)} %param.3) | data formatting | bytes 524288 | tf_op args[0]
  6.7 1.6 %collective-permute-done.3.refs_6_.refs_2_ = bf16[256,256]{1,0:T(8,128)(2,1)S(1)} collective-permute-done((bf16[256,256]{1,0:T(8,128)(2,1)S(1)}, bf16[256,256]{1,0:T(8,128)(2,1)S(1)}, u32[]{:S(2)}, u32[]{:S(2)}) %collective-permute-start.3) | collective-permute-done | bytes 131104 | tf_op jit(solution)/shard_map/ppermute | solution.py:255
  8.2 1.7 %collective-permute-start.4 = (bf16[256,256]{1,0:T(8,128)(2,1)S(1)}, bf16[256,256]{1,0:T(8,128)(2,1)S(1)}, u32[]{:S(2)}, u32[]{:S(2)}) collective-permute-start(bf16[256,256]{1,0:T(8,128)(2,1)S(1)} %collective-permute-done.3.refs_6_.refs_2_), channel_id=1, source_target_pairs={{8,0},{16,8},{24,16},{28,24},{20,28},{12,20},{4,12},{0,4},{9,1},{1... | collective-permute-start | bytes 393224 | tf_op jit(solution)/shard_map/ppermute | solution.py:255
  11.3 3.2 %shard_map.59 = (f32[256,256]{1,0:T(8,128)S(1)}, f32[256,256]{1,0:T(8,128)S(1)}, f32[256,256]{1,0:T(8,128)S(1)}, f32[256,256]{1,0:T(8,128)S(1)}, f32[256,256]{1,...) custom-call(s32[8]{0:T(128)S(1)} %compare_select_fusion.rows_ref, ...), custom_call_target="tpu_custom_call" | custom-call | tf_op jit(solution)/shard_map/pallas_call | solution.py:221
  16.0 1.7 %collective-permute-start.6 = (f16[400,256]{1,0:T(8,128)(2,1)S(1)}, f16[400,256]{1,0:T(8,128)(2,1)S(1)}, u32[]{:S(2)}, u32[]{:S(2)}) collective-permute-start(f16[400,256]{1,0:T(8,128)(2,1)S(1)} %convert_element_type.38), channel_id=1, source_target_pairs={{8,0},{16,8},{24,16},{28,24},{20,28},{12,20},{4,12},{0,4},{9,1},{1... | collective-permute-start | bytes 614408 | tf_op jit(solution)/shard_map/ppermute | solution.py:255
  18.1 2.6 %shard_map.61 = (f32[3,576,256]{2,1,0:T(8,128)S(1)}, f32[8,128]{1,0:T(8,128)S(1)}) custom-call(s32[8]{0:T(128)S(1)} %compare_select_fusion.rows_ref, bf16[10,192,512]{2,1,0:T(8,128)(2,1)S(1)} %shard_map.58.ext_ref, bf16[256,256]{1,0:T(8,128)(2,1)S(1)} %bitcast.22, bf16[256,256]{1,0:T(8,128)(2,1)S(1)} %collective-permute-done.1.refs_5_.refs_1_, ...), custom_call_target="tpu_custom_call" | custom-call | tf_op jit(solution)/shard_map/pallas_call | solution.py:221
  20.7 2.8 %collective-permute-done.6 = f16[400,256]{1,0:T(8,128)(2,1)S(1)} collective-permute-done((f16[400,256]{1,0:T(8,128)(2,1)S(1)}, f16[400,256]{1,0:T(8,128)(2,1)S(1)}, u32[]{:S(2)}, u32[]{:S(2)}) %collective-permute-start.6) | collective-permute-done | bytes 204832 | tf_op jit(solution)/shard_map/ppermute | solution.py:255
  23.5 1.4 %collective-permute-done.5 = f16[400,256]{1,0:T(8,128)(2,1)S(1)} collective-permute-done((f16[400,256]{1,0:T(8,128)(2,1)S(1)}, f16[400,256]{1,0:T(8,128)(2,1)S(1)}, u32[]{:S(2)}, u32[]{:S(2)}) %collective-permute-start.5) | collective-permute-done | bytes 204832 | tf_op jit(solution)/shard_map/ppermute | solution.py:255
  26.8 2.0 %shard_map.62 = (f32[10,64,256]{2,1,0:T(8,128)S(1)}, f32[8,128]{1,0:T(8,128)S(1)}) custom-call(s32[8]{0:T(128)S(1)} %compare_select_fusion.rows_ref, s32[1]{0:T(128)} %bitcast.4.here_ref, bf16[3,576,256]{2,1,0:T(8,128)(2,1)S(1)} %bitcast.17, bf16[5,256,128]{2,1,0:T(8,128)(2,1)S(1)} %collective-permute-done.7.halo_ref, bf16[256,256]{1,0:T(8,128)(2,1)S(1)} %bitcast.23, ...), custom_call_target="tpu_custom_call" | custom-call | tf_op jit(solution)/shard_map/pallas_call | solution.py:221
  29.2 1.6 %collective-permute-start.9 = (f16[400,256]{1,0:T(8,128)(2,1)S(1)}, f16[400,256]{1,0:T(8,128)(2,1)S(1)}, u32[]{:S(2)}, u32[]{:S(2)}) collective-permute-start(f16[400,256]{1,0:T(8,128)(2,1)S(1)} %convert_element_type.42), channel_id=1, source_target_pairs={{8,0},{16,8},{24,16},{28,24},{20,28},{12,20},{4,12},{0,4},{9,1},{1... | collective-permute-start | bytes 614408 | tf_op jit(solution)/shard_map/ppermute | solution.py:255
  31.3 4.3 %collective-permute-done.9 = f16[400,256]{1,0:T(8,128)(2,1)S(1)} collective-permute-done((f16[400,256]{1,0:T(8,128)(2,1)S(1)}, f16[400,256]{1,0:T(8,128)(2,1)S(1)}, u32[]{:S(2)}, u32[]{:S(2)}) %collective-permute-start.9) | collective-permute-done | bytes 204832 | tf_op jit(solution)/shard_map/ppermute | solution.py:255
  35.7 1.3 %collective-permute-done.8 = f16[400,256]{1,0:T(8,128)(2,1)S(1)} collective-permute-done((f16[400,256]{1,0:T(8,128)(2,1)S(1)}, f16[400,256]{1,0:T(8,128)(2,1)S(1)}, u32[]{:S(2)}, u32[]{:S(2)}) %collective-permute-start.8) | collective-permute-done | bytes 204832 | tf_op jit(solution)/shard_map/ppermute | solution.py:255
  37.9 2.0 %shard_map.65 = (f32[3,576,256]{2,1,0:T(8,128)S(1)}, f32[8,128]{1,0:T(8,128)S(1)}) custom-call(s32[8]{0:T(128)S(1)} %compare_select_fusion.rows_ref, bf16[10,192,512]{2,1,0:T(8,128)(2,1)S(1)} %shard_map.58.ext_ref, bf16[256,256]{1,0:T(8,128)(2,1)S(1)} %get-tuple-element.49.refs_4_.refs_0_, ...), custom_call_target="tpu_custom_call", output_to_operand_aliasing={{0}: (5, {})} | custom-call | tf_op jit(solution)/shard_map/pallas_call | solution.py:221
  41.1 1.6 %collective-permute-start.11 = (f16[272,256]{1,0:T(8,128)(2,1)}, f16[272,256]{1,0:T(8,128)(2,1)}, u32[]{:S(2)}, u32[]{:S(2)}) collective-permute-start(f16[272,256]{1,0:T(8,128)(2,1)} %convert_element_type.46), channel_id=1, source_target_pairs={{8,0},{16,8},{24,16},{28,24},{20,28},{12,20},{4,12},{0,4},{9,1},{1... | collective-permute-start | bytes 417800 | tf_op jit(solution)/shard_map/ppermute | solution.py:255
  43.8 3.3 %collective-permute-done.11 = f16[272,256]{1,0:T(8,128)(2,1)} collective-permute-done((f16[272,256]{1,0:T(8,128)(2,1)}, f16[272,256]{1,0:T(8,128)(2,1)}, u32[]{:S(2)}, u32[]{:S(2)}) %collective-permute-start.11) | collective-permute-done | bytes 139296 | tf_op jit(solution)/shard_map/ppermute | solution.py:255
  47.1 1.0 %convert_element_type.47.refs_3_ = f32[272,256]{1,0:T(8,128)S(1)} convert(f16[272,256]{1,0:T(8,128)(2,1)} %collective-permute-done.11) | non-fusion elementwise | flops 69632 | bytes 417792 | tf_op jit(solution)/shard_map/convert_element_type | solution.py:338
  48.1 1.0 %collective-permute-done.10 = f16[272,256]{1,0:T(8,128)(2,1)} collective-permute-done((f16[272,256]{1,0:T(8,128)(2,1)}, f16[272,256]{1,0:T(8,128)(2,1)}, u32[]{:S(2)}, u32[]{:S(2)}) %collective-permute-start.10) | collective-permute-done | bytes 139296 | tf_op jit(solution)/shard_map/ppermute | solution.py:255
  49.1 0.9 %convert_element_type.45.refs_2_ = f32[272,256]{1,0:T(8,128)S(1)} convert(f16[272,256]{1,0:T(8,128)(2,1)} %collective-permute-done.10) | non-fusion elementwise | flops 69632 | bytes 417792 | tf_op jit(solution)/shard_map/convert_element_type | solution.py:338
  51.8 2.0 %shard_map.66 = (f32[10,64,256]{2,1,0:T(8,128)S(1)}, f32[8,128]{1,0:T(8,128)S(1)}) custom-call(s32[8]{0:T(128)S(1)} %compare_select_fusion.rows_ref, s32[1]{0:T(128)} %bitcast.4.here_ref, bf16[3,576,256]{2,1,0:T(8,128)(2,1)S(1)} %bitcast.18, bf16[3,256,128]{2,1,0:T(8,128)(2,1)} %collective-permute-done.12.halo_ref, ...), custom_call_target="tpu_custom_call", output_to_operand_aliasing={{0}: (7, {})} | custom-call | tf_op jit(solution)/shard_map/pallas_call | solution.py:221
  53.9 1.6 %collective-permute-start.16 = (f32[4,64,256]{2,1,0:T(8,128)S(1)}, f32[4,64,256]{2,1,0:T(8,128)S(1)}, u32[]{:S(2)}, u32[]{:S(2)}) collective-permute-start(f32[4,64,256]{2,1,0:T(8,128)S(1)} %get-tuple-element.65), channel_id=1, source_target_pairs={{0,2},{2,0},{1,3},{3,1},{4,6},{6,4},{5,7},{7,5},{8,10},{10,8},{9,1... | collective-permute-start | bytes 786440 | tf_op jit(solution)/shard_map/ppermute | solution.py:404
  56.1 1.6 %collective-permute-start.14 = (f32[256,256]{1,0:T(8,128)S(1)}, f32[256,256]{1,0:T(8,128)S(1)}, u32[]{:S(2)}, u32[]{:S(2)}) collective-permute-start(f32[256,256]{1,0:T(8,128)S(1)} %get-tuple-element.60), channel_id=1, source_target_pairs={{8,0},{16,8},{24,16},{28,24},{20,28},{12,20},{4,12},{0,4},{9,1},{1... | collective-permute-start | bytes 786440 | tf_op jit(solution)/shard_map/ppermute | solution.py:255
  57.6 2.8 %shard_map.68 = (f32[3,576,256]{2,1,0:T(8,128)}, f32[8,128]{1,0:T(8,128)S(1)}) custom-call(f32[3,576,256]{2,1,0:T(8,128)S(1)} %get-tuple-element.61.own_ref, f32[3,576,256]{2,1,0:T(8,128)} %collective-permute-done.15.other_ref), custom_call_target="tpu_custom_call" | custom-call | tf_op jit(solution)/shard_map/pallas_call | solution.py:387
  (75 shorter events, 15.7 us)
Async XLA Ops:
  0.6 5.3 %copy-start = (bf16[27,256,64]{1,2,0:T(8,128)(2,1)S(1)}, bf16[27,256,64]{1,2,0:T(8,128)(2,1)}, u32[]{:S(2)}) copy-start(bf16[27,256,64]{1,2,0:T(8,128)(2,1)} %param.4) | copy-start | bytes 2654212
  1.6 6.6 %collective-permute-start.3 = (bf16[256,256]{1,0:T(8,128)(2,1)S(1)}, bf16[256,256]{1,0:T(8,128)(2,1)S(1)}, u32[]{:S(2)}, u32[]{:S(2)}) collective-permute-start(bf16[256,256]{1,0:T(8,128)(2,1)S(1)} %bitcast.19), channel_id=1, source_target_pairs={{8,0},{16,8},{24,16},{28,24},{20,28},{12,20},{4,12},{0,4},{9,1},{1... | collective-permute-start | bytes 393224 | tf_op jit(solution)/shard_map/ppermute | solution.py:255
  4.6 5.2 %collective-permute-start.1 = (bf16[256,256]{1,0:T(8,128)(2,1)S(1)}, bf16[256,256]{1,0:T(8,128)(2,1)S(1)}, u32[]{:S(2)}, u32[]{:S(2)}) collective-permute-start(bf16[256,256]{1,0:T(8,128)(2,1)S(1)} %bitcast.20), channel_id=1, source_target_pairs={{0,8},{8,16},{16,24},{24,28},{28,20},{20,12},{12,4},{4,0},{1,9},{9... | collective-permute-start | bytes 393224 | tf_op jit(solution)/shard_map/ppermute | solution.py:255
  5.8 4.4 %collective-permute-start = (bf16[8,64,1,128]{3,1,2,0:T(8,128)(2,1)S(1)}, bf16[8,64,1,128]{3,1,2,0:T(8,128)(2,1)S(1)}, u32[]{:S(2)}, u32[]{:S(2)}) collective-permute-start(bf16[8,64,1,128]{3,1,2,0:T(8,128)(2,1)S(1)} %slice_select_fusion.2), channel_id=1, source_target_pairs={{0,1},{1,0},{2,3},{3,2},{4,5},{5,4},{6,7},{7,6},{8,9},{9,8},{10,11... | collective-permute-start | bytes 393224 | tf_op jit(solution)/shard_map/ppermute | solution.py:263
  8.2 9.9 %copy-start.1 = (bf16[256,256]{1,0:T(8,128)(2,1)}, bf16[256,256]{1,0:T(8,128)(2,1)S(1)}, u32[]{:S(2)}) copy-start(bf16[256,256]{1,0:T(8,128)(2,1)S(1)} %collective-permute-done.3.refs_6_.refs_2_) | copy-start | bytes 393220
  8.2 6.9 %collective-permute-start.4 = (bf16[256,256]{1,0:T(8,128)(2,1)S(1)}, bf16[256,256]{1,0:T(8,128)(2,1)S(1)}, u32[]{:S(2)}, u32[]{:S(2)}) collective-permute-start(bf16[256,256]{1,0:T(8,128)(2,1)S(1)} %collective-permute-done.3.refs_6_.refs_2_), channel_id=1, source_target_pairs={{8,0},{16,8},{24,16},{28,24},{20,28},{12,20},{4,12},{0,4},{9,1},{1... | collective-permute-start | bytes 393224 | tf_op jit(solution)/shard_map/ppermute | solution.py:255
  9.9 8.2 %copy-start.3 = (bf16[256,256]{1,0:T(8,128)(2,1)}, bf16[256,256]{1,0:T(8,128)(2,1)S(1)}, u32[]{:S(2)}) copy-start(bf16[256,256]{1,0:T(8,128)(2,1)S(1)} %collective-permute-done.1.refs_5_.refs_1_) | copy-start | bytes 393220
  9.9 5.3 %collective-permute-start.2 = (bf16[256,256]{1,0:T(8,128)(2,1)S(1)}, bf16[256,256]{1,0:T(8,128)(2,1)S(1)}, u32[]{:S(2)}, u32[]{:S(2)}) collective-permute-start(bf16[256,256]{1,0:T(8,128)(2,1)S(1)} %collective-permute-done.1.refs_5_.refs_1_), channel_id=1, source_target_pairs={{0,8},{8,16},{16,24},{24,28},{28,20},{20,12},{12,4},{4,0},{1,9},{9... | collective-permute-start | bytes 393224 | tf_op jit(solution)/shard_map/ppermute | solution.py:255
  15.9 9.1 %collective-permute-start.7 = (bf16[5,256,128]{2,1,0:T(8,128)(2,1)S(1)}, bf16[5,256,128]{2,1,0:T(8,128)(2,1)S(1)}, u32[]{:S(2)}, u32[]{:S(2)}) collective-permute-start(bf16[5,256,128]{2,1,0:T(8,128)(2,1)S(1)} %get-tuple-element.45), channel_id=1, source_target_pairs={{0,1},{1,0},{2,3},{3,2},{4,5},{5,4},{6,7},{7,6},{8,9},{9,8},{10,11... | collective-permute-start | bytes 983048 | tf_op jit(solution)/shard_map/ppermute | solution.py:378
  16.0 7.5 %collective-permute-start.6 = (f16[400,256]{1,0:T(8,128)(2,1)S(1)}, f16[400,256]{1,0:T(8,128)(2,1)S(1)}, u32[]{:S(2)}, u32[]{:S(2)}) collective-permute-start(f16[400,256]{1,0:T(8,128)(2,1)S(1)} %convert_element_type.38), channel_id=1, source_target_pairs={{8,0},{16,8},{24,16},{28,24},{20,28},{12,20},{4,12},{0,4},{9,1},{1... | collective-permute-start | bytes 614408 | tf_op jit(solution)/shard_map/ppermute | solution.py:255
  17.7 7.3 %collective-permute-start.5 = (f16[400,256]{1,0:T(8,128)(2,1)S(1)}, f16[400,256]{1,0:T(8,128)(2,1)S(1)}, u32[]{:S(2)}, u32[]{:S(2)}) collective-permute-start(f16[400,256]{1,0:T(8,128)(2,1)S(1)} %convert_element_type.36), channel_id=1, source_target_pairs={{0,8},{8,16},{16,24},{24,28},{28,20},{20,12},{12,4},{4,0},{1,9},{9... | collective-permute-start | bytes 614408 | tf_op jit(solution)/shard_map/ppermute | solution.py:255
  29.1 8.8 %copy-start.5 = (bf16[256,256]{1,0:T(8,128)(2,1)}, bf16[256,256]{1,0:T(8,128)(2,1)S(1)}, u32[]{:S(2)}) copy-start(bf16[256,256]{1,0:T(8,128)(2,1)S(1)} %get-tuple-element.49.refs_4_.refs_0_) | copy-start | bytes 393220
  29.2 6.4 %collective-permute-start.9 = (f16[400,256]{1,0:T(8,128)(2,1)S(1)}, f16[400,256]{1,0:T(8,128)(2,1)S(1)}, u32[]{:S(2)}, u32[]{:S(2)}) collective-permute-start(f16[400,256]{1,0:T(8,128)(2,1)S(1)} %convert_element_type.42), channel_id=1, source_target_pairs={{8,0},{16,8},{24,16},{28,24},{20,28},{12,20},{4,12},{0,4},{9,1},{1... | collective-permute-start | bytes 614408 | tf_op jit(solution)/shard_map/ppermute | solution.py:255
  30.8 6.2 %collective-permute-start.8 = (f16[400,256]{1,0:T(8,128)(2,1)S(1)}, f16[400,256]{1,0:T(8,128)(2,1)S(1)}, u32[]{:S(2)}, u32[]{:S(2)}) collective-permute-start(f16[400,256]{1,0:T(8,128)(2,1)S(1)} %convert_element_type.40), channel_id=1, source_target_pairs={{0,8},{8,16},{16,24},{24,28},{28,20},{20,12},{12,4},{4,0},{1,9},{9... | collective-permute-start | bytes 614408 | tf_op jit(solution)/shard_map/ppermute | solution.py:255
  39.9 17.8 %collective-permute-start.15 = (f32[3,576,256]{2,1,0:T(8,128)S(1)}, f32[3,576,256]{2,1,0:T(8,128)}, u32[]{:S(2)}, u32[]{:S(2)}) collective-permute-start(f32[3,576,256]{2,1,0:T(8,128)S(1)} %get-tuple-element.61.own_ref), channel_id=1, source_target_pairs={{0,1},{1,0},{2,3},{3,2},{4,5},{5,4},{6,7},{7,6},{8,9},{9,8},{10,11... | collective-permute-start | bytes 5308424 | tf_op jit(solution)/shard_map/ppermute | solution.py:395
  40.0 10.1 %collective-permute-start.12 = (bf16[3,256,128]{2,1,0:T(8,128)(2,1)}, bf16[3,256,128]{2,1,0:T(8,128)(2,1)}, u32[]{:S(2)}, u32[]{:S(2)}) collective-permute-start(bf16[3,256,128]{2,1,0:T(8,128)(2,1)} %get-tuple-element.56), channel_id=1, source_target_pairs={{0,1},{1,0},{2,3},{3,2},{4,5},{5,4},{6,7},{7,6},{8,9},{9,8},{10,11... | collective-permute-start | bytes 589832 | tf_op jit(solution)/shard_map/ppermute | solution.py:378
  41.1 6.0 %collective-permute-start.11 = (f16[272,256]{1,0:T(8,128)(2,1)}, f16[272,256]{1,0:T(8,128)(2,1)}, u32[]{:S(2)}, u32[]{:S(2)}) collective-permute-start(f16[272,256]{1,0:T(8,128)(2,1)} %convert_element_type.46), channel_id=1, source_target_pairs={{8,0},{16,8},{24,16},{28,24},{20,28},{12,20},{4,12},{0,4},{9,1},{1... | collective-permute-start | bytes 417800 | tf_op jit(solution)/shard_map/ppermute | solution.py:255
  43.4 5.7 %collective-permute-start.10 = (f16[272,256]{1,0:T(8,128)(2,1)}, f16[272,256]{1,0:T(8,128)(2,1)}, u32[]{:S(2)}, u32[]{:S(2)}) collective-permute-start(f16[272,256]{1,0:T(8,128)(2,1)} %convert_element_type.44), channel_id=1, source_target_pairs={{0,8},{8,16},{16,24},{24,28},{28,20},{20,12},{12,4},{4,0},{1,9},{9... | collective-permute-start | bytes 417800 | tf_op jit(solution)/shard_map/ppermute | solution.py:255
  47.1 8.4 %copy-start.14 = (f32[256,256]{1,0:T(8,128)S(1)}, f32[256,256]{1,0:T(8,128)}, u32[]{:S(2)}) copy-start(f32[256,256]{1,0:T(8,128)} %copy-done.13) | copy-start | bytes 786436
  48.1 7.4 %copy-start.12 = (f32[256,256]{1,0:T(8,128)S(1)}, f32[256,256]{1,0:T(8,128)}, u32[]{:S(2)}) copy-start(f32[256,256]{1,0:T(8,128)} %copy-done.11) | copy-start | bytes 786436
  53.9 7.2 %collective-permute-start.16 = (f32[4,64,256]{2,1,0:T(8,128)S(1)}, f32[4,64,256]{2,1,0:T(8,128)S(1)}, u32[]{:S(2)}, u32[]{:S(2)}) collective-permute-start(f32[4,64,256]{2,1,0:T(8,128)S(1)} %get-tuple-element.65), channel_id=1, source_target_pairs={{0,2},{2,0},{1,3},{3,1},{4,6},{6,4},{5,7},{7,5},{8,10},{10,8},{9,1... | collective-permute-start | bytes 786440 | tf_op jit(solution)/shard_map/ppermute | solution.py:404
  55.6 6.9 %collective-permute-start.13 = (f32[256,256]{1,0:T(8,128)S(1)}, f32[256,256]{1,0:T(8,128)S(1)}, u32[]{:S(2)}, u32[]{:S(2)}) collective-permute-start(f32[256,256]{1,0:T(8,128)S(1)} %get-tuple-element.59), channel_id=1, source_target_pairs={{0,8},{8,16},{16,24},{24,28},{28,20},{20,12},{12,4},{4,0},{1,9},{9... | collective-permute-start | bytes 786440 | tf_op jit(solution)/shard_map/ppermute | solution.py:255
  56.1 6.6 %copy-start.10 = (f32[256,256]{1,0:T(8,128)S(1)}, f32[256,256]{1,0:T(8,128)}, u32[]{:S(2)}) copy-start(f32[256,256]{1,0:T(8,128)} %copy-done.9) | copy-start | bytes 786436
  56.1 6.6 %collective-permute-start.14 = (f32[256,256]{1,0:T(8,128)S(1)}, f32[256,256]{1,0:T(8,128)S(1)}, u32[]{:S(2)}, u32[]{:S(2)}) collective-permute-start(f32[256,256]{1,0:T(8,128)S(1)} %get-tuple-element.60), channel_id=1, source_target_pairs={{8,0},{16,8},{24,16},{28,24},{20,28},{12,20},{4,12},{0,4},{9,1},{1... | collective-permute-start | bytes 786440 | tf_op jit(solution)/shard_map/ppermute | solution.py:255
  (8 other events, 7.8 us)

commit v3 on v0

v3 whole, which is shorter than its diff:
```python
import functools
import math

import jax
import jax.numpy as jnp
from jax import lax
from jax.experimental import pallas as pl
from jax.experimental.pallas import tpu as pltpu
from jax.sharding import PartitionSpec as P

F32 = jnp.float32
BF16 = jnp.bfloat16
VMEM_LIMIT = 8 * 1024 * 1024


def ring_of(size):
    return list(range(0, size, 2)) + list(range(size - 1 - size % 2, 0, -2))


def shifted(x, by):
    width = x.shape[1]
    lane = lax.broadcasted_iota(jnp.int32, x.shape, 1)
    edge = 0 if by == 1 else width - 1
    return jnp.where(lane == edge, 0.0, pltpu.roll(x, by % width, 1))


def ring_row(k, size):
    me = lax.axis_index("cin")
    spot = jnp.where(me % 2 == 0, me // 2, size - 1 - me // 2)
    spot = (spot + k) % size
    return jnp.where(2 * spot < size + size % 2, 2 * spot, 2 * (size - 1 - spot) + 1)


def extend_kernel(own, feat_ref, next_ref, ext_ref):
    count, slab, chan, width = feat_ref.shape
    low = lax.axis_index("depth") == (0 if own else 1)
    ext_ref[0] = jnp.zeros(ext_ref.shape[1:], BF16)
    ext_ref[count + 1] = jnp.zeros(ext_ref.shape[1:], BF16)

    @pl.loop(0, count)
    def _(h):
        for d in range(slab + 2):
            if d == 0:
                x = next_ref[h, slab - 1]
                x = jnp.where(low, jnp.zeros_like(x), x)
            elif d == slab + 1:
                x = next_ref[h, 0]
                x = jnp.where(low, x, jnp.zeros_like(x))
            else:
                x = feat_ref[h, d - 1]
            wide = x.astype(F32)
            cols = slice(d * width, (d + 1) * width)
            ext_ref[h + 1, 0:chan, cols] = shifted(wide, 1).astype(BF16)
            ext_ref[h + 1, chan : 2 * chan, cols] = x
            ext_ref[h + 1, 2 * chan : 3 * chan, cols] = shifted(wide, -1).astype(BF16)


def turn_kernel(in_ref, out_ref):
    for a in range(in_ref.shape[0]):
        out_ref[a] = in_ref[a].T


def forward_kernel(offsets, skip, width, ext_ref, weight_ref, *part_refs):
    part_refs = part_refs[skip:]
    chan3 = ext_ref.shape[1]
    cells = ext_ref.shape[2] - 2 * width
    for k, part_ref in zip(offsets, part_refs):
        row = ring_row(k, ext_ref.shape[0] - 2)
        total = None
        for a in range(3):
            right = ext_ref[pl.ds(row, 3), :, a * width : a * width + cells]
            right = right.reshape(3 * chan3, cells)
            term = jnp.dot(weight_ref[a], right, preferred_element_type=F32)
            total = term if total is None else total + term
        part_ref[...] = total


def weight_kernel(groups, width, scale, ext_ref, other_ref, *refs):
    stacks = refs[: 2 * len(groups)]
    out_ref, token_ref, held_ref, sems = refs[-4:]
    token_ref[...] = jnp.zeros(token_ref.shape, F32)
    chan3 = ext_ref.shape[1]
    cells = stacks[0].shape[2]
    terms = []
    for g, group in enumerate(groups):
        for i, k in enumerate(group):
            row = ring_row(k, ext_ref.shape[0] - 2)
            terms.append((row, ext_ref, stacks[g], i))
            terms.append((row, other_ref, stacks[len(groups) + g], i))
    copies = []
    for a in range(3):
        total = None
        for row, source, stack, i in terms:
            left = source[pl.ds(row, 3), :, a * width : a * width + cells]
            term = lax.dot_general(
                left.reshape(3 * chan3, cells),
                stack[i],
                (((1,), (1,)), ((), ())),
                preferred_element_type=F32,
            )
            total = term if total is None else total + term
        held_ref[a] = total * scale
        copies.append(pltpu.make_async_copy(held_ref.at[a], out_ref.at[a], sems.at[a]))
        copies[-1].start()
    for copy in copies:
        copy.wait()


def input_kernel(offsets, first, count, split, weight_ref, theirs_ref, *refs):
    size = len(offsets)
    grads = refs[:size]
    pad_ref = refs[-1]
    if split:
        mine_ref, sent_ref, acc_ref = refs[-4:-1]
    else:
        acc_ref, token_ref = refs[-3:-1]
        token_ref[...] = jnp.zeros(token_ref.shape, F32)
    chan, cells = acc_ref.shape[1:]
    width = (pad_ref.shape[2] - cells) // 2
    low = lax.axis_index("depth") == 0
    if first:
        acc_ref[...] = jnp.zeros(acc_ref.shape, F32)
    else:
        acc_ref[...] = refs[size][...]
    for i, (k, g_ref) in enumerate(zip(offsets, grads)):
        none = jnp.zeros((g_ref.shape[0], width), BF16)
        pad_ref[i, :, 0:width] = jnp.where(low, none, theirs_ref[i, :, cells - width :])
        pad_ref[i, :, width : width + cells] = g_ref[...]
        pad_ref[i, :, width + cells :] = jnp.where(low, theirs_ref[i, :, 0:width], none)
        for b in range(3):
            total = None
            for a in range(3):
                right = pad_ref[i, :, (2 - a) * width : (2 - a) * width + cells]
                left = weight_ref[a, 3 * b * chan : 3 * (b + 1) * chan]
                term = jnp.dot(left, right, preferred_element_type=F32)
                total = term if total is None else total + term
            row = ring_row(k, count) + b
            for d in range(cells // width):
                cols = slice(d * width, (d + 1) * width)
                acc_ref[row, :, cols] += (
                    shifted(total[0:chan, cols], -1)
                    + total[chan : 2 * chan, cols]
                    + shifted(total[2 * chan :, cols], 1)
                )
    if split:
        kept = count // 2
        side = lax.axis_index("cout")
        mine_ref[...] = acc_ref[pl.ds(1 + side * kept, kept)]
        sent_ref[...] = acc_ref[pl.ds(1 + (1 - side) * kept, kept)]


def power(k):
    whole = k.astype(jnp.int32)
    size = jnp.abs(whole)
    out = jnp.ones(k.shape, F32)
    for i in range(7):
        step = jnp.where(whole > 0, 2.0 ** (2**i), 2.0 ** -(2**i))
        out = out * jnp.where((size >> i) & 1 == 1, step, 1.0)
    return out


def packed(out_ref, at, spot, x):
    rows, cols = x.shape
    most = jnp.max(jnp.max(jnp.abs(x), axis=0, keepdims=True), axis=1, keepdims=True)
    most = jnp.broadcast_to(jnp.maximum(most, 2.0**-100), (8, cols))
    k = 13.0 - jnp.floor(jnp.log2(most))
    out_ref[at : at + rows] = x * power(k)[0:1]
    out_ref[spot : spot + 8] = k


def unpacked(ref, at, rows, spot):
    return ref[at : at + rows] * power(-ref[spot : spot + 8])[0:1]


def relay_kernel(plan, part_ref, *refs):
    back, rows_in, sums_in, rows_out = (plan[n] for n in ("back", "rows_in", "sums_in", "rows_out"))
    ins, outs = list(refs[: plan["ins"]]), list(refs[plan["ins"] + plan["skip"] :])
    full = part_ref.shape[0]
    mid = full // 2
    came = total = None
    if plan["raw"]:
        came = ins.pop(0)[...]
    if plan["unpack"]:
        ref = ins.pop(0)
        spot = ref.shape[0] - 16
        held = 0 if plan["raw"] else rows_in
        if held:
            came = unpacked(ref, 0, held, spot).astype(BF16)
        total = unpacked(ref, held, sums_in, spot + 8)
    elif sums_in:
        total = ins.pop(0)[...]
    if sums_in == 0:
        total = part_ref[mid:] if back else part_ref[0:mid]
    elif sums_in == mid:
        pair = [total, jnp.zeros_like(total)]
        total = part_ref[...] + jnp.concatenate(pair[::-1] if back else pair, axis=0)
    else:
        total = part_ref[...] + total
    if rows_out:
        passed = came[rows_in - rows_out :] if back else came[0:rows_out]
        if plan["apart"]:
            outs.pop(0)[...] = passed
            rows_out = 0
    if plan["packs"]:
        out_ref = outs.pop(0)
        spot = out_ref.shape[0] - 16
        if rows_out:
            packed(out_ref, 0, spot, passed.astype(F32))
        else:
            out_ref[spot : spot + 8] = jnp.zeros((8, out_ref.shape[1]), F32)
        packed(out_ref, rows_out, spot + 8, total)
    else:
        outs.pop(0)[...] = total
    if outs:
        outs.pop(0)[...] = came


def stack_kernel(count, *refs):
    out_ref = refs[-1]
    for i in range(count):
        out_ref[i] = refs[i][...]


def join_kernel(first_ref, second_ref, out_ref):
    mid = first_ref.shape[0]
    out_ref[0:mid] = first_ref[...]
    out_ref[mid:] = second_ref[...]


def add_kernel(count, *refs):
    out_ref, token_ref = refs[-2:]
    token_ref[...] = jnp.zeros(token_ref.shape, F32)
    total = refs[0][...]
    for ref in refs[1:count]:
        total = total + ref[...]
    out_ref[...] = total.astype(BF16)


def call(kernel, out_shape, args, scratch=(), alias=None, flops=0):
    whole = pl.BlockSpec(memory_space=pltpu.VMEM)
    outs = jax.tree.map(lambda _: whole, out_shape)
    return pl.pallas_call(
        kernel,
        out_shape=jax.tree.map(lambda x: pltpu.VMEM(x.shape, x.dtype), out_shape),
        in_specs=[whole] * len(args),
        out_specs=outs,
        scratch_shapes=list(scratch),
        input_output_aliases=alias or {},
        compiler_params=pltpu.CompilerParams(vmem_limit_bytes=VMEM_LIMIT),
        cost_estimate=pl.CostEstimate(flops=flops, bytes_accessed=0, transcendentals=0),
    )(*args)


def per_device(features, kernel, grad_out):
    count, chan, slab, width = features.shape
    outs = kernel.shape[1]
    ring_size = lax.axis_size("cin")
    assert count == ring_size and grad_out.shape[0] == 1 and lax.axis_size("depth") == 2
    cells = slab * width
    half = ring_size // 2
    mid = outs // 2
    ring = ring_of(ring_size)
    fwd = [(ring[i], ring[(i + 1) % ring_size]) for i in range(ring_size)]
    bwd = [(j, i) for i, j in fwd]
    swap = [(0, 1), (1, 0)]
    token = jax.ShapeDtypeStruct((8, cells), F32)

    def send(pair):
        return lax.ppermute(pair[0], "cin", fwd), lax.ppermute(pair[1], "cin", bwd)

    grads = [None] * ring_size
    own = lax.optimization_barrier(grad_out.reshape(outs, cells))
    grads[0] = own
    going = send((own, own))

    feat = lax.optimization_barrier(features.transpose(0, 2, 1, 3))
    got = lax.ppermute(feat, "depth", swap)
    taps = kernel.transpose(0, 2, 1).reshape(3, 9 * chan, outs)
    w_out = call(turn_kernel, jax.ShapeDtypeStruct((3, outs, 9 * chan), BF16), (taps,))
    ext_shape = jax.ShapeDtypeStruct((count + 2, 3 * chan, cells + 2 * width), BF16)
    ext = call(functools.partial(extend_kernel, True), ext_shape, (feat, got))
    ext_other = call(functools.partial(extend_kernel, False), ext_shape, (got, feat))

    def forward(offsets, after=()):
        return call(
            functools.partial(forward_kernel, offsets, len(after), width),
            [jax.ShapeDtypeStruct((outs, cells), F32)] * len(offsets),
            (ext, w_out, *after),
        )

    def weight_all(mine, theirs, after):
        shape = (3, 9 * chan, outs)
        scale = 1.0 / math.sqrt(count * cells * lax.axis_size("depth"))
        whole = pl.BlockSpec(memory_space=pltpu.VMEM)
        args = (ext, ext_other, *mine, *theirs, after)
        return pl.pallas_call(
            functools.partial(weight_kernel, (near, far), width, scale),
            out_shape=[jax.ShapeDtypeStruct(shape, F32), token],
            in_specs=[whole] * len(args),
            out_specs=[pl.BlockSpec(memory_space=pl.ANY), whole],
            scratch_shapes=[pltpu.VMEM(shape, F32), pltpu.SemaphoreType.DMA((3,))],
            compiler_params=pltpu.CompilerParams(vmem_limit_bytes=VMEM_LIMIT),
            cost_estimate=pl.CostEstimate(flops=0, bytes_accessed=0, transcendentals=0),
        )(*args)

    parts = lax.axis_size("cout")

    def input_part(group, theirs, back, split):
        held = [grads[k] for k in group]
        first = back is None
        size = len(group)
        args = (taps, theirs, *held)
        whole = jax.ShapeDtypeStruct((count + 2, chan, cells), F32)
        kept = jax.ShapeDtypeStruct((count // 2, chan, cells), F32)
        pad = pltpu.VMEM((size, outs, cells + 2 * width), BF16)
        return call(
            functools.partial(input_kernel, group, first, count, split),
            [kept, kept] if split else [whole, token],
            args if first else (*args, back),
            scratch=[pltpu.VMEM(whole.shape, F32), pad] if split else [pad],
        )

    part = [None] * ring_size
    (part[half],) = forward([half])
    others = [k for k in range(ring_size) if k != half]
    near = [0, ring_size - 1, 1, ring_size - 2, 2]
    far = [k for k in range(ring_size) if k not in near]

    def slim(r):
        return r < half and 8 * r * r <= 9 * ring_size

    row = jax.ShapeDtypeStruct((outs, cells), BF16)
    back = None
    stacks = []
    tokens = []
    going = [[x] for x in going]
    sums = [[], []]
    for r in range(1, half + 1):
        rows_in = mid if r == half else outs
        rows_out = 0 if r == half else mid if r + 1 == half else outs
        sums_in = 0 if r == 1 else mid if r == 2 else outs
        sums_out = mid if r == 1 else outs
        unpack = r > 1 and slim(r - 1)
        packs = slim(r)
        raw = r <= 2 or not unpack
        apart = rows_out if r == 1 or not packs else 0
        group = near if r == 2 else far if r == half else []
        if r == 2:
            for k, p in zip(others, forward(others, [x for pair in sent_on for x in pair])):
                part[k] = p
        left = half + 1 - r
        late = tokens[-1][0:1] if tokens else 0.0
        kept, sent_on = [], []
        for i, perm in ((0, fwd), (1, bwd)):
            ins = going[i] if raw else []
            if unpack:
                ins = ins + [sums[i][0].astype(F32) + late]
            else:
                ins = ins + sums[i]
            shapes = [jax.ShapeDtypeStruct((apart, cells), BF16)] if apart else []
            if packs:
                packed_rows = rows_out - apart + sums_out + 16
                shapes = shapes + [jax.ShapeDtypeStruct((packed_rows, cells), F32)]
            else:
                shapes = shapes + [jax.ShapeDtypeStruct((sums_out, cells), F32)]
            sent = len(shapes)
            if rows_in and not raw:
                shapes = shapes + [jax.ShapeDtypeStruct((rows_in, cells), BF16)]
            plan = dict(
                back=bool(i),
                raw=raw,
                rows_in=rows_in,
                sums_in=sums_in,
                rows_out=rows_out,
                apart=apart,
                packs=packs,
                unpack=unpack,
                ins=len(ins),
                skip=len(tokens),
            )
            term = part[ring_size - left if i else left]
            relay = functools.partial(relay_kernel, plan)
            made = call(relay, shapes, (term, *ins, *tokens))
            kept.append(going[i][0] if raw else made[-1])
            total = made[sent - 1]
            sent_on.append([total])
            if packs:
                total = total.astype(jnp.float16)
            going[i] = [lax.ppermute(x, "cin", perm) for x in made[: sent - 1]]
            sums[i] = [lax.ppermute(total, "cin", perm)]
        if r == half:
            grads[half] = call(join_kernel, row, kept)
        else:
            grads[ring_size - r], grads[r] = kept
        tokens = []
        if group:
            size = len(group)
            stack = jax.ShapeDtypeStruct((size, outs, cells), BF16)
            mine = [grads[k] for k in group]
            mine = call(functools.partial(stack_kernel, size), stack, (*mine, *[x for pair in sent_on for x in pair]))
            theirs = lax.ppermute(mine, "depth", swap)
            back, token_i = input_part(group, theirs, back, r == half and parts == 2)
            stacks.append((mine, theirs))
            if r == half:
                kernel_grad, token_k = weight_all(*zip(*stacks), back)
            else:
                tokens = [token_i]
    (f,), (b,) = sums

    kernel_grad = kernel_grad.reshape(27, chan, outs).transpose(0, 2, 1)
    if parts == 2:
        terms = [back, lax.ppermute(token_i, "cout", swap)]
    else:
        back = back[1 : count + 1]
        terms = [lax.psum_scatter(back, "cout", scatter_dimension=0, tiled=True)]
    input_grad, token_i = call(
        functools.partial(add_kernel, len(terms)),
        [jax.ShapeDtypeStruct((count // parts, chan, cells), BF16), token],
        tuple(terms),
    )
    input_grad = input_grad.reshape(count // parts, chan, slab, width)
    output, _ = call(
        functools.partial(add_kernel, 3),
        [jax.ShapeDtypeStruct((outs, cells), BF16), token],
        (part[0], f, b, token_k),
    )
    output = output.reshape(1, outs, slab, width)
    return (output, input_grad, kernel_grad)


def solution(mesh):
    return jax.shard_map(
        per_device,
        mesh=mesh,
        in_specs=(
            P(None, "cin", "depth", None),
            P(None, "cout", "cin"),
            P("cin", "cout", "depth", None),
        ),
        out_specs=(
            P("cin", "cout", "depth", None),
            P("cout", "cin", "depth", None),
            P(None, "cout", "cin"),
        ),
        check_vma=False,
    )
```

time: 190 us -> 50.3 us (0.26)
  waiting for transfers between devices: 115 us -> 14.2 us
  matrix products: 19.9 us -> 0 us
  local copies, waits for them, and re-layouts: 21.9 us -> 4.47 us
  Pallas kernels: 0 us -> 14.7 us
  between operations: 13.9 us -> 0.94 us
  other arithmetic: 11.9 us -> 0.31 us
  starting transfers between devices: 6.61 us -> 15.4 us
    reduce_scatter x2 -> x0, waiting for transfers between devices: 69.5 us -> none  [the longest x1 69.4 us: per_device(): lax.psum_scatter(conv_rows(block, kernel, lax.axis_size('cin') * rows_own...]
    all_gather x1 -> x0, waiting for transfers between devices: 28 us -> none  [per_device(): grad_full = lax.all_gather(grad_out, 'cin', axis=0, tiled=True)]
    dot_general x9 -> x0, matrix products: 19.9 us -> none  [the longest x3 9.56 us: conv_rows(): jnp.einsum('toc,htcdw->hodw', weight[9 * depth_off:9 * depth_off + 9], st...]
    psum x1 -> x0, waiting for transfers between devices: 17.4 us -> none  [per_device(): summed = lax.psum(local_terms, 'depth')]
    pallas_call x0 -> x21, Pallas kernels: none -> 14.7 us  [the longest x20 9.87 us: call(): pl.pallas_call(kernel, out_shape=jax.tree.map(lambda x: pltpu.VMEM(x.shap...]
    unnamed x25 -> x6, local copies, waits for them, and re-layouts: 17.7 us -> 3.09 us
    ppermute x4 -> x16, waiting for transfers between devices: 0.29 us -> 14.2 us  [the longest x8 13 us: per_device(): sums[i] = [lax.ppermute(total, 'cin', perm)]]
    ppermute x4 -> x16, starting transfers between devices: 6.27 us -> 15.4 us  [the longest x8 8.42 us: per_device(): sums[i] = [lax.ppermute(total, 'cin', perm)]]
  transfers between devices with their start and end apart: 8 -> 16, of which waited for: 4 -> 6; matrix products, arithmetic and copies ran while one was open for 22% -> 4% of each run, Pallas kernels for 0% -> 27%
where the time goes in v3:
time: 50.3 us; the launch traced here: 50.1 us
  starting transfers between devices  15.4 us (31%)
  Pallas kernels  14.7 us (29%)
  waiting for transfers between devices  14.2 us (28%)
  local copies, waits for them, and re-layouts  4.47 us (9%)
  between operations  0.94 us (2%)
    ppermute x8, waiting for transfers between devices, per_device(): sums[i] = [lax.ppermute(total, 'cin', perm)]  13 us
    pallas_call x20, Pallas kernels, call(): pl.pallas_call(kernel, out_shape=jax.tree.map(lambda x: pltpu.VMEM(x.shap...  9.87 us
    ppermute x8, starting transfers between devices, per_device(): sums[i] = [lax.ppermute(total, 'cin', perm)]  8.42 us
    pallas_call x1, Pallas kernels, weight_all(): pl.pallas_call(functools.partial(weight_kernel, (near, far), width, scale...  4.88 us
    unnamed x6, local copies, waits for them, and re-layouts  3.09 us
    ppermute x1, starting transfers between devices, send(): lax.ppermute(pair[0], 'cin', fwd)  2.64 us
    ppermute x2, starting transfers between devices, per_device(): going[i] = [lax.ppermute(x, 'cin', perm) for x in made[:sent - 1]]  2.13 us
    ppermute x1, starting transfers between devices, per_device(): terms = [back, lax.ppermute(token_i, 'cout', swap)]  1.59 us
  transfers between devices with their start and end apart: 16, of which 6 were waited for; matrix products, arithmetic and copies ran while one was open for 4% of the time, Pallas kernels for 27%

profile of v3, /device:TPU:0, one launch (start us, length us, event | category | flops | bytes accessed | tf_op | source)
XLA Modules:
  0.0 50.1 jit_solution(15801060063009169617)
XLA Ops:
  0.6 1.0 %copy.10 = bf16[8,64,2,128]{3,1,2,0:T(8,128)(2,1)S(1)} copy(bf16[8,64,2,128]{3,2,1,0:T(2,128)(2,1)} %param.3) | data formatting | bytes 524288 | tf_op args[0]
  2.1 0.9 %copy.11 = bf16[32,8,2,128]{3,1,2,0:T(8,128)(2,1)S(1)} copy(bf16[32,8,2,128]{3,2,1,0:T(2,128)(2,1)} %bitcast.25) | data formatting | bytes 262144
  3.1 2.6 %collective-permute-start.1 = (bf16[256,256]{1,0:T(8,128)(2,1)S(1)}, bf16[256,256]{1,0:T(8,128)(2,1)S(1)}, u32[]{:S(2)}, u32[]{:S(2)}) collective-permute-start(bf16[256,256]{1,0:T(8,128)(2,1)S(1)} %bitcast.21), channel_id=1, source_target_pairs={{0,8},{8,16},{16,24},{24,28},{28,20},{20,12},{12,4},{4,0},{1,9},{9... | collective-permute-start | bytes 393224 | tf_op jit(solution)/shard_map/ppermute | solution.py:269
  5.7 1.2 %copy-done = bf16[27,256,64]{1,2,0:T(8,128)(2,1)S(1)} copy-done((bf16[27,256,64]{1,2,0:T(8,128)(2,1)S(1)}, bf16[27,256,64]{1,2,0:T(8,128)(2,1)}, u32[]{:S(2)}) %copy-start) | copy-done | bytes 884760
  7.2 0.9 %shard_map.58.ext_ref = bf16[10,192,512]{2,1,0:T(8,128)(2,1)S(1)} custom-call(bf16[8,2,64,128]{3,2,1,0:T(8,128)(2,1)S(1)} %bitcast.19, bf16[8,2,64,128]{3,2,1,0:T(8,128)(2,1)S(1)} %collective-permute-done.next_ref.feat_ref), custom_call_target="tpu_custom_call" | custom-call | tf_op jit(solution)/shard_map/pallas_call | solution.py:242
  8.6 1.2 %collective-permute-done.1.refs_0_.refs_1_ = bf16[256,256]{1,0:T(8,128)(2,1)S(1)} collective-permute-done((bf16[256,256]{1,0:T(8,128)(2,1)S(1)}, bf16[256,256]{1,0:T(8,128)(2,1)S(1)}, u32[]{:S(2)}, u32[]{:S(2)}) %collective-permute-start.1) | collective-permute-done | bytes 131104 | tf_op jit(solution)/shard_map/ppermute | solution.py:269
  9.9 1.9 %collective-permute-start.3 = (bf16[256,256]{1,0:T(8,128)(2,1)S(1)}, bf16[256,256]{1,0:T(8,128)(2,1)S(1)}, u32[]{:S(2)}, u32[]{:S(2)}) collective-permute-start(bf16[256,256]{1,0:T(8,128)(2,1)S(1)} %get-tuple-element.36), channel_id=1, source_target_pairs={{0,8},{8,16},{16,24},{24,28},{28,20},{20,12},{12,4},{4,0},{1,9},{9... | collective-permute-start | bytes 393224 | tf_op jit(solution)/shard_map/ppermute | solution.py:389
  12.2 1.8 %collective-permute-start.7 = (f16[144,256]{1,0:T(8,128)(2,1)S(1)}, f16[144,256]{1,0:T(8,128)(2,1)S(1)}, u32[]{:S(2)}, u32[]{:S(2)}) collective-permute-start(f16[144,256]{1,0:T(8,128)(2,1)S(1)} %convert_element_type.40), channel_id=1, source_target_pairs={{8,0},{16,8},{24,16},{28,24},{20,28},{12,20},{4,12},{0,4},{9,1},{1... | collective-permute-start | bytes 221192 | tf_op jit(solution)/shard_map/ppermute | solution.py:390
  14.3 2.3 %shard_map.63 = (f32[256,256]{1,0:T(8,128)S(1)}, f32[256,256]{1,0:T(8,128)S(1)}, f32[256,256]{1,0:T(8,128)S(1)}, f32[256,256]{1,0:T(8,128)S(1)}, f32[256,256]{1,...) custom-call(bf16[10,192,512]{2,1,0:T(8,128)(2,1)S(1)} %shard_map.58.ext_ref, ...), custom_call_target="tpu_custom_call" | custom-call | tf_op jit(solution)/shard_map/pallas_call | solution.py:242
  16.6 1.8 %collective-permute-done.7 = f16[144,256]{1,0:T(8,128)(2,1)S(1)} collective-permute-done((f16[144,256]{1,0:T(8,128)(2,1)S(1)}, f16[144,256]{1,0:T(8,128)(2,1)S(1)}, u32[]{:S(2)}, u32[]{:S(2)}) %collective-permute-start.7) | collective-permute-done | bytes 73760 | tf_op jit(solution)/shard_map/ppermute | solution.py:390
  19.1 1.6 %collective-permute-start.5 = (f16[528,256]{1,0:T(8,128)(2,1)S(1)}, f16[528,256]{1,0:T(8,128)(2,1)S(1)}, u32[]{:S(2)}, u32[]{:S(2)}) collective-permute-start(f16[528,256]{1,0:T(8,128)(2,1)S(1)} %convert_element_type.38), channel_id=1, source_target_pairs={{0,8},{8,16},{16,24},{24,28},{28,20},{20,12},{12,4},{4,0},{1,9},{9... | collective-permute-start | bytes 811016 | tf_op jit(solution)/shard_map/ppermute | solution.py:390
  21.2 1.5 %shard_map.67 = (f32[10,64,256]{2,1,0:T(8,128)S(1)}, f32[8,256]{1,0:T(8,128)S(1)}) custom-call(bf16[3,576,256]{2,1,0:T(8,128)(2,1)S(1)} %bitcast.16, bf16[5,256,256]{2,1,0:T(8,128)(2,1)S(1)} %collective-permute-done.8.theirs_ref.refs_2_, bf16[256,256]{1,0:T(8,128)(2,1)S(1)} %bitcast.24, bf16[256,256]{1,0:T(8,128)(2,1)S(1)} %collective-permute-done.1.refs_0_.refs_1_, ...), custom_call_target="tpu_custom_call" | custom-call | tf_op jit(solution)/shard_map/pallas_call | solution.py:242
  22.7 5.4 %collective-permute-done.5 = f16[528,256]{1,0:T(8,128)(2,1)S(1)} collective-permute-done((f16[528,256]{1,0:T(8,128)(2,1)S(1)}, f16[528,256]{1,0:T(8,128)(2,1)S(1)}, u32[]{:S(2)}, u32[]{:S(2)}) %collective-permute-start.5) | collective-permute-done | bytes 270368 | tf_op jit(solution)/shard_map/ppermute | solution.py:390
  28.0 1.3 %collective-permute-done.11 = f16[528,256]{1,0:T(8,128)(2,1)S(1)} collective-permute-done((f16[528,256]{1,0:T(8,128)(2,1)S(1)}, f16[528,256]{1,0:T(8,128)(2,1)S(1)}, u32[]{:S(2)}, u32[]{:S(2)}) %collective-permute-start.11) | collective-permute-done | bytes 270368 | tf_op jit(solution)/shard_map/ppermute | solution.py:390
  30.4 1.6 %collective-permute-start.9 = (f16[400,256]{1,0:T(8,128)(2,1)S(1)}, f16[400,256]{1,0:T(8,128)(2,1)S(1)}, u32[]{:S(2)}, u32[]{:S(2)}) collective-permute-start(f16[400,256]{1,0:T(8,128)(2,1)S(1)} %convert_element_type.42), channel_id=1, source_target_pairs={{0,8},{8,16},{16,24},{24,28},{28,20},{20,12},{12,4},{4,0},{1,9},{9... | collective-permute-start | bytes 614408 | tf_op jit(solution)/shard_map/ppermute | solution.py:390
  32.0 4.0 %collective-permute-done.12 = f16[400,256]{1,0:T(8,128)(2,1)S(1)} collective-permute-done((f16[400,256]{1,0:T(8,128)(2,1)S(1)}, f16[400,256]{1,0:T(8,128)(2,1)S(1)}, u32[]{:S(2)}, u32[]{:S(2)}) %collective-permute-start.12) | collective-permute-done | bytes 204832 | tf_op jit(solution)/shard_map/ppermute | solution.py:390
  36.9 1.5 %collective-permute-start.10 = (f32[256,256]{1,0:T(8,128)S(1)}, f32[256,256]{1,0:T(8,128)S(1)}, u32[]{:S(2)}, u32[]{:S(2)}) collective-permute-start(f32[256,256]{1,0:T(8,128)S(1)} %get-tuple-element.41.refs_3_), channel_id=1, source_target_pairs={{0,8},{8,16},{16,24},{24,28},{28,20},{20,12},{12,4},{4,0},{1,9},{9... | collective-permute-start | bytes 786440 | tf_op jit(solution)/shard_map/ppermute | solution.py:390
  39.0 1.0 %shard_map.75 = (f32[4,64,256]{2,1,0:T(8,128)S(1)}, f32[4,64,256]{2,1,0:T(8,128)S(1)}) custom-call(bf16[3,576,256]{2,1,0:T(8,128)(2,1)S(1)} %bitcast.17, bf16[3,256,256]{2,1,0:T(8,128)(2,1)S(1)} %collective-permute-done.14.theirs_ref.refs_3_, bf16[256,256]{1,0:T(8,128)(2,1)S(1)} %get-tuple-element.46.refs_0_, bf16[256,256]{1,0:T(8,128)(2,1)S(1)} %shard_map.73.refs_1_, ...), custom_call_target="tpu_custom_call" | custom-call | tf_op jit(solution)/shard_map/pallas_call | solution.py:242
  40.0 1.6 %collective-permute-start.15 = (f32[4,64,256]{2,1,0:T(8,128)S(1)}, f32[4,64,256]{2,1,0:T(8,128)S(1)}, u32[]{:S(2)}, u32[]{:S(2)}) collective-permute-start(f32[4,64,256]{2,1,0:T(8,128)S(1)} %get-tuple-element.54), channel_id=1, source_target_pairs={{0,2},{2,0},{1,3},{3,1},{4,6},{6,4},{5,7},{7,5},{8,10},{10,8},{9,1... | collective-permute-start | bytes 786440 | tf_op jit(solution)/shard_map/ppermute | solution.py:412
  41.6 0.9 %shard_map.72.other_ref = bf16[10,192,512]{2,1,0:T(8,128)(2,1)S(1)} custom-call(bf16[8,2,64,128]{3,2,1,0:T(8,128)(2,1)S(1)} %collective-permute-done.next_ref.feat_ref, bf16[8,2,64,128]{3,2,1,0:T(8,128)(2,1)S(1)} %bitcast.20), custom_call_target="tpu_custom_call" | custom-call | tf_op jit(solution)/shard_map/pallas_call | solution.py:242
  42.5 4.9 %shard_map.76 = (f32[3,576,256]{2,1,0:T(8,128)}, f32[8,256]{1,0:T(8,128)S(1)}) custom-call(bf16[10,192,512]{2,1,0:T(8,128)(2,1)S(1)} %shard_map.58.ext_ref, bf16[10,192,512]{2,1,0:T(8,128)(2,1)S(1)} %shard_map.72.other_ref, bf16[5,256,256]{2,1,0:T(8,128)(2,1)S(1)} %shard_map.66.refs_0_, bf16[3,256,256]{2,1,0:T(8,128)(2,1)S(1)} %shard_map.74.refs_1_, ...), custom_call_target="tpu_custom_call" | custom-call | tf_op jit(solution)/shard_map/pallas_call | solution.py:296
  47.4 0.7 %shard_map.77 = (bf16[256,256]{1,0:T(8,128)(2,1)S(1)}, f32[8,256]{1,0:T(8,128)}) custom-call(f32[256,256]{1,0:T(8,128)S(1)} %get-tuple-element.32.refs_0_, f32[256,256]{1,0:T(8,128)S(1)} %collective-permute-done.10.refs_1_, f32[256,256]{1,0:T(8,128)S(1)} %collective-permute-done.13.refs_2_, f32[8,256]{1,0:T(8,128)S(1)} %get-tuple-element.52.refs_3_), custom_call_target="tpu_custom_call" | custom-call | tf_op jit(solution)/shard_map/pallas_call | solution.py:242
  48.1 0.7 %reshape.23 = bf16[1,256,2,128]{3,2,1,0:T(2,128)(2,1)} reshape(bf16[256,256]{1,0:T(8,128)(2,1)S(1)} %get-tuple-element.53) | data formatting | bytes 262144 | tf_op jit(solution)/shard_map/reshape | solution.py:427
  49.4 0.7 %reshape.24 = bf16[4,64,2,128]{3,2,1,0:T(2,128)(2,1)} reshape(bf16[4,64,256]{2,1,0:T(8,128)(2,1)S(1)} %get-tuple-element.55) | data formatting | bytes 262144 | tf_op jit(solution)/shard_map/reshape | solution.py:421
  (49 shorter events, 6.3 us)
Async XLA Ops:
  1.6 5.6 %collective-permute-start = (bf16[8,2,64,128]{3,2,1,0:T(8,128)(2,1)S(1)}, bf16[8,2,64,128]{3,2,1,0:T(8,128)(2,1)S(1)}, u32[]{:S(2)}, u32[]{:S(2)}) collective-permute-start(bf16[8,2,64,128]{3,2,1,0:T(8,128)(2,1)S(1)} %bitcast.18), channel_id=1, source_target_pairs={{0,1},{1,0},{2,3},{3,2},{4,5},{5,4},{6,7},{7,6},{8,9},{9,8},{10,11... | collective-permute-start | bytes 786440 | tf_op jit(solution)/shard_map/ppermute | solution.py:277
  3.1 6.7 %collective-permute-start.1 = (bf16[256,256]{1,0:T(8,128)(2,1)S(1)}, bf16[256,256]{1,0:T(8,128)(2,1)S(1)}, u32[]{:S(2)}, u32[]{:S(2)}) collective-permute-start(bf16[256,256]{1,0:T(8,128)(2,1)S(1)} %bitcast.21), channel_id=1, source_target_pairs={{0,8},{8,16},{16,24},{24,28},{28,20},{20,12},{12,4},{4,0},{1,9},{9... | collective-permute-start | bytes 393224 | tf_op jit(solution)/shard_map/ppermute | solution.py:269
  5.7 6.1 %collective-permute-start.2 = (bf16[256,256]{1,0:T(8,128)(2,1)S(1)}, bf16[256,256]{1,0:T(8,128)(2,1)S(1)}, u32[]{:S(2)}, u32[]{:S(2)}) collective-permute-start(bf16[256,256]{1,0:T(8,128)(2,1)S(1)} %bitcast.22), channel_id=1, source_target_pairs={{8,0},{16,8},{24,16},{28,24},{20,28},{12,20},{4,12},{0,4},{9,1},{1... | collective-permute-start | bytes 393224 | tf_op jit(solution)/shard_map/ppermute | solution.py:269
  5.7 1.2 %copy-start = (bf16[27,256,64]{1,2,0:T(8,128)(2,1)S(1)}, bf16[27,256,64]{1,2,0:T(8,128)(2,1)}, u32[]{:S(2)}) copy-start(bf16[27,256,64]{1,2,0:T(8,128)(2,1)} %param.4) | copy-start | bytes 2654212
  9.9 8.5 %collective-permute-start.3 = (bf16[256,256]{1,0:T(8,128)(2,1)S(1)}, bf16[256,256]{1,0:T(8,128)(2,1)S(1)}, u32[]{:S(2)}, u32[]{:S(2)}) collective-permute-start(bf16[256,256]{1,0:T(8,128)(2,1)S(1)} %get-tuple-element.36), channel_id=1, source_target_pairs={{0,8},{8,16},{16,24},{24,28},{28,20},{20,12},{12,4},{4,0},{1,9},{9... | collective-permute-start | bytes 393224 | tf_op jit(solution)/shard_map/ppermute | solution.py:389
  11.9 6.7 %collective-permute-start.6 = (bf16[256,256]{1,0:T(8,128)(2,1)S(1)}, bf16[256,256]{1,0:T(8,128)(2,1)S(1)}, u32[]{:S(2)}, u32[]{:S(2)}) collective-permute-start(bf16[256,256]{1,0:T(8,128)(2,1)S(1)} %get-tuple-element.37), channel_id=1, source_target_pairs={{8,0},{16,8},{24,16},{28,24},{20,28},{12,20},{4,12},{0,4},{9,1},{1... | collective-permute-start | bytes 393224 | tf_op jit(solution)/shard_map/ppermute | solution.py:389
  12.2 6.2 %collective-permute-start.7 = (f16[144,256]{1,0:T(8,128)(2,1)S(1)}, f16[144,256]{1,0:T(8,128)(2,1)S(1)}, u32[]{:S(2)}, u32[]{:S(2)}) collective-permute-start(f16[144,256]{1,0:T(8,128)(2,1)S(1)} %convert_element_type.40), channel_id=1, source_target_pairs={{8,0},{16,8},{24,16},{28,24},{20,28},{12,20},{4,12},{0,4},{9,1},{1... | collective-permute-start | bytes 221192 | tf_op jit(solution)/shard_map/ppermute | solution.py:390
  14.0 4.4 %collective-permute-start.4 = (f16[144,256]{1,0:T(8,128)(2,1)S(1)}, f16[144,256]{1,0:T(8,128)(2,1)S(1)}, u32[]{:S(2)}, u32[]{:S(2)}) collective-permute-start(f16[144,256]{1,0:T(8,128)(2,1)S(1)} %convert_element_type.36), channel_id=1, source_target_pairs={{0,8},{8,16},{16,24},{24,28},{28,20},{20,12},{12,4},{4,0},{1,9},{9... | collective-permute-start | bytes 221192 | tf_op jit(solution)/shard_map/ppermute | solution.py:390
  18.9 2.3 %copy-start.1 = (bf16[27,256,64]{1,2,0:T(8,128)(2,1)S(1)}, bf16[27,256,64]{1,2,0:T(8,128)(2,1)}, u32[]{:S(2)}) copy-start(bf16[27,256,64]{1,2,0:T(8,128)(2,1)} %param.4) | copy-start | bytes 2654212
  18.9 2.3 %collective-permute-start.8 = (bf16[5,256,256]{2,1,0:T(8,128)(2,1)S(1)}, bf16[5,256,256]{2,1,0:T(8,128)(2,1)S(1)}, u32[]{:S(2)}, u32[]{:S(2)}) collective-permute-start(bf16[5,256,256]{2,1,0:T(8,128)(2,1)S(1)} %shard_map.66.refs_0_), channel_id=1, source_target_pairs={{0,1},{1,0},{2,3},{3,2},{4,5},{5,4},{6,7},{7,6},{8,9},{9,8},{10,11... | collective-permute-start | bytes 1966088 | tf_op jit(solution)/shard_map/ppermute | solution.py:401
  19.1 8.9 %collective-permute-start.5 = (f16[528,256]{1,0:T(8,128)(2,1)S(1)}, f16[528,256]{1,0:T(8,128)(2,1)S(1)}, u32[]{:S(2)}, u32[]{:S(2)}) collective-permute-start(f16[528,256]{1,0:T(8,128)(2,1)S(1)} %convert_element_type.38), channel_id=1, source_target_pairs={{0,8},{8,16},{16,24},{24,28},{28,20},{20,12},{12,4},{4,0},{1,9},{9... | collective-permute-start | bytes 811016 | tf_op jit(solution)/shard_map/ppermute | solution.py:390
  20.7 8.6 %collective-permute-start.11 = (f16[528,256]{1,0:T(8,128)(2,1)S(1)}, f16[528,256]{1,0:T(8,128)(2,1)S(1)}, u32[]{:S(2)}, u32[]{:S(2)}) collective-permute-start(f16[528,256]{1,0:T(8,128)(2,1)S(1)} %convert_element_type.44), channel_id=1, source_target_pairs={{8,0},{16,8},{24,16},{28,24},{20,28},{12,20},{4,12},{0,4},{9,1},{1... | collective-permute-start | bytes 811016 | tf_op jit(solution)/shard_map/ppermute | solution.py:390
  29.7 6.4 %collective-permute-start.12 = (f16[400,256]{1,0:T(8,128)(2,1)S(1)}, f16[400,256]{1,0:T(8,128)(2,1)S(1)}, u32[]{:S(2)}, u32[]{:S(2)}) collective-permute-start(f16[400,256]{1,0:T(8,128)(2,1)S(1)} %convert_element_type.46), channel_id=1, source_target_pairs={{8,0},{16,8},{24,16},{28,24},{20,28},{12,20},{4,12},{0,4},{9,1},{1... | collective-permute-start | bytes 614408 | tf_op jit(solution)/shard_map/ppermute | solution.py:390
  30.4 6.3 %collective-permute-start.9 = (f16[400,256]{1,0:T(8,128)(2,1)S(1)}, f16[400,256]{1,0:T(8,128)(2,1)S(1)}, u32[]{:S(2)}, u32[]{:S(2)}) collective-permute-start(f16[400,256]{1,0:T(8,128)(2,1)S(1)} %convert_element_type.42), channel_id=1, source_target_pairs={{0,8},{8,16},{16,24},{24,28},{28,20},{20,12},{12,4},{4,0},{1,9},{9... | collective-permute-start | bytes 614408 | tf_op jit(solution)/shard_map/ppermute | solution.py:390
  36.8 2.2 %collective-permute-start.14 = (bf16[3,256,256]{2,1,0:T(8,128)(2,1)S(1)}, bf16[3,256,256]{2,1,0:T(8,128)(2,1)S(1)}, u32[]{:S(2)}, u32[]{:S(2)}) collective-permute-start(bf16[3,256,256]{2,1,0:T(8,128)(2,1)S(1)} %shard_map.74.refs_1_), channel_id=1, source_target_pairs={{0,1},{1,0},{2,3},{3,2},{4,5},{5,4},{6,7},{7,6},{8,9},{9,8},{10,11... | collective-permute-start | bytes 1179656 | tf_op jit(solution)/shard_map/ppermute | solution.py:401
  36.9 10.5 %collective-permute-start.10 = (f32[256,256]{1,0:T(8,128)S(1)}, f32[256,256]{1,0:T(8,128)S(1)}, u32[]{:S(2)}, u32[]{:S(2)}) collective-permute-start(f32[256,256]{1,0:T(8,128)S(1)} %get-tuple-element.41.refs_3_), channel_id=1, source_target_pairs={{0,8},{8,16},{16,24},{24,28},{28,20},{20,12},{12,4},{4,0},{1,9},{9... | collective-permute-start | bytes 786440 | tf_op jit(solution)/shard_map/ppermute | solution.py:390
  38.4 9.0 %collective-permute-start.13 = (f32[256,256]{1,0:T(8,128)S(1)}, f32[256,256]{1,0:T(8,128)S(1)}, u32[]{:S(2)}, u32[]{:S(2)}) collective-permute-start(f32[256,256]{1,0:T(8,128)S(1)} %get-tuple-element.45.refs_4_), channel_id=1, source_target_pairs={{8,0},{16,8},{24,16},{28,24},{20,28},{12,20},{4,12},{0,4},{9,1},{1... | collective-permute-start | bytes 786440 | tf_op jit(solution)/shard_map/ppermute | solution.py:390
  40.0 8.8 %collective-permute-start.15 = (f32[4,64,256]{2,1,0:T(8,128)S(1)}, f32[4,64,256]{2,1,0:T(8,128)S(1)}, u32[]{:S(2)}, u32[]{:S(2)}) collective-permute-start(f32[4,64,256]{2,1,0:T(8,128)S(1)} %get-tuple-element.54), channel_id=1, source_target_pairs={{0,2},{2,0},{1,3},{3,1},{4,6},{6,4},{5,7},{7,5},{8,10},{10,8},{9,1... | collective-permute-start | bytes 786440 | tf_op jit(solution)/shard_map/ppermute | solution.py:412

commit v4 on v3

--- a/solution.py
+++ b/solution.py
@@ -31,28 +31,44 @@
     return jnp.where(2 * spot < size + size % 2, 2 * spot, 2 * (size - 1 - spot) + 1)
 
 
-def extend_kernel(own, feat_ref, next_ref, ext_ref):
+def split_kernel(feat_ref, *outs):
+    low = lax.axis_index("depth") == 0
+    half = outs[0].shape[0]
+    first, second = feat_ref[:, 0], feat_ref[:, 1]
+    edge = jnp.where(low, second, first)
+    outs[0][...] = edge[0:half]
+    outs[1][...] = edge[half:]
+    outs[2][...] = jnp.where(low, first, second)
+
+
+def extend_kernel(own, feat_ref, edge_ref, second_edge_ref, *refs):
+    ext_ref = refs[-1]
     count, slab, chan, width = feat_ref.shape
-    low = lax.axis_index("depth") == (0 if own else 1)
+    half = edge_ref.shape[0]
+    low = lax.axis_index("depth") == 0
     ext_ref[0] = jnp.zeros(ext_ref.shape[1:], BF16)
     ext_ref[count + 1] = jnp.zeros(ext_ref.shape[1:], BF16)
-
-    @pl.loop(0, count)
-    def _(h):
-        for d in range(slab + 2):
-            if d == 0:
-                x = next_ref[h, slab - 1]
-                x = jnp.where(low, jnp.zeros_like(x), x)
-            elif d == slab + 1:
-                x = next_ref[h, 0]
-                x = jnp.where(low, x, jnp.zeros_like(x))
+    for part, near_ref in enumerate((edge_ref, second_edge_ref)):
+
+        @pl.loop(0, half)
+        def _(i):
+            h = part * half + i
+            edge = near_ref[i]
+            none = jnp.zeros_like(edge)
+            first, second = feat_ref[h, 0], feat_ref[h, 1]
+            if own:
+                layers = [jnp.where(low, none, edge), first, second, jnp.where(low, edge, none)]
             else:
-                x = feat_ref[h, d - 1]
-            wide = x.astype(F32)
-            cols = slice(d * width, (d + 1) * width)
-            ext_ref[h + 1, 0:chan, cols] = shifted(wide, 1).astype(BF16)
-            ext_ref[h + 1, chan : 2 * chan, cols] = x
-            ext_ref[h + 1, 2 * chan : 3 * chan, cols] = shifted(wide, -1).astype(BF16)
+                rest = refs[0][h]
+                layers = [jnp.where(low, second, none)]
+                layers += [jnp.where(low, edge, rest), jnp.where(low, rest, edge)]
+                layers += [jnp.where(low, none, first)]
+            for d, x in enumerate(layers):
+                wide = x.astype(F32)
+                cols = slice(d * width, (d + 1) * width)
+                ext_ref[h + 1, 0:chan, cols] = shifted(wide, 1).astype(BF16)
+                ext_ref[h + 1, chan : 2 * chan, cols] = x
+                ext_ref[h + 1, 2 * chan : 3 * chan, cols] = shifted(wide, -1).astype(BF16)
 
 
 def turn_kernel(in_ref, out_ref):
@@ -66,39 +82,50 @@
     cells = ext_ref.shape[2] - 2 * width
     for k, part_ref in zip(offsets, part_refs):
         row = ring_row(k, ext_ref.shape[0] - 2)
-        total = None
-        for a in range(3):
-            right = ext_ref[pl.ds(row, 3), :, a * width : a * width + cells]
-            right = right.reshape(3 * chan3, cells)
-            term = jnp.dot(weight_ref[a], right, preferred_element_type=F32)
-            total = term if total is None else total + term
+        right = [
+            ext_ref[pl.ds(row, 3), :, a * width : a * width + cells].reshape(3 * chan3, cells)
+            for a in range(3)
+        ]
+        total = jnp.dot(
+            jnp.concatenate([weight_ref[a] for a in range(3)], axis=1),
+            jnp.concatenate(right, axis=0),
+            preferred_element_type=F32,
+        )
         part_ref[...] = total
 
 
-def weight_kernel(groups, width, scale, ext_ref, other_ref, *refs):
-    stacks = refs[: 2 * len(groups)]
-    out_ref, token_ref, held_ref, sems = refs[-4:]
+def weight_kernel(group, width, scale, first, last, ext_ref, other_ref, mine_ref, theirs_ref, *refs):
+    before = refs[:3]
+    if not last:
+        *outs, token_ref, second_token_ref = refs[-5:]
+    else:
+        out_ref, token_ref, second_token_ref, held_ref, sems = refs[-5:]
+    second_token_ref[...] = jnp.zeros(second_token_ref.shape, F32)
     token_ref[...] = jnp.zeros(token_ref.shape, F32)
     chan3 = ext_ref.shape[1]
-    cells = stacks[0].shape[2]
+    cells = mine_ref.shape[2]
     terms = []
-    for g, group in enumerate(groups):
-        for i, k in enumerate(group):
-            row = ring_row(k, ext_ref.shape[0] - 2)
-            terms.append((row, ext_ref, stacks[g], i))
-            terms.append((row, other_ref, stacks[len(groups) + g], i))
+    for i, k in enumerate(group):
+        row = ring_row(k, ext_ref.shape[0] - 2)
+        terms.append((row, ext_ref, mine_ref, i))
+        terms.append((row, other_ref, theirs_ref, i))
     copies = []
     for a in range(3):
-        total = None
-        for row, source, stack, i in terms:
-            left = source[pl.ds(row, 3), :, a * width : a * width + cells]
-            term = lax.dot_general(
-                left.reshape(3 * chan3, cells),
-                stack[i],
-                (((1,), (1,)), ((), ())),
-                preferred_element_type=F32,
-            )
-            total = term if total is None else total + term
+        left = [
+            source[pl.ds(row, 3), :, a * width : a * width + cells].reshape(3 * chan3, cells)
+            for row, source, stack, i in terms
+        ]
+        total = lax.dot_general(
+            jnp.concatenate(left, axis=1),
+            jnp.concatenate([stack[i] for row, source, stack, i in terms], axis=1),
+            (((1,), (1,)), ((), ())),
+            preferred_element_type=F32,
+        )
+        if not first:
+            total = before[a][...] + total
+        if not last:
+            outs[a][...] = total
+            continue
         held_ref[a] = total * scale
         copies.append(pltpu.make_async_copy(held_ref.at[a], out_ref.at[a], sems.at[a]))
         copies[-1].start()
@@ -145,8 +172,10 @@
     if split:
         kept = count // 2
         side = lax.axis_index("cout")
-        mine_ref[...] = acc_ref[pl.ds(1 + side * kept, kept)]
-        sent_ref[...] = acc_ref[pl.ds(1 + (1 - side) * kept, kept)]
+        mine_ref[...] = acc_ref[pl.ds(1 + side * kept, kept)].reshape(kept * chan, cells)
+        sent = acc_ref[pl.ds(1 + (1 - side) * kept, kept)].reshape(kept * chan, cells)
+        sent_ref[kept * chan : kept * chan + 8] = jnp.zeros((8, cells), F32)
+        coded(sent_ref, 0, kept * chan + 8, sent)
 
 
 def power(k):
@@ -170,6 +199,31 @@
 
 def unpacked(ref, at, rows, spot):
     return ref[at : at + rows] * power(-ref[spot : spot + 8])[0:1]
+
+
+EDGE = 2.0**-3.5
+
+
+def coded(out_ref, at, spot, x):
+    rows, cols = x.shape
+    size = jnp.abs(x)
+    most = jnp.max(jnp.max(size, axis=0, keepdims=True), axis=1, keepdims=True)
+    most = jnp.broadcast_to(jnp.maximum(most, 2.0**-100), (8, cols))
+    k = 2.0 - jnp.floor(jnp.log2(most))
+    root = size * (power(k)[0:1] * 1.96) + EDGE
+    square = root * root
+    square = square * square
+    out_ref[at : at + rows] = jnp.where(x < 0.0, -square, square)
+    out_ref[spot : spot + 8] = k
+
+
+def decoded(ref, at, rows, spot):
+    value = ref[at : at + rows]
+    size = jnp.abs(value)
+    root = size * lax.rsqrt(size)
+    root = root * lax.rsqrt(root) - EDGE
+    root = root * (power(-ref[spot : spot + 8])[0:1] * (1.0 / 1.96))
+    return jnp.where(value < 0.0, -root, root)
 
 
 def relay_kernel(plan, part_ref, *refs):
@@ -186,7 +240,7 @@
         held = 0 if plan["raw"] else rows_in
         if held:
             came = unpacked(ref, 0, held, spot).astype(BF16)
-        total = unpacked(ref, held, sums_in, spot + 8)
+        total = decoded(ref, held, sums_in, spot + 8)
     elif sums_in:
         total = ins.pop(0)[...]
     if sums_in == 0:
@@ -208,7 +262,7 @@
             packed(out_ref, 0, spot, passed.astype(F32))
         else:
             out_ref[spot : spot + 8] = jnp.zeros((8, out_ref.shape[1]), F32)
-        packed(out_ref, rows_out, spot + 8, total)
+        coded(out_ref, rows_out, spot + 8, total)
     else:
         outs.pop(0)[...] = total
     if outs:
@@ -227,12 +281,12 @@
     out_ref[mid:] = second_ref[...]
 
 
-def add_kernel(count, *refs):
+def add_kernel(first_ref, *refs, skip=0):
     out_ref, token_ref = refs[-2:]
     token_ref[...] = jnp.zeros(token_ref.shape, F32)
-    total = refs[0][...]
-    for ref in refs[1:count]:
-        total = total + ref[...]
+    total = first_ref[...]
+    for ref in refs[: len(refs) - 2 - skip]:
+        total = total + decoded(ref, 0, total.shape[0], total.shape[0] + 8)
     out_ref[...] = total.astype(BF16)
 
 
@@ -255,7 +309,7 @@
     count, chan, slab, width = features.shape
     outs = kernel.shape[1]
     ring_size = lax.axis_size("cin")
-    assert count == ring_size and grad_out.shape[0] == 1 and lax.axis_size("depth") == 2
+    assert count == ring_size and slab == 2 and grad_out.shape[0] == 1 and lax.axis_size("depth") == 2
     cells = slab * width
     half = ring_size // 2
     mid = outs // 2
@@ -273,13 +327,14 @@
     grads[0] = own
     going = send((own, own))
 
-    feat = lax.optimization_barrier(features.transpose(0, 2, 1, 3))
-    got = lax.ppermute(feat, "depth", swap)
+    feat = features.transpose(0, 2, 1, 3)
+    layer = [jax.ShapeDtypeStruct((n, chan, width), BF16) for n in (count // 2, count // 2, count)]
+    got = [lax.ppermute(x, "depth", swap) for x in call(split_kernel, layer, (feat,))]
     taps = kernel.transpose(0, 2, 1).reshape(3, 9 * chan, outs)
     w_out = call(turn_kernel, jax.ShapeDtypeStruct((3, outs, 9 * chan), BF16), (taps,))
     ext_shape = jax.ShapeDtypeStruct((count + 2, 3 * chan, cells + 2 * width), BF16)
-    ext = call(functools.partial(extend_kernel, True), ext_shape, (feat, got))
-    ext_other = call(functools.partial(extend_kernel, False), ext_shape, (got, feat))
+    ext = call(functools.partial(extend_kernel, True), ext_shape, (feat, *got[:2]))
+    ext_other = call(functools.partial(extend_kernel, False), ext_shape, (feat, *got))
 
     def forward(offsets, after=()):
         return call(
@@ -288,16 +343,24 @@
             (ext, w_out, *after),
         )
 
-    def weight_all(mine, theirs, after):
+    def weight_part(group, mine, theirs, acc, after):
+        *acc, token_f, token_b = call(
+            functools.partial(weight_kernel, group, width, 1.0, not acc, False),
+            [jax.ShapeDtypeStruct((9 * chan, outs), F32)] * 3 + [token, token],
+            (ext, ext_other, mine, theirs, *acc, after),
+        )
+        return acc, (token_f, token_b)
+
+    def weight_last(group, mine, theirs, acc, after):
         shape = (3, 9 * chan, outs)
         scale = 1.0 / math.sqrt(count * cells * lax.axis_size("depth"))
         whole = pl.BlockSpec(memory_space=pltpu.VMEM)
-        args = (ext, ext_other, *mine, *theirs, after)
+        args = (ext, ext_other, mine, theirs, *acc, after)
         return pl.pallas_call(
-            functools.partial(weight_kernel, (near, far), width, scale),
-            out_shape=[jax.ShapeDtypeStruct(shape, F32), token],
+            functools.partial(weight_kernel, group, width, scale, False, True),
+            out_shape=[jax.ShapeDtypeStruct(shape, F32), token, token],
             in_specs=[whole] * len(args),
-            out_specs=[pl.BlockSpec(memory_space=pl.ANY), whole],
+            out_specs=[pl.BlockSpec(memory_space=pl.ANY), whole, whole],
             scratch_shapes=[pltpu.VMEM(shape, F32), pltpu.SemaphoreType.DMA((3,))],
             compiler_params=pltpu.CompilerParams(vmem_limit_bytes=VMEM_LIMIT),
             cost_estimate=pl.CostEstimate(flops=0, bytes_accessed=0, transcendentals=0),
@@ -311,11 +374,12 @@
         size = len(group)
         args = (taps, theirs, *held)
         whole = jax.ShapeDtypeStruct((count + 2, chan, cells), F32)
-        kept = jax.ShapeDtypeStruct((count // 2, chan, cells), F32)
+        kept = jax.ShapeDtypeStruct((count // 2 * chan, cells), F32)
+        sent = jax.ShapeDtypeStruct((count // 2 * chan + 16, cells), F32)
         pad = pltpu.VMEM((size, outs, cells + 2 * width), BF16)
         return call(
             functools.partial(input_kernel, group, first, count, split),
-            [kept, kept] if split else [whole, token],
+            [kept, sent] if split else [whole, token],
             args if first else (*args, back),
             scratch=[pltpu.VMEM(whole.shape, F32), pad] if split else [pad],
         )
@@ -326,12 +390,9 @@
     near = [0, ring_size - 1, 1, ring_size - 2, 2]
     far = [k for k in range(ring_size) if k not in near]
 
-    def slim(r):
-        return r < half and 8 * r * r <= 9 * ring_size
-
     row = jax.ShapeDtypeStruct((outs, cells), BF16)
     back = None
-    stacks = []
+    acc = []
     tokens = []
     going = [[x] for x in going]
     sums = [[], []]
@@ -340,8 +401,8 @@
         rows_out = 0 if r == half else mid if r + 1 == half else outs
         sums_in = 0 if r == 1 else mid if r == 2 else outs
         sums_out = mid if r == 1 else outs
-        unpack = r > 1 and slim(r - 1)
-        packs = slim(r)
+        unpack = r > 1
+        packs = True
         raw = r <= 2 or not unpack
         apart = rows_out if r == 1 or not packs else 0
         group = near if r == 2 else far if r == half else []
@@ -349,11 +410,11 @@
             for k, p in zip(others, forward(others, [x for pair in sent_on for x in pair])):
                 part[k] = p
         left = half + 1 - r
-        late = tokens[-1][0:1] if tokens else 0.0
         kept, sent_on = [], []
         for i, perm in ((0, fwd), (1, bwd)):
             ins = going[i] if raw else []
             if unpack:
+                late = tokens[i][0:1] if tokens else 0.0
                 ins = ins + [sums[i][0].astype(F32) + late]
             else:
                 ins = ins + sums[i]
@@ -376,11 +437,11 @@
                 packs=packs,
                 unpack=unpack,
                 ins=len(ins),
-                skip=len(tokens),
+                skip=0,
             )
             term = part[ring_size - left if i else left]
             relay = functools.partial(relay_kernel, plan)
-            made = call(relay, shapes, (term, *ins, *tokens))
+            made = call(relay, shapes, (term, *ins))
             kept.append(going[i][0] if raw else made[-1])
             total = made[sent - 1]
             sent_on.append([total])
@@ -400,29 +461,30 @@
             mine = call(functools.partial(stack_kernel, size), stack, (*mine, *[x for pair in sent_on for x in pair]))
             theirs = lax.ppermute(mine, "depth", swap)
             back, token_i = input_part(group, theirs, back, r == half and parts == 2)
-            stacks.append((mine, theirs))
             if r == half:
-                kernel_grad, token_k = weight_all(*zip(*stacks), back)
+                kernel_grad, *tokens = weight_last(group, mine, theirs, acc, back)
             else:
-                tokens = [token_i]
+                acc, tokens = weight_part(group, mine, theirs, acc, token_i)
     (f,), (b,) = sums
 
     kernel_grad = kernel_grad.reshape(27, chan, outs).transpose(0, 2, 1)
     if parts == 2:
-        terms = [back, lax.ppermute(token_i, "cout", swap)]
+        other = lax.ppermute(token_i.astype(jnp.float16), "cout", swap).astype(F32)
+        terms = [back, other]
     else:
         back = back[1 : count + 1]
         terms = [lax.psum_scatter(back, "cout", scatter_dimension=0, tiled=True)]
-    input_grad, token_i = call(
-        functools.partial(add_kernel, len(terms)),
-        [jax.ShapeDtypeStruct((count // parts, chan, cells), BF16), token],
+        terms = [terms[0].reshape(count // parts * chan, cells)]
+    input_grad, token_y = call(
+        add_kernel,
+        [jax.ShapeDtypeStruct((count // parts * chan, cells), BF16), token],
         tuple(terms),
     )
     input_grad = input_grad.reshape(count // parts, chan, slab, width)
     output, _ = call(
-        functools.partial(add_kernel, 3),
+        functools.partial(add_kernel, skip=1),
         [jax.ShapeDtypeStruct((outs, cells), BF16), token],
-        (part[0], f, b, token_k),
+        (part[0], f.astype(F32), b.astype(F32), token_y),
     )
     output = output.reshape(1, outs, slab, width)
     return (output, input_grad, kernel_grad)

time: 50.3 us -> 50.8 us (level)
  waiting for transfers between devices: 14.2 us -> 12.1 us
  Pallas kernels: 14.7 us -> 16.1 us
  starting transfers between devices: 15.4 us -> 16.4 us
    pallas_call x20 -> x22, Pallas kernels: 9.87 us -> 12.9 us  [call(): pl.pallas_call(kernel, out_shape=jax.tree.map(lambda x: pltpu.VMEM(x.shap...]
    pallas_call x1, Pallas kernels: 4.88 us -> 3.22 us  [weight_last(): pl.pallas_call(functools.partial(weight_kernel, group, width, scale, Fals...]
    ppermute x1, waiting for transfers between devices: 1.19 us -> 0.01 us  [send(): lax.ppermute(pair[0], 'cin', fwd)]
    ppermute x8, waiting for transfers between devices: 13 us -> 11.9 us  [per_device(): sums[i] = [lax.ppermute(total, 'cin', perm)]]
    ppermute x2 -> x4, starting transfers between devices: 2.11 us -> 2.36 us  [the longest x1 1.58 us: per_device(): other = lax.ppermute(token_i.astype(jnp.float16), 'cout', swap).astype(F32)]
  transfers between devices with their start and end apart: 16 -> 18, of which waited for: 6 -> 7; matrix products, arithmetic and copies ran while one was open for 4% -> 3% of each run, Pallas kernels for 27% -> 29%
where the time goes in v4:
time: 50.8 us; the launch traced here: 50.5 us
  starting transfers between devices  16.4 us (32%)
  Pallas kernels  16.1 us (32%)
  waiting for transfers between devices  12.1 us (24%)
  local copies, waits for them, and re-layouts  4.48 us (9%)
  between operations  1.04 us (2%)
    pallas_call x22, Pallas kernels, call(): pl.pallas_call(kernel, out_shape=jax.tree.map(lambda x: pltpu.VMEM(x.shap...  12.9 us
    ppermute x8, waiting for transfers between devices, per_device(): sums[i] = [lax.ppermute(total, 'cin', perm)]  11.9 us
    ppermute x8, starting transfers between devices, per_device(): sums[i] = [lax.ppermute(total, 'cin', perm)]  8.7 us
    pallas_call x1, Pallas kernels, weight_last(): pl.pallas_call(functools.partial(weight_kernel, group, width, scale, Fals...  3.22 us
    unnamed x6, local copies, waits for them, and re-layouts  3.09 us
    ppermute x1, starting transfers between devices, send(): lax.ppermute(pair[0], 'cin', fwd)  3.08 us
    ppermute x2, starting transfers between devices, per_device(): going[i] = [lax.ppermute(x, 'cin', perm) for x in made[:sent - 1]]  2.13 us
    ppermute x1, starting transfers between devices, per_device(): other = lax.ppermute(token_i.astype(jnp.float16), 'cout', swap).astype(F32)  1.58 us
  transfers between devices with their start and end apart: 18, of which 7 were waited for; matrix products, arithmetic and copies ran while one was open for 3% of the time, Pallas kernels for 29%

profile of v4, /device:TPU:0, one launch (start us, length us, event | category | flops | bytes accessed | tf_op | source)
XLA Modules:
  0.0 50.5 jit_solution(14726717948975737766)
XLA Ops:
  0.6 0.9 %copy.11 = bf16[32,8,2,128]{3,1,2,0:T(8,128)(2,1)S(1)} copy(bf16[32,8,2,128]{3,2,1,0:T(2,128)(2,1)} %bitcast.26) | data formatting | bytes 262144
  1.6 3.1 %collective-permute-start.2 = (bf16[256,256]{1,0:T(8,128)(2,1)S(1)}, bf16[256,256]{1,0:T(8,128)(2,1)S(1)}, u32[]{:S(2)}, u32[]{:S(2)}) collective-permute-start(bf16[256,256]{1,0:T(8,128)(2,1)S(1)} %bitcast.22), channel_id=1, source_target_pairs={{0,8},{8,16},{16,24},{24,28},{28,20},{20,12},{12,4},{4,0},{1,9},{9... | collective-permute-start | bytes 393224 | tf_op jit(solution)/shard_map/ppermute | solution.py:323
  4.6 1.0 %copy.10 = bf16[8,64,2,128]{3,1,2,0:T(8,128)(2,1)S(1)} copy(bf16[8,64,2,128]{3,2,1,0:T(2,128)(2,1)} %param.3) | data formatting | bytes 524288 | tf_op args[0]
  6.3 1.2 %copy-done = bf16[27,256,64]{1,2,0:T(8,128)(2,1)S(1)} copy-done((bf16[27,256,64]{1,2,0:T(8,128)(2,1)S(1)}, bf16[27,256,64]{1,2,0:T(8,128)(2,1)}, u32[]{:S(2)}) %copy-start) | copy-done | bytes 884760
  7.8 0.9 %shard_map.59.ext_ref = bf16[10,192,512]{2,1,0:T(8,128)(2,1)S(1)} custom-call(bf16[8,2,64,128]{3,2,1,0:T(8,128)(2,1)S(1)} %bitcast.20, bf16[4,64,128]{2,1,0:T(8,128)(2,1)S(1)} %collective-permute-done.edge_ref, bf16[4,64,128]{2,1,0:T(8,128)(2,1)S(1)} %collective-permute-done.1.second_edge_ref), custom_call_target="tpu_custom_call" | custom-call | tf_op jit(solution)/shard_map/pallas_call | solution.py:296
  9.3 2.1 %collective-permute-start.4 = (bf16[256,256]{1,0:T(8,128)(2,1)S(1)}, bf16[256,256]{1,0:T(8,128)(2,1)S(1)}, u32[]{:S(2)}, u32[]{:S(2)}) collective-permute-start(bf16[256,256]{1,0:T(8,128)(2,1)S(1)} %get-tuple-element.46), channel_id=1, source_target_pairs={{0,8},{8,16},{16,24},{24,28},{28,20},{20,12},{12,4},{4,0},{1,9},{9... | collective-permute-start | bytes 393224 | tf_op jit(solution)/shard_map/ppermute | solution.py:450
  11.6 2.0 %collective-permute-start.9 = (f16[144,256]{1,0:T(8,128)(2,1)S(1)}, f16[144,256]{1,0:T(8,128)(2,1)S(1)}, u32[]{:S(2)}, u32[]{:S(2)}) collective-permute-start(f16[144,256]{1,0:T(8,128)(2,1)S(1)} %convert_element_type.58), channel_id=1, source_target_pairs={{8,0},{16,8},{24,16},{28,24},{20,28},{12,20},{4,12},{0,4},{9,1},{1... | collective-permute-start | bytes 221192 | tf_op jit(solution)/shard_map/ppermute | solution.py:451
  13.8 1.9 %shard_map.64 = (f32[256,256]{1,0:T(8,128)S(1)}, f32[256,256]{1,0:T(8,128)S(1)}, f32[256,256]{1,0:T(8,128)S(1)}, f32[256,256]{1,0:T(8,128)S(1)}, f32[256,256]{1,...) custom-call(bf16[10,192,512]{2,1,0:T(8,128)(2,1)S(1)} %shard_map.59.ext_ref, ...), custom_call_target="tpu_custom_call" | custom-call | tf_op jit(solution)/shard_map/pallas_call | solution.py:296
  15.6 2.7 %collective-permute-done.9 = f16[144,256]{1,0:T(8,128)(2,1)S(1)} collective-permute-done((f16[144,256]{1,0:T(8,128)(2,1)S(1)}, f16[144,256]{1,0:T(8,128)(2,1)S(1)}, u32[]{:S(2)}, u32[]{:S(2)}) %collective-permute-start.9) | collective-permute-done | bytes 73760 | tf_op jit(solution)/shard_map/ppermute | solution.py:451
  19.3 1.2 %collective-permute-start.13 = (f16[528,256]{1,0:T(8,128)(2,1)S(1)}, f16[528,256]{1,0:T(8,128)(2,1)S(1)}, u32[]{:S(2)}, u32[]{:S(2)}) collective-permute-start(f16[528,256]{1,0:T(8,128)(2,1)S(1)} %convert_element_type.64), channel_id=1, source_target_pairs={{8,0},{16,8},{24,16},{28,24},{20,28},{12,20},{4,12},{0,4},{9,1},{1... | collective-permute-start | bytes 811016 | tf_op jit(solution)/shard_map/ppermute | solution.py:451
  20.8 0.9 %collective-permute-start.6 = (f16[528,256]{1,0:T(8,128)(2,1)S(1)}, f16[528,256]{1,0:T(8,128)(2,1)S(1)}, u32[]{:S(2)}, u32[]{:S(2)}) collective-permute-start(f16[528,256]{1,0:T(8,128)(2,1)S(1)} %convert_element_type.56), channel_id=1, source_target_pairs={{0,8},{8,16},{16,24},{24,28},{28,20},{20,12},{12,4},{4,0},{1,9},{9... | collective-permute-start | bytes 811016 | tf_op jit(solution)/shard_map/ppermute | solution.py:451
  22.8 1.5 %shard_map.69 = (f32[10,64,256]{2,1,0:T(8,128)S(1)}, f32[8,256]{1,0:T(8,128)S(1)}) custom-call(bf16[3,576,256]{2,1,0:T(8,128)(2,1)S(1)} %bitcast.17, bf16[5,256,256]{2,1,0:T(8,128)(2,1)S(1)} %collective-permute-done.10.theirs_ref, bf16[256,256]{1,0:T(8,128)(2,1)S(1)} %bitcast.25, bf16[256,256]{1,0:T(8,128)(2,1)S(1)} %collective-permute-done.2.refs_0_.refs_1_, ...), custom_call_target="tpu_custom_call" | custom-call | tf_op jit(solution)/shard_map/pallas_call | solution.py:296
  24.3 2.5 %shard_map.70 = (f32[576,256]{1,0:T(8,128)S(1)}, f32[576,256]{1,0:T(8,128)S(1)}, f32[576,256]{1,0:T(8,128)S(1)}, f32[8,256]{1,0:T(8,128)S(1)}, f32[8,256]{1,0:T(8,128)S(1)}) custom-call(bf16[10,192,512]{2,1,0:T(8,128)(2,1)S(1)} %shard_map.59.ext_ref, bf16[10,192,512]{2,1,0:T(8,128)(2,1)S(1)} %shard_map.66.other_ref, ...), custom_call_target="tpu_custom_call" | custom-call | tf_op jit(solution)/shard_map/pallas_call | solution.py:296
  26.8 1.4 %collective-permute-done.13 = f16[528,256]{1,0:T(8,128)(2,1)S(1)} collective-permute-done((f16[528,256]{1,0:T(8,128)(2,1)S(1)}, f16[528,256]{1,0:T(8,128)(2,1)S(1)}, u32[]{:S(2)}, u32[]{:S(2)}) %collective-permute-start.13) | collective-permute-done | bytes 270368 | tf_op jit(solution)/shard_map/ppermute | solution.py:451
  28.7 1.2 %collective-permute-start.14 = (f16[400,256]{1,0:T(8,128)(2,1)S(1)}, f16[400,256]{1,0:T(8,128)(2,1)S(1)}, u32[]{:S(2)}, u32[]{:S(2)}) collective-permute-start(f16[400,256]{1,0:T(8,128)(2,1)S(1)} %convert_element_type.66), channel_id=1, source_target_pairs={{8,0},{16,8},{24,16},{28,24},{20,28},{12,20},{4,12},{0,4},{9,1},{1... | collective-permute-start | bytes 614408 | tf_op jit(solution)/shard_map/ppermute | solution.py:451
  30.4 0.9 %collective-permute-start.11 = (f16[400,256]{1,0:T(8,128)(2,1)S(1)}, f16[400,256]{1,0:T(8,128)(2,1)S(1)}, u32[]{:S(2)}, u32[]{:S(2)}) collective-permute-start(f16[400,256]{1,0:T(8,128)(2,1)S(1)} %convert_element_type.60), channel_id=1, source_target_pairs={{0,8},{8,16},{16,24},{24,28},{28,20},{20,12},{12,4},{4,0},{1,9},{9... | collective-permute-start | bytes 614408 | tf_op jit(solution)/shard_map/ppermute | solution.py:451
  31.3 4.1 %collective-permute-done.14 = f16[400,256]{1,0:T(8,128)(2,1)S(1)} collective-permute-done((f16[400,256]{1,0:T(8,128)(2,1)S(1)}, f16[400,256]{1,0:T(8,128)(2,1)S(1)}, u32[]{:S(2)}, u32[]{:S(2)}) %collective-permute-start.14) | collective-permute-done | bytes 204832 | tf_op jit(solution)/shard_map/ppermute | solution.py:451
  35.8 1.1 %collective-permute-done.11 = f16[400,256]{1,0:T(8,128)(2,1)S(1)} collective-permute-done((f16[400,256]{1,0:T(8,128)(2,1)S(1)}, f16[400,256]{1,0:T(8,128)(2,1)S(1)}, u32[]{:S(2)}, u32[]{:S(2)}) %collective-permute-start.11) | collective-permute-done | bytes 204832 | tf_op jit(solution)/shard_map/ppermute | solution.py:451
  37.5 1.6 %collective-permute-start.15 = (f16[272,256]{1,0:T(8,128)(2,1)S(1)}, f16[272,256]{1,0:T(8,128)(2,1)S(1)}, u32[]{:S(2)}, u32[]{:S(2)}) collective-permute-start(f16[272,256]{1,0:T(8,128)(2,1)S(1)} %convert_element_type.68), channel_id=1, source_target_pairs={{8,0},{16,8},{24,16},{28,24},{20,28},{12,20},{4,12},{0,4},{9,1},{1... | collective-permute-start | bytes 417800 | tf_op jit(solution)/shard_map/ppermute | solution.py:451
  39.8 1.2 %shard_map.77 = (f32[256,256]{1,0:T(8,128)S(1)}, f32[272,256]{1,0:T(8,128)S(1)}) custom-call(bf16[3,576,256]{2,1,0:T(8,128)(2,1)S(1)} %bitcast.18, bf16[3,256,256]{2,1,0:T(8,128)(2,1)S(1)} %collective-permute-done.16.theirs_ref, bf16[256,256]{1,0:T(8,128)(2,1)S(1)} %get-tuple-element.59.refs_0_, bf16[256,256]{1,0:T(8,128)(2,1)S(1)} %shard_map.75.refs_1_, ...), custom_call_target="tpu_custom_call" | custom-call | tf_op jit(solution)/shard_map/pallas_call | solution.py:296
  41.0 1.6 %collective-permute-start.17 = (f16[272,256]{1,0:T(8,128)(2,1)S(1)}, f16[272,256]{1,0:T(8,128)(2,1)S(1)}, u32[]{:S(2)}, u32[]{:S(2)}) collective-permute-start(f16[272,256]{1,0:T(8,128)(2,1)S(1)} %convert_element_type.70), channel_id=1, source_target_pairs={{0,2},{2,0},{1,3},{3,1},{4,6},{6,4},{5,7},{7,5},{8,10},{10,8},{9,1... | collective-permute-start | bytes 417800 | tf_op jit(solution)/shard_map/ppermute | solution.py:472
  42.6 1.0 %collective-permute-done.15 = f16[272,256]{1,0:T(8,128)(2,1)S(1)} collective-permute-done((f16[272,256]{1,0:T(8,128)(2,1)S(1)}, f16[272,256]{1,0:T(8,128)(2,1)S(1)}, u32[]{:S(2)}, u32[]{:S(2)}) %collective-permute-start.15) | collective-permute-done | bytes 139296 | tf_op jit(solution)/shard_map/ppermute | solution.py:451
  43.6 1.5 %collective-permute-done.12 = f16[272,256]{1,0:T(8,128)(2,1)S(1)} collective-permute-done((f16[272,256]{1,0:T(8,128)(2,1)S(1)}, f16[272,256]{1,0:T(8,128)(2,1)S(1)}, u32[]{:S(2)}, u32[]{:S(2)}) %collective-permute-start.12) | collective-permute-done | bytes 139296 | tf_op jit(solution)/shard_map/ppermute | solution.py:451
  45.1 3.2 %shard_map.80 = (f32[3,576,256]{2,1,0:T(8,128)}, f32[8,256]{1,0:T(8,128)}, f32[8,256]{1,0:T(8,128)}) custom-call(bf16[10,192,512]{2,1,0:T(8,128)(2,1)S(1)} %shard_map.59.ext_ref, bf16[10,192,512]{2,1,0:T(8,128)(2,1)S(1)} %shard_map.66.other_ref, bf16[3,256,256]{2,1,0:T(8,128)(2,1)S(1)} %shard_map.76.mine_ref, ...), custom_call_target="tpu_custom_call" | custom-call | tf_op jit(solution)/shard_map/pallas_call | solution.py:359
  (63 shorter events, 8.8 us)
Async XLA Ops:
  1.6 7.6 %collective-permute-start.2 = (bf16[256,256]{1,0:T(8,128)(2,1)S(1)}, bf16[256,256]{1,0:T(8,128)(2,1)S(1)}, u32[]{:S(2)}, u32[]{:S(2)}) collective-permute-start(bf16[256,256]{1,0:T(8,128)(2,1)S(1)} %bitcast.22), channel_id=1, source_target_pairs={{0,8},{8,16},{16,24},{24,28},{28,20},{20,12},{12,4},{4,0},{1,9},{9... | collective-permute-start | bytes 393224 | tf_op jit(solution)/shard_map/ppermute | solution.py:323
  4.6 6.7 %collective-permute-start.3 = (bf16[256,256]{1,0:T(8,128)(2,1)S(1)}, bf16[256,256]{1,0:T(8,128)(2,1)S(1)}, u32[]{:S(2)}, u32[]{:S(2)}) collective-permute-start(bf16[256,256]{1,0:T(8,128)(2,1)S(1)} %bitcast.23), channel_id=1, source_target_pairs={{8,0},{16,8},{24,16},{28,24},{20,28},{12,20},{4,12},{0,4},{9,1},{1... | collective-permute-start | bytes 393224 | tf_op jit(solution)/shard_map/ppermute | solution.py:323
  5.7 2.1 %collective-permute-start = (bf16[4,64,128]{2,1,0:T(8,128)(2,1)S(1)}, bf16[4,64,128]{2,1,0:T(8,128)(2,1)S(1)}, u32[]{:S(2)}, u32[]{:S(2)}) collective-permute-start(bf16[4,64,128]{2,1,0:T(8,128)(2,1)S(1)} %get-tuple-element.38), channel_id=1, source_target_pairs={{0,1},{1,0},{2,3},{3,2},{4,5},{5,4},{6,7},{7,6},{8,9},{9,8},{10,11... | collective-permute-start | bytes 196616 | tf_op jit(solution)/shard_map/ppermute | solution.py:332
  5.8 2.0 %collective-permute-start.1 = (bf16[4,64,128]{2,1,0:T(8,128)(2,1)S(1)}, bf16[4,64,128]{2,1,0:T(8,128)(2,1)S(1)}, u32[]{:S(2)}, u32[]{:S(2)}) collective-permute-start(bf16[4,64,128]{2,1,0:T(8,128)(2,1)S(1)} %get-tuple-element.39), channel_id=1, source_target_pairs={{0,1},{1,0},{2,3},{3,2},{4,5},{5,4},{6,7},{7,6},{8,9},{9,8},{10,11... | collective-permute-start | bytes 196616 | tf_op jit(solution)/shard_map/ppermute | solution.py:332
  6.3 1.2 %copy-start = (bf16[27,256,64]{1,2,0:T(8,128)(2,1)S(1)}, bf16[27,256,64]{1,2,0:T(8,128)(2,1)}, u32[]{:S(2)}) copy-start(bf16[27,256,64]{1,2,0:T(8,128)(2,1)} %param.4) | copy-start | bytes 2654212
  9.3 9.1 %collective-permute-start.4 = (bf16[256,256]{1,0:T(8,128)(2,1)S(1)}, bf16[256,256]{1,0:T(8,128)(2,1)S(1)}, u32[]{:S(2)}, u32[]{:S(2)}) collective-permute-start(bf16[256,256]{1,0:T(8,128)(2,1)S(1)} %get-tuple-element.46), channel_id=1, source_target_pairs={{0,8},{8,16},{16,24},{24,28},{28,20},{20,12},{12,4},{4,0},{1,9},{9... | collective-permute-start | bytes 393224 | tf_op jit(solution)/shard_map/ppermute | solution.py:450
  11.5 7.2 %collective-permute-start.8 = (bf16[256,256]{1,0:T(8,128)(2,1)S(1)}, bf16[256,256]{1,0:T(8,128)(2,1)S(1)}, u32[]{:S(2)}, u32[]{:S(2)}) collective-permute-start(bf16[256,256]{1,0:T(8,128)(2,1)S(1)} %get-tuple-element.48), channel_id=1, source_target_pairs={{8,0},{16,8},{24,16},{28,24},{20,28},{12,20},{4,12},{0,4},{9,1},{1... | collective-permute-start | bytes 393224 | tf_op jit(solution)/shard_map/ppermute | solution.py:450
  11.6 6.7 %collective-permute-start.9 = (f16[144,256]{1,0:T(8,128)(2,1)S(1)}, f16[144,256]{1,0:T(8,128)(2,1)S(1)}, u32[]{:S(2)}, u32[]{:S(2)}) collective-permute-start(f16[144,256]{1,0:T(8,128)(2,1)S(1)} %convert_element_type.58), channel_id=1, source_target_pairs={{8,0},{16,8},{24,16},{28,24},{20,28},{12,20},{4,12},{0,4},{9,1},{1... | collective-permute-start | bytes 221192 | tf_op jit(solution)/shard_map/ppermute | solution.py:451
  13.6 4.8 %collective-permute-start.5 = (f16[144,256]{1,0:T(8,128)(2,1)S(1)}, f16[144,256]{1,0:T(8,128)(2,1)S(1)}, u32[]{:S(2)}, u32[]{:S(2)}) collective-permute-start(f16[144,256]{1,0:T(8,128)(2,1)S(1)} %convert_element_type.54), channel_id=1, source_target_pairs={{0,8},{8,16},{16,24},{24,28},{28,20},{20,12},{12,4},{4,0},{1,9},{9... | collective-permute-start | bytes 221192 | tf_op jit(solution)/shard_map/ppermute | solution.py:451
  19.1 3.6 %copy-start.1 = (bf16[27,256,64]{1,2,0:T(8,128)(2,1)S(1)}, bf16[27,256,64]{1,2,0:T(8,128)(2,1)}, u32[]{:S(2)}) copy-start(bf16[27,256,64]{1,2,0:T(8,128)(2,1)} %param.4) | copy-start | bytes 2654212
  19.2 3.6 %collective-permute-start.10 = (bf16[5,256,256]{2,1,0:T(8,128)(2,1)S(1)}, bf16[5,256,256]{2,1,0:T(8,128)(2,1)S(1)}, u32[]{:S(2)}, u32[]{:S(2)}) collective-permute-start(bf16[5,256,256]{2,1,0:T(8,128)(2,1)S(1)} %shard_map.68.mine_ref), channel_id=1, source_target_pairs={{0,1},{1,0},{2,3},{3,2},{4,5},{5,4},{6,7},{7,6},{8,9},{9,8},{10,11... | collective-permute-start | bytes 1966088 | tf_op jit(solution)/shard_map/ppermute | solution.py:462
  19.3 8.9 %collective-permute-start.13 = (f16[528,256]{1,0:T(8,128)(2,1)S(1)}, f16[528,256]{1,0:T(8,128)(2,1)S(1)}, u32[]{:S(2)}, u32[]{:S(2)}) collective-permute-start(f16[528,256]{1,0:T(8,128)(2,1)S(1)} %convert_element_type.64), channel_id=1, source_target_pairs={{8,0},{16,8},{24,16},{28,24},{20,28},{12,20},{4,12},{0,4},{9,1},{1... | collective-permute-start | bytes 811016 | tf_op jit(solution)/shard_map/ppermute | solution.py:451
  20.5 1.3 %collective-permute-start.7 = (bf16[8,64,128]{2,1,0:T(8,128)(2,1)S(1)}, bf16[8,64,128]{2,1,0:T(8,128)(2,1)S(1)}, u32[]{:S(2)}, u32[]{:S(2)}) collective-permute-start(bf16[8,64,128]{2,1,0:T(8,128)(2,1)S(1)} %get-tuple-element.47), channel_id=1, source_target_pairs={{0,1},{1,0},{2,3},{3,2},{4,5},{5,4},{6,7},{7,6},{8,9},{9,8},{10,11... | collective-permute-start | bytes 393224 | tf_op jit(solution)/shard_map/ppermute | solution.py:332
  20.8 9.2 %collective-permute-start.6 = (f16[528,256]{1,0:T(8,128)(2,1)S(1)}, f16[528,256]{1,0:T(8,128)(2,1)S(1)}, u32[]{:S(2)}, u32[]{:S(2)}) collective-permute-start(f16[528,256]{1,0:T(8,128)(2,1)S(1)} %convert_element_type.56), channel_id=1, source_target_pairs={{0,8},{8,16},{16,24},{24,28},{28,20},{20,12},{12,4},{4,0},{1,9},{9... | collective-permute-start | bytes 811016 | tf_op jit(solution)/shard_map/ppermute | solution.py:451
  28.7 6.7 %collective-permute-start.14 = (f16[400,256]{1,0:T(8,128)(2,1)S(1)}, f16[400,256]{1,0:T(8,128)(2,1)S(1)}, u32[]{:S(2)}, u32[]{:S(2)}) collective-permute-start(f16[400,256]{1,0:T(8,128)(2,1)S(1)} %convert_element_type.66), channel_id=1, source_target_pairs={{8,0},{16,8},{24,16},{28,24},{20,28},{12,20},{4,12},{0,4},{9,1},{1... | collective-permute-start | bytes 614408 | tf_op jit(solution)/shard_map/ppermute | solution.py:451
  30.4 6.5 %collective-permute-start.11 = (f16[400,256]{1,0:T(8,128)(2,1)S(1)}, f16[400,256]{1,0:T(8,128)(2,1)S(1)}, u32[]{:S(2)}, u32[]{:S(2)}) collective-permute-start(f16[400,256]{1,0:T(8,128)(2,1)S(1)} %convert_element_type.60), channel_id=1, source_target_pairs={{0,8},{8,16},{16,24},{24,28},{28,20},{20,12},{12,4},{4,0},{1,9},{9... | collective-permute-start | bytes 614408 | tf_op jit(solution)/shard_map/ppermute | solution.py:451
  37.3 2.4 %collective-permute-start.16 = (bf16[3,256,256]{2,1,0:T(8,128)(2,1)S(1)}, bf16[3,256,256]{2,1,0:T(8,128)(2,1)S(1)}, u32[]{:S(2)}, u32[]{:S(2)}) collective-permute-start(bf16[3,256,256]{2,1,0:T(8,128)(2,1)S(1)} %shard_map.76.mine_ref), channel_id=1, source_target_pairs={{0,1},{1,0},{2,3},{3,2},{4,5},{5,4},{6,7},{7,6},{8,9},{9,8},{10,11... | collective-permute-start | bytes 1179656 | tf_op jit(solution)/shard_map/ppermute | solution.py:462
  37.5 6.1 %collective-permute-start.15 = (f16[272,256]{1,0:T(8,128)(2,1)S(1)}, f16[272,256]{1,0:T(8,128)(2,1)S(1)}, u32[]{:S(2)}, u32[]{:S(2)}) collective-permute-start(f16[272,256]{1,0:T(8,128)(2,1)S(1)} %convert_element_type.68), channel_id=1, source_target_pairs={{8,0},{16,8},{24,16},{28,24},{20,28},{12,20},{4,12},{0,4},{9,1},{1... | collective-permute-start | bytes 417800 | tf_op jit(solution)/shard_map/ppermute | solution.py:451
  39.1 6.0 %collective-permute-start.12 = (f16[272,256]{1,0:T(8,128)(2,1)S(1)}, f16[272,256]{1,0:T(8,128)(2,1)S(1)}, u32[]{:S(2)}, u32[]{:S(2)}) collective-permute-start(f16[272,256]{1,0:T(8,128)(2,1)S(1)} %convert_element_type.62), channel_id=1, source_target_pairs={{0,8},{8,16},{16,24},{24,28},{28,20},{20,12},{12,4},{4,0},{1,9},{9... | collective-permute-start | bytes 417800 | tf_op jit(solution)/shard_map/ppermute | solution.py:451
  41.0 7.4 %collective-permute-start.17 = (f16[272,256]{1,0:T(8,128)(2,1)S(1)}, f16[272,256]{1,0:T(8,128)(2,1)S(1)}, u32[]{:S(2)}, u32[]{:S(2)}) collective-permute-start(f16[272,256]{1,0:T(8,128)(2,1)S(1)} %convert_element_type.70), channel_id=1, source_target_pairs={{0,2},{2,0},{1,3},{3,1},{4,6},{6,4},{5,7},{7,5},{8,10},{10,8},{9,1... | collective-permute-start | bytes 417800 | tf_op jit(solution)/shard_map/ppermute | solution.py:472

commit v5 on v4

--- a/solution.py
+++ b/solution.py
@@ -71,7 +71,7 @@
                 ext_ref[h + 1, 2 * chan : 3 * chan, cols] = shifted(wide, -1).astype(BF16)
 
 
-def turn_kernel(in_ref, out_ref):
+def turn_kernel(in_ref, after_ref, out_ref):
     for a in range(in_ref.shape[0]):
         out_ref[a] = in_ref[a].T
 
@@ -94,14 +94,14 @@
         part_ref[...] = total
 
 
-def weight_kernel(group, width, scale, first, last, ext_ref, other_ref, mine_ref, theirs_ref, *refs):
+def weight_kernel(group, width, scale, first, last, depths, ext_ref, other_ref, mine_ref, theirs_ref, *refs):
     before = refs[:3]
     if not last:
         *outs, token_ref, second_token_ref = refs[-5:]
+        second_token_ref[...] = jnp.zeros(second_token_ref.shape, F32)
+        token_ref[...] = jnp.zeros(token_ref.shape, F32)
     else:
-        out_ref, token_ref, second_token_ref, held_ref, sems = refs[-5:]
-    second_token_ref[...] = jnp.zeros(second_token_ref.shape, F32)
-    token_ref[...] = jnp.zeros(token_ref.shape, F32)
+        out_ref, held_ref, sems = refs[-3:]
     chan3 = ext_ref.shape[1]
     cells = mine_ref.shape[2]
     terms = []
@@ -110,7 +110,7 @@
         terms.append((row, ext_ref, mine_ref, i))
         terms.append((row, other_ref, theirs_ref, i))
     copies = []
-    for a in range(3):
+    for a in depths:
         left = [
             source[pl.ds(row, 3), :, a * width : a * width + cells].reshape(3 * chan3, cells)
             for row, source, stack, i in terms
@@ -126,8 +126,10 @@
         if not last:
             outs[a][...] = total
             continue
-        held_ref[a] = total * scale
-        copies.append(pltpu.make_async_copy(held_ref.at[a], out_ref.at[a], sems.at[a]))
+        slot = len(copies)
+        held_ref[slot] = total * scale
+        copy = pltpu.make_async_copy(held_ref.at[slot], out_ref.at[a], sems.at[slot])
+        copies.append(copy)
         copies[-1].start()
     for copy in copies:
         copy.wait()
@@ -269,6 +271,11 @@
         outs.pop(0)[...] = came
 
 
+def mark_kernel(after_ref, token_ref, second_token_ref):
+    token_ref[...] = jnp.zeros(token_ref.shape, F32)
+    second_token_ref[...] = jnp.zeros(second_token_ref.shape, F32)
+
+
 def stack_kernel(count, *refs):
     out_ref = refs[-1]
     for i in range(count):
@@ -282,10 +289,9 @@
 
 
 def add_kernel(first_ref, *refs, skip=0):
-    out_ref, token_ref = refs[-2:]
-    token_ref[...] = jnp.zeros(token_ref.shape, F32)
+    out_ref = refs[-1]
     total = first_ref[...]
-    for ref in refs[: len(refs) - 2 - skip]:
+    for ref in refs[: len(refs) - 1 - skip]:
         total = total + decoded(ref, 0, total.shape[0], total.shape[0] + 8)
     out_ref[...] = total.astype(BF16)
 
@@ -331,9 +337,9 @@
     layer = [jax.ShapeDtypeStruct((n, chan, width), BF16) for n in (count // 2, count // 2, count)]
     got = [lax.ppermute(x, "depth", swap) for x in call(split_kernel, layer, (feat,))]
     taps = kernel.transpose(0, 2, 1).reshape(3, 9 * chan, outs)
-    w_out = call(turn_kernel, jax.ShapeDtypeStruct((3, outs, 9 * chan), BF16), (taps,))
     ext_shape = jax.ShapeDtypeStruct((count + 2, 3 * chan, cells + 2 * width), BF16)
     ext = call(functools.partial(extend_kernel, True), ext_shape, (feat, *got[:2]))
+    w_out = call(turn_kernel, jax.ShapeDtypeStruct((3, outs, 9 * chan), BF16), (taps, ext))
     ext_other = call(functools.partial(extend_kernel, False), ext_shape, (feat, *got))
 
     def forward(offsets, after=()):
@@ -345,23 +351,26 @@
 
     def weight_part(group, mine, theirs, acc, after):
         *acc, token_f, token_b = call(
-            functools.partial(weight_kernel, group, width, 1.0, not acc, False),
+            functools.partial(weight_kernel, group, width, 1.0, not acc, False, range(3)),
             [jax.ShapeDtypeStruct((9 * chan, outs), F32)] * 3 + [token, token],
             (ext, ext_other, mine, theirs, *acc, after),
         )
         return acc, (token_f, token_b)
 
-    def weight_last(group, mine, theirs, acc, after):
+    def weight_last(group, mine, theirs, acc, after, depths, made):
         shape = (3, 9 * chan, outs)
         scale = 1.0 / math.sqrt(count * cells * lax.axis_size("depth"))
         whole = pl.BlockSpec(memory_space=pltpu.VMEM)
-        args = (ext, ext_other, mine, theirs, *acc, after)
+        anywhere = pl.BlockSpec(memory_space=pl.ANY)
+        args = (ext, ext_other, mine, theirs, *acc, after, *made)
+        size = len(depths)
         return pl.pallas_call(
-            functools.partial(weight_kernel, group, width, scale, False, True),
-            out_shape=[jax.ShapeDtypeStruct(shape, F32), token, token],
-            in_specs=[whole] * len(args),
-            out_specs=[pl.BlockSpec(memory_space=pl.ANY), whole, whole],
-            scratch_shapes=[pltpu.VMEM(shape, F32), pltpu.SemaphoreType.DMA((3,))],
+            functools.partial(weight_kernel, group, width, scale, False, True, depths),
+            out_shape=jax.ShapeDtypeStruct(shape, F32),
+            in_specs=[whole] * (len(args) - len(made)) + [anywhere] * len(made),
+            out_specs=anywhere,
+            scratch_shapes=[pltpu.VMEM((size, *shape[1:]), F32), pltpu.SemaphoreType.DMA((size,))],
+            input_output_aliases={len(args) - 1: 0} if made else {},
             compiler_params=pltpu.CompilerParams(vmem_limit_bytes=VMEM_LIMIT),
             cost_estimate=pl.CostEstimate(flops=0, bytes_accessed=0, transcendentals=0),
         )(*args)
@@ -462,7 +471,8 @@
             theirs = lax.ppermute(mine, "depth", swap)
             back, token_i = input_part(group, theirs, back, r == half and parts == 2)
             if r == half:
-                kernel_grad, *tokens = weight_last(group, mine, theirs, acc, back)
+                tokens = call(mark_kernel, [token, token], (back,))
+                kernel_grad = weight_last(group, mine, theirs, acc, tokens[0], range(3), ())
             else:
                 acc, tokens = weight_part(group, mine, theirs, acc, token_i)
     (f,), (b,) = sums
@@ -475,16 +485,16 @@
         back = back[1 : count + 1]
         terms = [lax.psum_scatter(back, "cout", scatter_dimension=0, tiled=True)]
         terms = [terms[0].reshape(count // parts * chan, cells)]
-    input_grad, token_y = call(
+    input_grad = call(
         add_kernel,
-        [jax.ShapeDtypeStruct((count // parts * chan, cells), BF16), token],
+        jax.ShapeDtypeStruct((count // parts * chan, cells), BF16),
         tuple(terms),
     )
     input_grad = input_grad.reshape(count // parts, chan, slab, width)
-    output, _ = call(
+    output = call(
         functools.partial(add_kernel, skip=1),
-        [jax.ShapeDtypeStruct((outs, cells), BF16), token],
-        (part[0], f.astype(F32), b.astype(F32), token_y),
+        jax.ShapeDtypeStruct((outs, cells), BF16),
+        (part[0], f.astype(F32) + tokens[0][0:1], b.astype(F32) + tokens[1][0:1], input_grad),
     )
     output = output.reshape(1, outs, slab, width)
     return (output, input_grad, kernel_grad)

time: 50.8 us -> 47.7 us (0.939)
  local copies, waits for them, and re-layouts: 4.48 us -> 2.74 us
  Pallas kernels: 16.1 us -> 15.1 us
    ppermute x8, waiting for transfers between devices: 11.9 us -> 9.61 us  [per_device(): sums[i] = [lax.ppermute(total, 'cin', perm)]]
    ppermute x1, waiting for transfers between devices: 0.01 us -> 1.29 us  [per_device(): other = lax.ppermute(token_i.astype(jnp.float16), 'cout', swap).astype(F32)]
    unnamed x6, local copies, waits for them, and re-layouts: 3.09 us -> 2.01 us
    ppermute x3, waiting for transfers between devices: 0.21 us -> 0.9 us  [per_device(): lax.ppermute(x, 'depth', swap)]
    reshape x1, local copies, waits for them, and re-layouts: 0.69 us -> 0.04 us  [per_device(): input_grad = input_grad.reshape(count // parts, chan, slab, width)]
    pallas_call x1, Pallas kernels: 3.22 us -> 2.61 us  [weight_last(): pl.pallas_call(functools.partial(weight_kernel, group, width, scale, Fals...]
    pallas_call x22 -> x23, Pallas kernels: 12.9 us -> 12.5 us  [call(): pl.pallas_call(kernel, out_shape=jax.tree.map(lambda x: pltpu.VMEM(x.shap...]
where the time goes in v5:
time: 47.7 us; the launch traced here: 47.6 us
  starting transfers between devices  16.4 us (34%)
  Pallas kernels  15.1 us (32%)
  waiting for transfers between devices  11.8 us (25%)
  local copies, waits for them, and re-layouts  2.74 us (6%)
  between operations  1.08 us (2%)
    pallas_call x23, Pallas kernels, call(): pl.pallas_call(kernel, out_shape=jax.tree.map(lambda x: pltpu.VMEM(x.shap...  12.5 us
    ppermute x8, waiting for transfers between devices, per_device(): sums[i] = [lax.ppermute(total, 'cin', perm)]  9.61 us
    ppermute x8, starting transfers between devices, per_device(): sums[i] = [lax.ppermute(total, 'cin', perm)]  8.7 us
    ppermute x1, starting transfers between devices, send(): lax.ppermute(pair[0], 'cin', fwd)  3.08 us
    pallas_call x1, Pallas kernels, weight_last(): pl.pallas_call(functools.partial(weight_kernel, group, width, scale, Fals...  2.61 us
    ppermute x2, starting transfers between devices, per_device(): going[i] = [lax.ppermute(x, 'cin', perm) for x in made[:sent - 1]]  2.13 us
    unnamed x6, local copies, waits for them, and re-layouts  2.01 us
    ppermute x1, starting transfers between devices, per_device(): other = lax.ppermute(token_i.astype(jnp.float16), 'cout', swap).astype(F32)  1.58 us
  transfers between devices with their start and end apart: 18, of which 7 were waited for; matrix products, arithmetic and copies ran while one was open for 3% of the time, Pallas kernels for 29%

profile of v5, /device:TPU:0, one launch (start us, length us, event | category | flops | bytes accessed | tf_op | source)
XLA Modules:
  0.0 47.6 jit_solution(12560331898168167382)
XLA Ops:
  0.6 1.0 %copy.11 = bf16[32,8,2,128]{3,1,2,0:T(8,128)(2,1)S(1)} copy(bf16[32,8,2,128]{3,2,1,0:T(2,128)(2,1)} %bitcast.29) | data formatting | bytes 262144
  1.6 3.1 %collective-permute-start.2 = (bf16[256,256]{1,0:T(8,128)(2,1)S(1)}, bf16[256,256]{1,0:T(8,128)(2,1)S(1)}, u32[]{:S(2)}, u32[]{:S(2)}) collective-permute-start(bf16[256,256]{1,0:T(8,128)(2,1)S(1)} %bitcast.24), channel_id=1, source_target_pairs={{0,8},{8,16},{16,24},{24,28},{28,20},{20,12},{12,4},{4,0},{1,9},{9... | collective-permute-start | bytes 393224 | tf_op jit(solution)/shard_map/ppermute | solution.py:329
  4.7 1.0 %copy.10 = bf16[8,64,2,128]{3,1,2,0:T(8,128)(2,1)S(1)} copy(bf16[8,64,2,128]{3,2,1,0:T(2,128)(2,1)} %param.3) | data formatting | bytes 524288 | tf_op args[0]
  7.3 0.9 %shard_map.59.after_ref.ext_ref = bf16[10,192,512]{2,1,0:T(8,128)(2,1)S(1)} custom-call(bf16[8,2,64,128]{3,2,1,0:T(8,128)(2,1)S(1)} %bitcast.22, bf16[4,64,128]{2,1,0:T(8,128)(2,1)S(1)} %collective-permute-done.edge_ref, bf16[4,64,128]{2,1,0:T(8,128)(2,1)S(1)} %collective-permute-done.1.second_edge_ref), custom_call_target="tpu_custom_call" | custom-call | tf_op jit(solution)/shard_map/pallas_call | solution.py:302
  9.1 2.1 %collective-permute-start.4 = (bf16[256,256]{1,0:T(8,128)(2,1)S(1)}, bf16[256,256]{1,0:T(8,128)(2,1)S(1)}, u32[]{:S(2)}, u32[]{:S(2)}) collective-permute-start(bf16[256,256]{1,0:T(8,128)(2,1)S(1)} %get-tuple-element.44), channel_id=1, source_target_pairs={{0,8},{8,16},{16,24},{24,28},{28,20},{20,12},{12,4},{4,0},{1,9},{9... | collective-permute-start | bytes 393224 | tf_op jit(solution)/shard_map/ppermute | solution.py:459
  11.4 2.0 %collective-permute-start.9 = (f16[144,256]{1,0:T(8,128)(2,1)S(1)}, f16[144,256]{1,0:T(8,128)(2,1)S(1)}, u32[]{:S(2)}, u32[]{:S(2)}) collective-permute-start(f16[144,256]{1,0:T(8,128)(2,1)S(1)} %convert_element_type.58), channel_id=1, source_target_pairs={{8,0},{16,8},{24,16},{28,24},{20,28},{12,20},{4,12},{0,4},{9,1},{1... | collective-permute-start | bytes 221192 | tf_op jit(solution)/shard_map/ppermute | solution.py:460
  13.6 1.8 %shard_map.64 = (f32[256,256]{1,0:T(8,128)S(1)}, f32[256,256]{1,0:T(8,128)S(1)}, f32[256,256]{1,0:T(8,128)S(1)}, f32[256,256]{1,0:T(8,128)S(1)}, f32[256,256]{1,...) custom-call(bf16[10,192,512]{2,1,0:T(8,128)(2,1)S(1)} %shard_map.59.after_ref.ext_ref, ...), custom_call_target="tpu_custom_call" | custom-call | tf_op jit(solution)/shard_map/pallas_call | solution.py:302
  15.4 3.0 %collective-permute-done.9 = f16[144,256]{1,0:T(8,128)(2,1)S(1)} collective-permute-done((f16[144,256]{1,0:T(8,128)(2,1)S(1)}, f16[144,256]{1,0:T(8,128)(2,1)S(1)}, u32[]{:S(2)}, u32[]{:S(2)}) %collective-permute-start.9) | collective-permute-done | bytes 73760 | tf_op jit(solution)/shard_map/ppermute | solution.py:460
  19.4 1.0 %collective-permute-start.13 = (f16[528,256]{1,0:T(8,128)(2,1)S(1)}, f16[528,256]{1,0:T(8,128)(2,1)S(1)}, u32[]{:S(2)}, u32[]{:S(2)}) collective-permute-start(f16[528,256]{1,0:T(8,128)(2,1)S(1)} %convert_element_type.64), channel_id=1, source_target_pairs={{8,0},{16,8},{24,16},{28,24},{20,28},{12,20},{4,12},{0,4},{9,1},{1... | collective-permute-start | bytes 811016 | tf_op jit(solution)/shard_map/ppermute | solution.py:460
  20.6 1.2 %collective-permute-start.6 = (f16[528,256]{1,0:T(8,128)(2,1)S(1)}, f16[528,256]{1,0:T(8,128)(2,1)S(1)}, u32[]{:S(2)}, u32[]{:S(2)}) collective-permute-start(f16[528,256]{1,0:T(8,128)(2,1)S(1)} %convert_element_type.56), channel_id=1, source_target_pairs={{0,8},{8,16},{16,24},{24,28},{28,20},{20,12},{12,4},{4,0},{1,9},{9... | collective-permute-start | bytes 811016 | tf_op jit(solution)/shard_map/ppermute | solution.py:460
  21.7 0.9 %shard_map.66.other_ref = bf16[10,192,512]{2,1,0:T(8,128)(2,1)S(1)} custom-call(bf16[8,2,64,128]{3,2,1,0:T(8,128)(2,1)S(1)} %bitcast.23, bf16[4,64,128]{2,1,0:T(8,128)(2,1)S(1)} %collective-permute-done.edge_ref, bf16[4,64,128]{2,1,0:T(8,128)(2,1)S(1)} %collective-permute-done.1.second_edge_ref, bf16[8,64,128]{2,1,0:T(8,128)(2,1)S(1)} %collective-permute-done.7.refs_0_), custom_call_target="tpu_custom_call" | custom-call | tf_op jit(solution)/shard_map/pallas_call | solution.py:302
  22.6 1.5 %shard_map.69 = (f32[10,64,256]{2,1,0:T(8,128)S(1)}, f32[8,256]{1,0:T(8,128)S(1)}) custom-call(bf16[3,576,256]{2,1,0:T(8,128)(2,1)S(1)} %bitcast.19, bf16[5,256,256]{2,1,0:T(8,128)(2,1)S(1)} %collective-permute-done.10.theirs_ref, bf16[256,256]{1,0:T(8,128)(2,1)S(1)} %bitcast.27, bf16[256,256]{1,0:T(8,128)(2,1)S(1)} %collective-permute-done.2.refs_0_.refs_1_, ...), custom_call_target="tpu_custom_call" | custom-call | tf_op jit(solution)/shard_map/pallas_call | solution.py:302
  24.1 2.5 %shard_map.70 = (f32[576,256]{1,0:T(8,128)S(1)}, f32[576,256]{1,0:T(8,128)S(1)}, f32[576,256]{1,0:T(8,128)S(1)}, f32[8,256]{1,0:T(8,128)S(1)}, f32[8,256]{1,0:T(8,128)S(1)}) custom-call(bf16[10,192,512]{2,1,0:T(8,128)(2,1)S(1)} %shard_map.59.after_ref.ext_ref, bf16[10,192,512]{2,1,0:T(8,128)(2,1)S(1)} %shard_map.66.other_ref, ...), custom_call_target="tpu_custom_call" | custom-call | tf_op jit(solution)/shard_map/pallas_call | solution.py:302
  26.6 1.7 %collective-permute-done.13 = f16[528,256]{1,0:T(8,128)(2,1)S(1)} collective-permute-done((f16[528,256]{1,0:T(8,128)(2,1)S(1)}, f16[528,256]{1,0:T(8,128)(2,1)S(1)}, u32[]{:S(2)}, u32[]{:S(2)}) %collective-permute-start.13) | collective-permute-done | bytes 270368 | tf_op jit(solution)/shard_map/ppermute | solution.py:460
  28.8 1.0 %collective-permute-start.14 = (f16[400,256]{1,0:T(8,128)(2,1)S(1)}, f16[400,256]{1,0:T(8,128)(2,1)S(1)}, u32[]{:S(2)}, u32[]{:S(2)}) collective-permute-start(f16[400,256]{1,0:T(8,128)(2,1)S(1)} %convert_element_type.66), channel_id=1, source_target_pairs={{8,0},{16,8},{24,16},{28,24},{20,28},{12,20},{4,12},{0,4},{9,1},{1... | collective-permute-start | bytes 614408 | tf_op jit(solution)/shard_map/ppermute | solution.py:460
  30.2 1.2 %collective-permute-start.11 = (f16[400,256]{1,0:T(8,128)(2,1)S(1)}, f16[400,256]{1,0:T(8,128)(2,1)S(1)}, u32[]{:S(2)}, u32[]{:S(2)}) collective-permute-start(f16[400,256]{1,0:T(8,128)(2,1)S(1)} %convert_element_type.60), channel_id=1, source_target_pairs={{0,8},{8,16},{16,24},{24,28},{28,20},{20,12},{12,4},{4,0},{1,9},{9... | collective-permute-start | bytes 614408 | tf_op jit(solution)/shard_map/ppermute | solution.py:460
  31.4 4.1 %collective-permute-done.14 = f16[400,256]{1,0:T(8,128)(2,1)S(1)} collective-permute-done((f16[400,256]{1,0:T(8,128)(2,1)S(1)}, f16[400,256]{1,0:T(8,128)(2,1)S(1)}, u32[]{:S(2)}, u32[]{:S(2)}) %collective-permute-start.14) | collective-permute-done | bytes 204832 | tf_op jit(solution)/shard_map/ppermute | solution.py:460
  35.9 0.8 %collective-permute-done.11 = f16[400,256]{1,0:T(8,128)(2,1)S(1)} collective-permute-done((f16[400,256]{1,0:T(8,128)(2,1)S(1)}, f16[400,256]{1,0:T(8,128)(2,1)S(1)}, u32[]{:S(2)}, u32[]{:S(2)}) %collective-permute-start.11) | collective-permute-done | bytes 204832 | tf_op jit(solution)/shard_map/ppermute | solution.py:460
  37.2 1.2 %collective-permute-start.12 = (f16[272,256]{1,0:T(8,128)(2,1)S(1)}, f16[272,256]{1,0:T(8,128)(2,1)S(1)}, u32[]{:S(2)}, u32[]{:S(2)}) collective-permute-start(f16[272,256]{1,0:T(8,128)(2,1)S(1)} %convert_element_type.62), channel_id=1, source_target_pairs={{0,8},{8,16},{16,24},{24,28},{28,20},{20,12},{12,4},{4,0},{1,9},{9... | collective-permute-start | bytes 417800 | tf_op jit(solution)/shard_map/ppermute | solution.py:460
  38.4 1.1 %collective-permute-start.16 = (f16[272,256]{1,0:T(8,128)(2,1)S(1)}, f16[272,256]{1,0:T(8,128)(2,1)S(1)}, u32[]{:S(2)}, u32[]{:S(2)}) collective-permute-start(f16[272,256]{1,0:T(8,128)(2,1)S(1)} %convert_element_type.68), channel_id=1, source_target_pairs={{8,0},{16,8},{24,16},{28,24},{20,28},{12,20},{4,12},{0,4},{9,1},{1... | collective-permute-start | bytes 417800 | tf_op jit(solution)/shard_map/ppermute | solution.py:460
  39.6 1.2 %shard_map.77 = (f32[256,256]{1,0:T(8,128)S(1)}, f32[272,256]{1,0:T(8,128)S(1)}) custom-call(bf16[3,576,256]{2,1,0:T(8,128)(2,1)S(1)} %bitcast.20, bf16[3,256,256]{2,1,0:T(8,128)(2,1)S(1)} %collective-permute-done.15.theirs_ref, bf16[256,256]{1,0:T(8,128)(2,1)S(1)} %get-tuple-element.54.refs_0_, bf16[256,256]{1,0:T(8,128)(2,1)S(1)} %shard_map.75.refs_1_, ...), custom_call_target="tpu_custom_call" | custom-call | tf_op jit(solution)/shard_map/pallas_call | solution.py:302
  40.9 1.6 %collective-permute-start.17 = (f16[272,256]{1,0:T(8,128)(2,1)S(1)}, f16[272,256]{1,0:T(8,128)(2,1)S(1)}, u32[]{:S(2)}, u32[]{:S(2)}) collective-permute-start(f16[272,256]{1,0:T(8,128)(2,1)S(1)} %convert_element_type.70), channel_id=1, source_target_pairs={{0,2},{2,0},{1,3},{3,1},{4,6},{6,4},{5,7},{7,5},{8,10},{10,8},{9,1... | collective-permute-start | bytes 417800 | tf_op jit(solution)/shard_map/ppermute | solution.py:482
  42.4 2.6 %shard_map.81 = f32[3,576,256]{2,1,0:T(8,128)} custom-call(bf16[10,192,512]{2,1,0:T(8,128)(2,1)S(1)} %shard_map.59.after_ref.ext_ref, bf16[10,192,512]{2,1,0:T(8,128)(2,1)S(1)} %shard_map.66.other_ref, bf16[3,256,256]{2,1,0:T(8,128)(2,1)S(1)} %shard_map.76.mine_ref, bf16[3,256,256]{2,1,0:T(8,128)(2,1)S(1)} %collective-permute-done.15.theirs_ref, ...), custom_call_target="tpu_custom_call" | custom-call | tf_op jit(solution)/shard_map/pallas_call | solution.py:367
  45.1 1.3 %collective-permute-done.17 = f16[272,256]{1,0:T(8,128)(2,1)S(1)} collective-permute-done((f16[272,256]{1,0:T(8,128)(2,1)S(1)}, f16[272,256]{1,0:T(8,128)(2,1)S(1)}, u32[]{:S(2)}, u32[]{:S(2)}) %collective-permute-start.17) | collective-permute-done | bytes 139296 | tf_op jit(solution)/shard_map/ppermute | solution.py:482
  (66 shorter events, 7.0 us)
Async XLA Ops:
  0.6 7.5 %copy-start = (bf16[27,256,64]{1,2,0:T(8,128)(2,1)S(1)}, bf16[27,256,64]{1,2,0:T(8,128)(2,1)}, u32[]{:S(2)}) copy-start(bf16[27,256,64]{1,2,0:T(8,128)(2,1)} %param.4) | copy-start | bytes 2654212
  1.6 7.3 %collective-permute-start.2 = (bf16[256,256]{1,0:T(8,128)(2,1)S(1)}, bf16[256,256]{1,0:T(8,128)(2,1)S(1)}, u32[]{:S(2)}, u32[]{:S(2)}) collective-permute-start(bf16[256,256]{1,0:T(8,128)(2,1)S(1)} %bitcast.24), channel_id=1, source_target_pairs={{0,8},{8,16},{16,24},{24,28},{28,20},{20,12},{12,4},{4,0},{1,9},{9... | collective-permute-start | bytes 393224 | tf_op jit(solution)/shard_map/ppermute | solution.py:329
  4.7 6.5 %collective-permute-start.3 = (bf16[256,256]{1,0:T(8,128)(2,1)S(1)}, bf16[256,256]{1,0:T(8,128)(2,1)S(1)}, u32[]{:S(2)}, u32[]{:S(2)}) collective-permute-start(bf16[256,256]{1,0:T(8,128)(2,1)S(1)} %bitcast.25), channel_id=1, source_target_pairs={{8,0},{16,8},{24,16},{28,24},{20,28},{12,20},{4,12},{0,4},{9,1},{1... | collective-permute-start | bytes 393224 | tf_op jit(solution)/shard_map/ppermute | solution.py:329
  5.8 1.3 %collective-permute-start = (bf16[4,64,128]{2,1,0:T(8,128)(2,1)S(1)}, bf16[4,64,128]{2,1,0:T(8,128)(2,1)S(1)}, u32[]{:S(2)}, u32[]{:S(2)}) collective-permute-start(bf16[4,64,128]{2,1,0:T(8,128)(2,1)S(1)} %get-tuple-element.36), channel_id=1, source_target_pairs={{0,1},{1,0},{2,3},{3,2},{4,5},{5,4},{6,7},{7,6},{8,9},{9,8},{10,11... | collective-permute-start | bytes 196616 | tf_op jit(solution)/shard_map/ppermute | solution.py:338
  5.9 1.4 %collective-permute-start.1 = (bf16[4,64,128]{2,1,0:T(8,128)(2,1)S(1)}, bf16[4,64,128]{2,1,0:T(8,128)(2,1)S(1)}, u32[]{:S(2)}, u32[]{:S(2)}) collective-permute-start(bf16[4,64,128]{2,1,0:T(8,128)(2,1)S(1)} %get-tuple-element.37), channel_id=1, source_target_pairs={{0,1},{1,0},{2,3},{3,2},{4,5},{5,4},{6,7},{7,6},{8,9},{9,8},{10,11... | collective-permute-start | bytes 196616 | tf_op jit(solution)/shard_map/ppermute | solution.py:338
  9.1 9.4 %collective-permute-start.4 = (bf16[256,256]{1,0:T(8,128)(2,1)S(1)}, bf16[256,256]{1,0:T(8,128)(2,1)S(1)}, u32[]{:S(2)}, u32[]{:S(2)}) collective-permute-start(bf16[256,256]{1,0:T(8,128)(2,1)S(1)} %get-tuple-element.44), channel_id=1, source_target_pairs={{0,8},{8,16},{16,24},{24,28},{28,20},{20,12},{12,4},{4,0},{1,9},{9... | collective-permute-start | bytes 393224 | tf_op jit(solution)/shard_map/ppermute | solution.py:459
  11.4 7.5 %collective-permute-start.8 = (bf16[256,256]{1,0:T(8,128)(2,1)S(1)}, bf16[256,256]{1,0:T(8,128)(2,1)S(1)}, u32[]{:S(2)}, u32[]{:S(2)}) collective-permute-start(bf16[256,256]{1,0:T(8,128)(2,1)S(1)} %get-tuple-element.46), channel_id=1, source_target_pairs={{8,0},{16,8},{24,16},{28,24},{20,28},{12,20},{4,12},{0,4},{9,1},{1... | collective-permute-start | bytes 393224 | tf_op jit(solution)/shard_map/ppermute | solution.py:459
  11.4 7.0 %collective-permute-start.9 = (f16[144,256]{1,0:T(8,128)(2,1)S(1)}, f16[144,256]{1,0:T(8,128)(2,1)S(1)}, u32[]{:S(2)}, u32[]{:S(2)}) collective-permute-start(f16[144,256]{1,0:T(8,128)(2,1)S(1)} %convert_element_type.58), channel_id=1, source_target_pairs={{8,0},{16,8},{24,16},{28,24},{20,28},{12,20},{4,12},{0,4},{9,1},{1... | collective-permute-start | bytes 221192 | tf_op jit(solution)/shard_map/ppermute | solution.py:460
  13.4 5.1 %collective-permute-start.5 = (f16[144,256]{1,0:T(8,128)(2,1)S(1)}, f16[144,256]{1,0:T(8,128)(2,1)S(1)}, u32[]{:S(2)}, u32[]{:S(2)}) collective-permute-start(f16[144,256]{1,0:T(8,128)(2,1)S(1)} %convert_element_type.54), channel_id=1, source_target_pairs={{0,8},{8,16},{16,24},{24,28},{28,20},{20,12},{12,4},{4,0},{1,9},{9... | collective-permute-start | bytes 221192 | tf_op jit(solution)/shard_map/ppermute | solution.py:460
  19.2 3.4 %collective-permute-start.10 = (bf16[5,256,256]{2,1,0:T(8,128)(2,1)S(1)}, bf16[5,256,256]{2,1,0:T(8,128)(2,1)S(1)}, u32[]{:S(2)}, u32[]{:S(2)}) collective-permute-start(bf16[5,256,256]{2,1,0:T(8,128)(2,1)S(1)} %shard_map.68.mine_ref), channel_id=1, source_target_pairs={{0,1},{1,0},{2,3},{3,2},{4,5},{5,4},{6,7},{7,6},{8,9},{9,8},{10,11... | collective-permute-start | bytes 1966088 | tf_op jit(solution)/shard_map/ppermute | solution.py:471
  19.4 8.9 %collective-permute-start.13 = (f16[528,256]{1,0:T(8,128)(2,1)S(1)}, f16[528,256]{1,0:T(8,128)(2,1)S(1)}, u32[]{:S(2)}, u32[]{:S(2)}) collective-permute-start(f16[528,256]{1,0:T(8,128)(2,1)S(1)} %convert_element_type.64), channel_id=1, source_target_pairs={{8,0},{16,8},{24,16},{28,24},{20,28},{12,20},{4,12},{0,4},{9,1},{1... | collective-permute-start | bytes 811016 | tf_op jit(solution)/shard_map/ppermute | solution.py:460
  20.3 1.4 %collective-permute-start.7 = (bf16[8,64,128]{2,1,0:T(8,128)(2,1)S(1)}, bf16[8,64,128]{2,1,0:T(8,128)(2,1)S(1)}, u32[]{:S(2)}, u32[]{:S(2)}) collective-permute-start(bf16[8,64,128]{2,1,0:T(8,128)(2,1)S(1)} %get-tuple-element.45), channel_id=1, source_target_pairs={{0,1},{1,0},{2,3},{3,2},{4,5},{5,4},{6,7},{7,6},{8,9},{9,8},{10,11... | collective-permute-start | bytes 393224 | tf_op jit(solution)/shard_map/ppermute | solution.py:338
  20.6 9.2 %collective-permute-start.6 = (f16[528,256]{1,0:T(8,128)(2,1)S(1)}, f16[528,256]{1,0:T(8,128)(2,1)S(1)}, u32[]{:S(2)}, u32[]{:S(2)}) collective-permute-start(f16[528,256]{1,0:T(8,128)(2,1)S(1)} %convert_element_type.56), channel_id=1, source_target_pairs={{0,8},{8,16},{16,24},{24,28},{28,20},{20,12},{12,4},{4,0},{1,9},{9... | collective-permute-start | bytes 811016 | tf_op jit(solution)/shard_map/ppermute | solution.py:460
  28.8 6.7 %collective-permute-start.14 = (f16[400,256]{1,0:T(8,128)(2,1)S(1)}, f16[400,256]{1,0:T(8,128)(2,1)S(1)}, u32[]{:S(2)}, u32[]{:S(2)}) collective-permute-start(f16[400,256]{1,0:T(8,128)(2,1)S(1)} %convert_element_type.66), channel_id=1, source_target_pairs={{8,0},{16,8},{24,16},{28,24},{20,28},{12,20},{4,12},{0,4},{9,1},{1... | collective-permute-start | bytes 614408 | tf_op jit(solution)/shard_map/ppermute | solution.py:460
  30.2 6.5 %collective-permute-start.11 = (f16[400,256]{1,0:T(8,128)(2,1)S(1)}, f16[400,256]{1,0:T(8,128)(2,1)S(1)}, u32[]{:S(2)}, u32[]{:S(2)}) collective-permute-start(f16[400,256]{1,0:T(8,128)(2,1)S(1)} %convert_element_type.60), channel_id=1, source_target_pairs={{0,8},{8,16},{16,24},{24,28},{28,20},{20,12},{12,4},{4,0},{1,9},{9... | collective-permute-start | bytes 614408 | tf_op jit(solution)/shard_map/ppermute | solution.py:460
  37.1 2.4 %collective-permute-start.15 = (bf16[3,256,256]{2,1,0:T(8,128)(2,1)S(1)}, bf16[3,256,256]{2,1,0:T(8,128)(2,1)S(1)}, u32[]{:S(2)}, u32[]{:S(2)}) collective-permute-start(bf16[3,256,256]{2,1,0:T(8,128)(2,1)S(1)} %shard_map.76.mine_ref), channel_id=1, source_target_pairs={{0,1},{1,0},{2,3},{3,2},{4,5},{5,4},{6,7},{7,6},{8,9},{9,8},{10,11... | collective-permute-start | bytes 1179656 | tf_op jit(solution)/shard_map/ppermute | solution.py:471
  37.2 7.8 %collective-permute-start.12 = (f16[272,256]{1,0:T(8,128)(2,1)S(1)}, f16[272,256]{1,0:T(8,128)(2,1)S(1)}, u32[]{:S(2)}, u32[]{:S(2)}) collective-permute-start(f16[272,256]{1,0:T(8,128)(2,1)S(1)} %convert_element_type.62), channel_id=1, source_target_pairs={{0,8},{8,16},{16,24},{24,28},{28,20},{20,12},{12,4},{4,0},{1,9},{9... | collective-permute-start | bytes 417800 | tf_op jit(solution)/shard_map/ppermute | solution.py:460
  38.4 6.7 %collective-permute-start.16 = (f16[272,256]{1,0:T(8,128)(2,1)S(1)}, f16[272,256]{1,0:T(8,128)(2,1)S(1)}, u32[]{:S(2)}, u32[]{:S(2)}) collective-permute-start(f16[272,256]{1,0:T(8,128)(2,1)S(1)} %convert_element_type.68), channel_id=1, source_target_pairs={{8,0},{16,8},{24,16},{28,24},{20,28},{12,20},{4,12},{0,4},{9,1},{1... | collective-permute-start | bytes 417800 | tf_op jit(solution)/shard_map/ppermute | solution.py:460
  40.9 5.6 %collective-permute-start.17 = (f16[272,256]{1,0:T(8,128)(2,1)S(1)}, f16[272,256]{1,0:T(8,128)(2,1)S(1)}, u32[]{:S(2)}, u32[]{:S(2)}) collective-permute-start(f16[272,256]{1,0:T(8,128)(2,1)S(1)} %convert_element_type.70), channel_id=1, source_target_pairs={{0,2},{2,0},{1,3},{3,1},{4,6},{6,4},{5,7},{7,5},{8,10},{10,8},{9,1... | collective-permute-start | bytes 417800 | tf_op jit(solution)/shard_map/ppermute | solution.py:482
  46.6 0.9 %copy-start.1 = (bf16[4,64,2,128]{3,2,1,0:T(2,128)(2,1)}, bf16[4,64,2,128]{3,2,1,0:T(2,128)(2,1)S(1)}, u32[]{:S(2)}) copy-start(bf16[4,64,2,128]{3,2,1,0:T(2,128)(2,1)S(1)} %reshape.23.refs_2_) | copy-start | bytes 393220

commit v6 on v5

--- a/solution.py
+++ b/solution.py
@@ -156,13 +156,15 @@
         pad_ref[i, :, 0:width] = jnp.where(low, none, theirs_ref[i, :, cells - width :])
         pad_ref[i, :, width : width + cells] = g_ref[...]
         pad_ref[i, :, width + cells :] = jnp.where(low, theirs_ref[i, :, 0:width], none)
+        right = [
+            pad_ref[i, :, (2 - a) * width : (2 - a) * width + cells] for a in range(3)
+        ]
+        right = jnp.concatenate(right, axis=0)
         for b in range(3):
-            total = None
-            for a in range(3):
-                right = pad_ref[i, :, (2 - a) * width : (2 - a) * width + cells]
-                left = weight_ref[a, 3 * b * chan : 3 * (b + 1) * chan]
-                term = jnp.dot(left, right, preferred_element_type=F32)
-                total = term if total is None else total + term
+            left = [weight_ref[a, 3 * b * chan : 3 * (b + 1) * chan] for a in range(3)]
+            total = jnp.dot(
+                jnp.concatenate(left, axis=1), right, preferred_element_type=F32
+            )
             row = ring_row(k, count) + b
             for d in range(cells // width):
                 cols = slice(d * width, (d + 1) * width)
@@ -260,7 +262,11 @@
     if plan["packs"]:
         out_ref = outs.pop(0)
         spot = out_ref.shape[0] - 16
-        if rows_out:
+        if rows_out and not plan["raw"]:
+            start = rows_in - rows_out if back else 0
+            out_ref[0:rows_out] = ref[start : start + rows_out]
+            out_ref[spot : spot + 8] = ref[ref.shape[0] - 16 : ref.shape[0] - 8]
+        elif rows_out:
             packed(out_ref, 0, spot, passed.astype(F32))
         else:
             out_ref[spot : spot + 8] = jnp.zeros((8, out_ref.shape[1]), F32)

time: 47.7 us -> 47.7 us (level)
  no operation moved by 1% of the time
where the time goes in v6:
time: 47.7 us; the launch traced here: 47.5 us
  starting transfers between devices  16.4 us (34%)
  Pallas kernels  15.1 us (32%)
  waiting for transfers between devices  11.8 us (25%)
  local copies, waits for them, and re-layouts  2.74 us (6%)
  between operations  1.07 us (2%)
    pallas_call x23, Pallas kernels, call(): pl.pallas_call(kernel, out_shape=jax.tree.map(lambda x: pltpu.VMEM(x.shap...  12.4 us
    ppermute x8, waiting for transfers between devices, per_device(): sums[i] = [lax.ppermute(total, 'cin', perm)]  9.58 us
    ppermute x8, starting transfers between devices, per_device(): sums[i] = [lax.ppermute(total, 'cin', perm)]  8.7 us
    ppermute x1, starting transfers between devices, send(): lax.ppermute(pair[0], 'cin', fwd)  3.08 us
    pallas_call x1, Pallas kernels, weight_last(): pl.pallas_call(functools.partial(weight_kernel, group, width, scale, Fals...  2.62 us
    ppermute x2, starting transfers between devices, per_device(): going[i] = [lax.ppermute(x, 'cin', perm) for x in made[:sent - 1]]  2.13 us
    unnamed x6, local copies, waits for them, and re-layouts  2.01 us
    ppermute x1, starting transfers between devices, per_device(): other = lax.ppermute(token_i.astype(jnp.float16), 'cout', swap).astype(F32)  1.59 us
  transfers between devices with their start and end apart: 18, of which 7 were waited for; matrix products, arithmetic and copies ran while one was open for 3% of the time, Pallas kernels for 29%

profile of v6, /device:TPU:0, one launch (start us, length us, event | category | flops | bytes accessed | tf_op | source)
XLA Modules:
  0.0 47.5 jit_solution(16475004289251044276)
XLA Ops:
  0.6 1.0 %copy.11 = bf16[32,8,2,128]{3,1,2,0:T(8,128)(2,1)S(1)} copy(bf16[32,8,2,128]{3,2,1,0:T(2,128)(2,1)} %bitcast.29) | data formatting | bytes 262144
  1.6 3.1 %collective-permute-start.2 = (bf16[256,256]{1,0:T(8,128)(2,1)S(1)}, bf16[256,256]{1,0:T(8,128)(2,1)S(1)}, u32[]{:S(2)}, u32[]{:S(2)}) collective-permute-start(bf16[256,256]{1,0:T(8,128)(2,1)S(1)} %bitcast.24), channel_id=1, source_target_pairs={{0,8},{8,16},{16,24},{24,28},{28,20},{20,12},{12,4},{4,0},{1,9},{9... | collective-permute-start | bytes 393224 | tf_op jit(solution)/shard_map/ppermute | solution.py:335
  4.7 1.0 %copy.10 = bf16[8,64,2,128]{3,1,2,0:T(8,128)(2,1)S(1)} copy(bf16[8,64,2,128]{3,2,1,0:T(2,128)(2,1)} %param.3) | data formatting | bytes 524288 | tf_op args[0]
  7.3 0.9 %shard_map.59.after_ref.ext_ref = bf16[10,192,512]{2,1,0:T(8,128)(2,1)S(1)} custom-call(bf16[8,2,64,128]{3,2,1,0:T(8,128)(2,1)S(1)} %bitcast.22, bf16[4,64,128]{2,1,0:T(8,128)(2,1)S(1)} %collective-permute-done.edge_ref, bf16[4,64,128]{2,1,0:T(8,128)(2,1)S(1)} %collective-permute-done.1.second_edge_ref), custom_call_target="tpu_custom_call" | custom-call | tf_op jit(solution)/shard_map/pallas_call | solution.py:308
  9.1 2.1 %collective-permute-start.4 = (bf16[256,256]{1,0:T(8,128)(2,1)S(1)}, bf16[256,256]{1,0:T(8,128)(2,1)S(1)}, u32[]{:S(2)}, u32[]{:S(2)}) collective-permute-start(bf16[256,256]{1,0:T(8,128)(2,1)S(1)} %get-tuple-element.44), channel_id=1, source_target_pairs={{0,8},{8,16},{16,24},{24,28},{28,20},{20,12},{12,4},{4,0},{1,9},{9... | collective-permute-start | bytes 393224 | tf_op jit(solution)/shard_map/ppermute | solution.py:465
  11.4 2.0 %collective-permute-start.9 = (f16[144,256]{1,0:T(8,128)(2,1)S(1)}, f16[144,256]{1,0:T(8,128)(2,1)S(1)}, u32[]{:S(2)}, u32[]{:S(2)}) collective-permute-start(f16[144,256]{1,0:T(8,128)(2,1)S(1)} %convert_element_type.58), channel_id=1, source_target_pairs={{8,0},{16,8},{24,16},{28,24},{20,28},{12,20},{4,12},{0,4},{9,1},{1... | collective-permute-start | bytes 221192 | tf_op jit(solution)/shard_map/ppermute | solution.py:466
  13.6 1.8 %shard_map.64 = (f32[256,256]{1,0:T(8,128)S(1)}, f32[256,256]{1,0:T(8,128)S(1)}, f32[256,256]{1,0:T(8,128)S(1)}, f32[256,256]{1,0:T(8,128)S(1)}, f32[256,256]{1,...) custom-call(bf16[10,192,512]{2,1,0:T(8,128)(2,1)S(1)} %shard_map.59.after_ref.ext_ref, ...), custom_call_target="tpu_custom_call" | custom-call | tf_op jit(solution)/shard_map/pallas_call | solution.py:308
  15.4 3.0 %collective-permute-done.9 = f16[144,256]{1,0:T(8,128)(2,1)S(1)} collective-permute-done((f16[144,256]{1,0:T(8,128)(2,1)S(1)}, f16[144,256]{1,0:T(8,128)(2,1)S(1)}, u32[]{:S(2)}, u32[]{:S(2)}) %collective-permute-start.9) | collective-permute-done | bytes 73760 | tf_op jit(solution)/shard_map/ppermute | solution.py:466
  19.4 1.0 %collective-permute-start.13 = (f16[528,256]{1,0:T(8,128)(2,1)S(1)}, f16[528,256]{1,0:T(8,128)(2,1)S(1)}, u32[]{:S(2)}, u32[]{:S(2)}) collective-permute-start(f16[528,256]{1,0:T(8,128)(2,1)S(1)} %convert_element_type.64), channel_id=1, source_target_pairs={{8,0},{16,8},{24,16},{28,24},{20,28},{12,20},{4,12},{0,4},{9,1},{1... | collective-permute-start | bytes 811016 | tf_op jit(solution)/shard_map/ppermute | solution.py:466
  20.6 1.2 %collective-permute-start.6 = (f16[528,256]{1,0:T(8,128)(2,1)S(1)}, f16[528,256]{1,0:T(8,128)(2,1)S(1)}, u32[]{:S(2)}, u32[]{:S(2)}) collective-permute-start(f16[528,256]{1,0:T(8,128)(2,1)S(1)} %convert_element_type.56), channel_id=1, source_target_pairs={{0,8},{8,16},{16,24},{24,28},{28,20},{20,12},{12,4},{4,0},{1,9},{9... | collective-permute-start | bytes 811016 | tf_op jit(solution)/shard_map/ppermute | solution.py:466
  21.7 0.9 %shard_map.66.other_ref = bf16[10,192,512]{2,1,0:T(8,128)(2,1)S(1)} custom-call(bf16[8,2,64,128]{3,2,1,0:T(8,128)(2,1)S(1)} %bitcast.23, bf16[4,64,128]{2,1,0:T(8,128)(2,1)S(1)} %collective-permute-done.edge_ref, bf16[4,64,128]{2,1,0:T(8,128)(2,1)S(1)} %collective-permute-done.1.second_edge_ref, bf16[8,64,128]{2,1,0:T(8,128)(2,1)S(1)} %collective-permute-done.7.refs_0_), custom_call_target="tpu_custom_call" | custom-call | tf_op jit(solution)/shard_map/pallas_call | solution.py:308
  22.6 1.5 %shard_map.69 = (f32[10,64,256]{2,1,0:T(8,128)S(1)}, f32[8,256]{1,0:T(8,128)S(1)}) custom-call(bf16[3,576,256]{2,1,0:T(8,128)(2,1)S(1)} %bitcast.19, bf16[5,256,256]{2,1,0:T(8,128)(2,1)S(1)} %collective-permute-done.10.theirs_ref, bf16[256,256]{1,0:T(8,128)(2,1)S(1)} %bitcast.27, bf16[256,256]{1,0:T(8,128)(2,1)S(1)} %collective-permute-done.2.refs_0_.refs_1_, ...), custom_call_target="tpu_custom_call" | custom-call | tf_op jit(solution)/shard_map/pallas_call | solution.py:308
  24.2 2.5 %shard_map.70 = (f32[576,256]{1,0:T(8,128)S(1)}, f32[576,256]{1,0:T(8,128)S(1)}, f32[576,256]{1,0:T(8,128)S(1)}, f32[8,256]{1,0:T(8,128)S(1)}, f32[8,256]{1,0:T(8,128)S(1)}) custom-call(bf16[10,192,512]{2,1,0:T(8,128)(2,1)S(1)} %shard_map.59.after_ref.ext_ref, bf16[10,192,512]{2,1,0:T(8,128)(2,1)S(1)} %shard_map.66.other_ref, ...), custom_call_target="tpu_custom_call" | custom-call | tf_op jit(solution)/shard_map/pallas_call | solution.py:308
  26.7 1.6 %collective-permute-done.13 = f16[528,256]{1,0:T(8,128)(2,1)S(1)} collective-permute-done((f16[528,256]{1,0:T(8,128)(2,1)S(1)}, f16[528,256]{1,0:T(8,128)(2,1)S(1)}, u32[]{:S(2)}, u32[]{:S(2)}) %collective-permute-start.13) | collective-permute-done | bytes 270368 | tf_op jit(solution)/shard_map/ppermute | solution.py:466
  28.7 1.0 %collective-permute-start.14 = (f16[400,256]{1,0:T(8,128)(2,1)S(1)}, f16[400,256]{1,0:T(8,128)(2,1)S(1)}, u32[]{:S(2)}, u32[]{:S(2)}) collective-permute-start(f16[400,256]{1,0:T(8,128)(2,1)S(1)} %convert_element_type.66), channel_id=1, source_target_pairs={{8,0},{16,8},{24,16},{28,24},{20,28},{12,20},{4,12},{0,4},{9,1},{1... | collective-permute-start | bytes 614408 | tf_op jit(solution)/shard_map/ppermute | solution.py:466
  30.2 1.2 %collective-permute-start.11 = (f16[400,256]{1,0:T(8,128)(2,1)S(1)}, f16[400,256]{1,0:T(8,128)(2,1)S(1)}, u32[]{:S(2)}, u32[]{:S(2)}) collective-permute-start(f16[400,256]{1,0:T(8,128)(2,1)S(1)} %convert_element_type.60), channel_id=1, source_target_pairs={{0,8},{8,16},{16,24},{24,28},{28,20},{20,12},{12,4},{4,0},{1,9},{9... | collective-permute-start | bytes 614408 | tf_op jit(solution)/shard_map/ppermute | solution.py:466
  31.3 4.2 %collective-permute-done.14 = f16[400,256]{1,0:T(8,128)(2,1)S(1)} collective-permute-done((f16[400,256]{1,0:T(8,128)(2,1)S(1)}, f16[400,256]{1,0:T(8,128)(2,1)S(1)}, u32[]{:S(2)}, u32[]{:S(2)}) %collective-permute-start.14) | collective-permute-done | bytes 204832 | tf_op jit(solution)/shard_map/ppermute | solution.py:466
  35.9 0.7 %collective-permute-done.11 = f16[400,256]{1,0:T(8,128)(2,1)S(1)} collective-permute-done((f16[400,256]{1,0:T(8,128)(2,1)S(1)}, f16[400,256]{1,0:T(8,128)(2,1)S(1)}, u32[]{:S(2)}, u32[]{:S(2)}) %collective-permute-start.11) | collective-permute-done | bytes 204832 | tf_op jit(solution)/shard_map/ppermute | solution.py:466
  37.2 1.2 %collective-permute-start.12 = (f16[272,256]{1,0:T(8,128)(2,1)S(1)}, f16[272,256]{1,0:T(8,128)(2,1)S(1)}, u32[]{:S(2)}, u32[]{:S(2)}) collective-permute-start(f16[272,256]{1,0:T(8,128)(2,1)S(1)} %convert_element_type.62), channel_id=1, source_target_pairs={{0,8},{8,16},{16,24},{24,28},{28,20},{20,12},{12,4},{4,0},{1,9},{9... | collective-permute-start | bytes 417800 | tf_op jit(solution)/shard_map/ppermute | solution.py:466
  38.3 1.1 %collective-permute-start.16 = (f16[272,256]{1,0:T(8,128)(2,1)S(1)}, f16[272,256]{1,0:T(8,128)(2,1)S(1)}, u32[]{:S(2)}, u32[]{:S(2)}) collective-permute-start(f16[272,256]{1,0:T(8,128)(2,1)S(1)} %convert_element_type.68), channel_id=1, source_target_pairs={{8,0},{16,8},{24,16},{28,24},{20,28},{12,20},{4,12},{0,4},{9,1},{1... | collective-permute-start | bytes 417800 | tf_op jit(solution)/shard_map/ppermute | solution.py:466
  39.5 1.2 %shard_map.77 = (f32[256,256]{1,0:T(8,128)S(1)}, f32[272,256]{1,0:T(8,128)S(1)}) custom-call(bf16[3,576,256]{2,1,0:T(8,128)(2,1)S(1)} %bitcast.20, bf16[3,256,256]{2,1,0:T(8,128)(2,1)S(1)} %collective-permute-done.15.theirs_ref, bf16[256,256]{1,0:T(8,128)(2,1)S(1)} %get-tuple-element.54.refs_0_, bf16[256,256]{1,0:T(8,128)(2,1)S(1)} %shard_map.75.refs_1_, ...), custom_call_target="tpu_custom_call" | custom-call | tf_op jit(solution)/shard_map/pallas_call | solution.py:308
  40.8 1.6 %collective-permute-start.17 = (f16[272,256]{1,0:T(8,128)(2,1)S(1)}, f16[272,256]{1,0:T(8,128)(2,1)S(1)}, u32[]{:S(2)}, u32[]{:S(2)}) collective-permute-start(f16[272,256]{1,0:T(8,128)(2,1)S(1)} %convert_element_type.70), channel_id=1, source_target_pairs={{0,2},{2,0},{1,3},{3,1},{4,6},{6,4},{5,7},{7,5},{8,10},{10,8},{9,1... | collective-permute-start | bytes 417800 | tf_op jit(solution)/shard_map/ppermute | solution.py:488
  42.4 2.6 %shard_map.81 = f32[3,576,256]{2,1,0:T(8,128)} custom-call(bf16[10,192,512]{2,1,0:T(8,128)(2,1)S(1)} %shard_map.59.after_ref.ext_ref, bf16[10,192,512]{2,1,0:T(8,128)(2,1)S(1)} %shard_map.66.other_ref, bf16[3,256,256]{2,1,0:T(8,128)(2,1)S(1)} %shard_map.76.mine_ref, bf16[3,256,256]{2,1,0:T(8,128)(2,1)S(1)} %collective-permute-done.15.theirs_ref, ...), custom_call_target="tpu_custom_call" | custom-call | tf_op jit(solution)/shard_map/pallas_call | solution.py:373
  45.1 1.3 %collective-permute-done.17 = f16[272,256]{1,0:T(8,128)(2,1)S(1)} collective-permute-done((f16[272,256]{1,0:T(8,128)(2,1)S(1)}, f16[272,256]{1,0:T(8,128)(2,1)S(1)}, u32[]{:S(2)}, u32[]{:S(2)}) %collective-permute-start.17) | collective-permute-done | bytes 139296 | tf_op jit(solution)/shard_map/ppermute | solution.py:488
  (66 shorter events, 6.9 us)
Async XLA Ops:
  0.6 7.5 %copy-start = (bf16[27,256,64]{1,2,0:T(8,128)(2,1)S(1)}, bf16[27,256,64]{1,2,0:T(8,128)(2,1)}, u32[]{:S(2)}) copy-start(bf16[27,256,64]{1,2,0:T(8,128)(2,1)} %param.4) | copy-start | bytes 2654212
  1.6 7.3 %collective-permute-start.2 = (bf16[256,256]{1,0:T(8,128)(2,1)S(1)}, bf16[256,256]{1,0:T(8,128)(2,1)S(1)}, u32[]{:S(2)}, u32[]{:S(2)}) collective-permute-start(bf16[256,256]{1,0:T(8,128)(2,1)S(1)} %bitcast.24), channel_id=1, source_target_pairs={{0,8},{8,16},{16,24},{24,28},{28,20},{20,12},{12,4},{4,0},{1,9},{9... | collective-permute-start | bytes 393224 | tf_op jit(solution)/shard_map/ppermute | solution.py:335
  4.7 6.5 %collective-permute-start.3 = (bf16[256,256]{1,0:T(8,128)(2,1)S(1)}, bf16[256,256]{1,0:T(8,128)(2,1)S(1)}, u32[]{:S(2)}, u32[]{:S(2)}) collective-permute-start(bf16[256,256]{1,0:T(8,128)(2,1)S(1)} %bitcast.25), channel_id=1, source_target_pairs={{8,0},{16,8},{24,16},{28,24},{20,28},{12,20},{4,12},{0,4},{9,1},{1... | collective-permute-start | bytes 393224 | tf_op jit(solution)/shard_map/ppermute | solution.py:335
  5.8 1.3 %collective-permute-start = (bf16[4,64,128]{2,1,0:T(8,128)(2,1)S(1)}, bf16[4,64,128]{2,1,0:T(8,128)(2,1)S(1)}, u32[]{:S(2)}, u32[]{:S(2)}) collective-permute-start(bf16[4,64,128]{2,1,0:T(8,128)(2,1)S(1)} %get-tuple-element.36), channel_id=1, source_target_pairs={{0,1},{1,0},{2,3},{3,2},{4,5},{5,4},{6,7},{7,6},{8,9},{9,8},{10,11... | collective-permute-start | bytes 196616 | tf_op jit(solution)/shard_map/ppermute | solution.py:344
  5.9 1.4 %collective-permute-start.1 = (bf16[4,64,128]{2,1,0:T(8,128)(2,1)S(1)}, bf16[4,64,128]{2,1,0:T(8,128)(2,1)S(1)}, u32[]{:S(2)}, u32[]{:S(2)}) collective-permute-start(bf16[4,64,128]{2,1,0:T(8,128)(2,1)S(1)} %get-tuple-element.37), channel_id=1, source_target_pairs={{0,1},{1,0},{2,3},{3,2},{4,5},{5,4},{6,7},{7,6},{8,9},{9,8},{10,11... | collective-permute-start | bytes 196616 | tf_op jit(solution)/shard_map/ppermute | solution.py:344
  9.1 9.4 %collective-permute-start.4 = (bf16[256,256]{1,0:T(8,128)(2,1)S(1)}, bf16[256,256]{1,0:T(8,128)(2,1)S(1)}, u32[]{:S(2)}, u32[]{:S(2)}) collective-permute-start(bf16[256,256]{1,0:T(8,128)(2,1)S(1)} %get-tuple-element.44), channel_id=1, source_target_pairs={{0,8},{8,16},{16,24},{24,28},{28,20},{20,12},{12,4},{4,0},{1,9},{9... | collective-permute-start | bytes 393224 | tf_op jit(solution)/shard_map/ppermute | solution.py:465
  11.4 7.5 %collective-permute-start.8 = (bf16[256,256]{1,0:T(8,128)(2,1)S(1)}, bf16[256,256]{1,0:T(8,128)(2,1)S(1)}, u32[]{:S(2)}, u32[]{:S(2)}) collective-permute-start(bf16[256,256]{1,0:T(8,128)(2,1)S(1)} %get-tuple-element.46), channel_id=1, source_target_pairs={{8,0},{16,8},{24,16},{28,24},{20,28},{12,20},{4,12},{0,4},{9,1},{1... | collective-permute-start | bytes 393224 | tf_op jit(solution)/shard_map/ppermute | solution.py:465
  11.4 7.0 %collective-permute-start.9 = (f16[144,256]{1,0:T(8,128)(2,1)S(1)}, f16[144,256]{1,0:T(8,128)(2,1)S(1)}, u32[]{:S(2)}, u32[]{:S(2)}) collective-permute-start(f16[144,256]{1,0:T(8,128)(2,1)S(1)} %convert_element_type.58), channel_id=1, source_target_pairs={{8,0},{16,8},{24,16},{28,24},{20,28},{12,20},{4,12},{0,4},{9,1},{1... | collective-permute-start | bytes 221192 | tf_op jit(solution)/shard_map/ppermute | solution.py:466
  13.4 5.1 %collective-permute-start.5 = (f16[144,256]{1,0:T(8,128)(2,1)S(1)}, f16[144,256]{1,0:T(8,128)(2,1)S(1)}, u32[]{:S(2)}, u32[]{:S(2)}) collective-permute-start(f16[144,256]{1,0:T(8,128)(2,1)S(1)} %convert_element_type.54), channel_id=1, source_target_pairs={{0,8},{8,16},{16,24},{24,28},{28,20},{20,12},{12,4},{4,0},{1,9},{9... | collective-permute-start | bytes 221192 | tf_op jit(solution)/shard_map/ppermute | solution.py:466
  19.2 3.4 %collective-permute-start.10 = (bf16[5,256,256]{2,1,0:T(8,128)(2,1)S(1)}, bf16[5,256,256]{2,1,0:T(8,128)(2,1)S(1)}, u32[]{:S(2)}, u32[]{:S(2)}) collective-permute-start(bf16[5,256,256]{2,1,0:T(8,128)(2,1)S(1)} %shard_map.68.mine_ref), channel_id=1, source_target_pairs={{0,1},{1,0},{2,3},{3,2},{4,5},{5,4},{6,7},{7,6},{8,9},{9,8},{10,11... | collective-permute-start | bytes 1966088 | tf_op jit(solution)/shard_map/ppermute | solution.py:477
  19.4 8.9 %collective-permute-start.13 = (f16[528,256]{1,0:T(8,128)(2,1)S(1)}, f16[528,256]{1,0:T(8,128)(2,1)S(1)}, u32[]{:S(2)}, u32[]{:S(2)}) collective-permute-start(f16[528,256]{1,0:T(8,128)(2,1)S(1)} %convert_element_type.64), channel_id=1, source_target_pairs={{8,0},{16,8},{24,16},{28,24},{20,28},{12,20},{4,12},{0,4},{9,1},{1... | collective-permute-start | bytes 811016 | tf_op jit(solution)/shard_map/ppermute | solution.py:466
  20.3 1.4 %collective-permute-start.7 = (bf16[8,64,128]{2,1,0:T(8,128)(2,1)S(1)}, bf16[8,64,128]{2,1,0:T(8,128)(2,1)S(1)}, u32[]{:S(2)}, u32[]{:S(2)}) collective-permute-start(bf16[8,64,128]{2,1,0:T(8,128)(2,1)S(1)} %get-tuple-element.45), channel_id=1, source_target_pairs={{0,1},{1,0},{2,3},{3,2},{4,5},{5,4},{6,7},{7,6},{8,9},{9,8},{10,11... | collective-permute-start | bytes 393224 | tf_op jit(solution)/shard_map/ppermute | solution.py:344
  20.6 9.1 %collective-permute-start.6 = (f16[528,256]{1,0:T(8,128)(2,1)S(1)}, f16[528,256]{1,0:T(8,128)(2,1)S(1)}, u32[]{:S(2)}, u32[]{:S(2)}) collective-permute-start(f16[528,256]{1,0:T(8,128)(2,1)S(1)} %convert_element_type.56), channel_id=1, source_target_pairs={{0,8},{8,16},{16,24},{24,28},{28,20},{20,12},{12,4},{4,0},{1,9},{9... | collective-permute-start | bytes 811016 | tf_op jit(solution)/shard_map/ppermute | solution.py:466
  28.7 6.7 %collective-permute-start.14 = (f16[400,256]{1,0:T(8,128)(2,1)S(1)}, f16[400,256]{1,0:T(8,128)(2,1)S(1)}, u32[]{:S(2)}, u32[]{:S(2)}) collective-permute-start(f16[400,256]{1,0:T(8,128)(2,1)S(1)} %convert_element_type.66), channel_id=1, source_target_pairs={{8,0},{16,8},{24,16},{28,24},{20,28},{12,20},{4,12},{0,4},{9,1},{1... | collective-permute-start | bytes 614408 | tf_op jit(solution)/shard_map/ppermute | solution.py:466
  30.2 6.5 %collective-permute-start.11 = (f16[400,256]{1,0:T(8,128)(2,1)S(1)}, f16[400,256]{1,0:T(8,128)(2,1)S(1)}, u32[]{:S(2)}, u32[]{:S(2)}) collective-permute-start(f16[400,256]{1,0:T(8,128)(2,1)S(1)} %convert_element_type.60), channel_id=1, source_target_pairs={{0,8},{8,16},{16,24},{24,28},{28,20},{20,12},{12,4},{4,0},{1,9},{9... | collective-permute-start | bytes 614408 | tf_op jit(solution)/shard_map/ppermute | solution.py:466
  37.1 2.4 %collective-permute-start.15 = (bf16[3,256,256]{2,1,0:T(8,128)(2,1)S(1)}, bf16[3,256,256]{2,1,0:T(8,128)(2,1)S(1)}, u32[]{:S(2)}, u32[]{:S(2)}) collective-permute-start(bf16[3,256,256]{2,1,0:T(8,128)(2,1)S(1)} %shard_map.76.mine_ref), channel_id=1, source_target_pairs={{0,1},{1,0},{2,3},{3,2},{4,5},{5,4},{6,7},{7,6},{8,9},{9,8},{10,11... | collective-permute-start | bytes 1179656 | tf_op jit(solution)/shard_map/ppermute | solution.py:477
  37.2 7.8 %collective-permute-start.12 = (f16[272,256]{1,0:T(8,128)(2,1)S(1)}, f16[272,256]{1,0:T(8,128)(2,1)S(1)}, u32[]{:S(2)}, u32[]{:S(2)}) collective-permute-start(f16[272,256]{1,0:T(8,128)(2,1)S(1)} %convert_element_type.62), channel_id=1, source_target_pairs={{0,8},{8,16},{16,24},{24,28},{28,20},{20,12},{12,4},{4,0},{1,9},{9... | collective-permute-start | bytes 417800 | tf_op jit(solution)/shard_map/ppermute | solution.py:466
  38.3 6.7 %collective-permute-start.16 = (f16[272,256]{1,0:T(8,128)(2,1)S(1)}, f16[272,256]{1,0:T(8,128)(2,1)S(1)}, u32[]{:S(2)}, u32[]{:S(2)}) collective-permute-start(f16[272,256]{1,0:T(8,128)(2,1)S(1)} %convert_element_type.68), channel_id=1, source_target_pairs={{8,0},{16,8},{24,16},{28,24},{20,28},{12,20},{4,12},{0,4},{9,1},{1... | collective-permute-start | bytes 417800 | tf_op jit(solution)/shard_map/ppermute | solution.py:466
  40.8 5.6 %collective-permute-start.17 = (f16[272,256]{1,0:T(8,128)(2,1)S(1)}, f16[272,256]{1,0:T(8,128)(2,1)S(1)}, u32[]{:S(2)}, u32[]{:S(2)}) collective-permute-start(f16[272,256]{1,0:T(8,128)(2,1)S(1)} %convert_element_type.70), channel_id=1, source_target_pairs={{0,2},{2,0},{1,3},{3,1},{4,6},{6,4},{5,7},{7,5},{8,10},{10,8},{9,1... | collective-permute-start | bytes 417800 | tf_op jit(solution)/shard_map/ppermute | solution.py:488
  46.5 0.9 %copy-start.1 = (bf16[4,64,2,128]{3,2,1,0:T(2,128)(2,1)}, bf16[4,64,2,128]{3,2,1,0:T(2,128)(2,1)S(1)}, u32[]{:S(2)}) copy-start(bf16[4,64,2,128]{3,2,1,0:T(2,128)(2,1)S(1)} %reshape.23.refs_2_) | copy-start | bytes 393220
